TPU v7x, 128 devices: a whole 4x4x4 slice. The times are simulated.
128 devices in a mesh: user: 16 (over z, x), item: 8 (over y, core).
Axes of the slice: x: 4, y: 4, z: 4, core: 2. Of those that a mesh axis runs over, the one named last changes fastest.
Arguments:
- counts: int32 [32768, 128, 128], P(('user', 'item')), may hold values from 0 to 5, as said below
- tile_user: int32 [32768], P(('user', 'item')), may hold values from 0 to 7
- tile_slot: int32 [32768], P(('user', 'item')), may hold values from 0 to 31
- live_tiles: int32 [128], P(('user', 'item')), may hold values from 64 to 256, as said below
- touched: int32 [2048, 2], P(('user', 'item')), may hold values from 0 to 3, as said below
- user_shape: float32 [16384, 256], P('user'), may hold values from 0.3 to 3
- user_rate: float32 [16384, 256], P('user'), may hold values from 0.5 to 5
- item_shape: float32 [65536, 256], P(('user', 'item')), may hold values from 0.3 to 3
- item_rate: float32 [65536, 256], P(('user', 'item')), may hold values from 32768 to 327680
Outputs:
- user_shape_new: float32 [16384, 256], P('user')
- user_rate_new: float32 [16384, 256], P('user')
- item_shape_new: float32 [65536, 256], P(('user', 'item'))
- item_elog: float32 [65536, 256], P(('user', 'item'))
Inputs may be any that keep to these rules, and one draw needn't show every extreme that they name: `counts`: mostly zero. Slots of device d at positions live_tiles[d] and beyond are padding and carry no data; some device has all 256 slots live. `touched`: the 2 block numbers in one row are distinct.
All inputs are finite; a program needn't handle non-finite values.
Results may differ from a plain program's by a relative error of at most 0.0026.
The roundings to bfloat16 on the way count: a program that leaves them out, or rounds other values in their place, can miss the bound.
Values may be sent and summed in bfloat16 or wider, within the bound.
No kernel may reach another device: no remote copies, remote signals or barrier semaphores. Data moves between devices by JAX's collectives and lax.ppermute only.
A program may use at most 128 MiB of HBM per device.

v0:
```python
import math

import jax
import jax.numpy as jnp
from jax import lax
from jax.sharding import PartitionSpec as P

user_prior = 0.3
activity_prior = 0.3
activity_scale = 1.0
item_prior = 0.3
popularity_prior = 0.3
popularity_scale = 1.0


def expected_gain(shape_values, rate_values):
    return jnp.exp(lax.digamma(shape_values) - jnp.log(rate_values)).astype(jnp.bfloat16)


def shards(
    counts, tile_user, tile_slot, live_tiles, touched, user_shape, user_rate, item_shape, item_rate
):
    tile_total = counts.shape[0]
    tile_edge = counts.shape[1]
    factors = user_shape.shape[1]
    user_blocks = user_shape.shape[0] // tile_edge
    item_blocks = item_shape.shape[0] // tile_edge
    owners = lax.axis_size("user")
    per_owner = touched.shape[1]
    slot_count = owners * per_owner
    item_mean = item_shape / item_rate
    item_total = lax.psum(jnp.sum(item_mean, axis=0), ("user", "item"))
    user_gain = expected_gain(user_shape, user_rate).reshape(user_blocks, tile_edge, factors)
    item_gain = expected_gain(item_shape, item_rate)
    shard_rows = lax.all_gather(item_gain, "user", axis=0, tiled=True)
    shard_blocks = shard_rows.reshape(owners * item_blocks, tile_edge, factors)
    block_index = (jnp.arange(owners, dtype=jnp.int32)[:, None] * item_blocks + touched).reshape(
        slot_count
    )
    fetched = shard_blocks[block_index]
    group_size = math.gcd(tile_total, 64)
    live_count = live_tiles[0]

    def add_group(counter, carry):
        user_acc, item_acc = carry
        first_tile = counter * group_size
        tile_counts = lax.dynamic_slice_in_dim(counts, first_tile, group_size, 0)
        user_index = lax.dynamic_slice_in_dim(tile_user, first_tile, group_size, 0)
        slot_index = lax.dynamic_slice_in_dim(tile_slot, first_tile, group_size, 0)
        live_mask = first_tile + jnp.arange(group_size, dtype=jnp.int32) < live_count
        user_rows = user_gain[user_index]
        item_rows = fetched[slot_index]
        denominator = jnp.einsum(
            "gek,gfk->gef", user_rows, item_rows, preferred_element_type=jnp.float32
        )
        keep_mask = (tile_counts > 0) & live_mask[:, None, None]
        ratios = jnp.where(keep_mask, tile_counts.astype(jnp.float32) / denominator, 0.0).astype(
            jnp.bfloat16
        )
        user_term = user_rows.astype(jnp.float32) * jnp.einsum(
            "gef,gfk->gek", ratios, item_rows, preferred_element_type=jnp.float32
        )
        item_term = item_rows.astype(jnp.float32) * jnp.einsum(
            "gef,gek->gfk", ratios, user_rows, preferred_element_type=jnp.float32
        )
        user_acc = user_acc.at[user_index].add(user_term)
        item_acc = item_acc.at[slot_index].add(item_term)
        return (user_acc, item_acc)

    initial = (
        jnp.zeros((user_blocks, tile_edge, factors), jnp.float32),
        jnp.zeros((slot_count, tile_edge, factors), jnp.float32),
    )
    turn_count = tile_total // group_size
    user_acc, item_acc = lax.fori_loop(0, turn_count, add_group, initial)
    dense_sums = (
        jnp.zeros((owners * item_blocks, tile_edge, factors), jnp.float32)
        .at[block_index]
        .add(item_acc)
    )
    item_sum = lax.psum_scatter(
        dense_sums.reshape(owners * item_blocks * tile_edge, factors),
        "user",
        scatter_dimension=0,
        tiled=True,
    )
    user_sum = lax.psum(user_acc.reshape(user_blocks * tile_edge, factors), "item")
    user_shape_new = user_prior + user_sum
    kappa_rate = activity_prior / activity_scale + jnp.sum(
        user_shape / user_rate, axis=1, keepdims=True
    )
    user_rate_new = (activity_prior + factors * user_prior) / kappa_rate + item_total
    user_total = lax.psum(jnp.sum(user_shape_new / user_rate_new, axis=0), "user")
    item_shape_new = item_prior + item_sum
    tau_rate = popularity_prior / popularity_scale + jnp.sum(item_mean, axis=1, keepdims=True)
    item_rate_new = (popularity_prior + factors * item_prior) / tau_rate + user_total
    item_elog = lax.digamma(item_shape_new) - jnp.log(item_rate_new)
    return (user_shape_new, user_rate_new, item_shape_new, item_elog)


def solution(mesh):
    return jax.shard_map(
        shards,
        mesh=mesh,
        in_specs=(
            P(("user", "item"), None, None),
            P(("user", "item")),
            P(("user", "item")),
            P(("user", "item")),
            P(("user", "item"), None),
            P("user", None),
            P("user", None),
            P(("user", "item"), None),
            P(("user", "item"), None),
        ),
        out_specs=(
            P("user", None),
            P("user", None),
            P(("user", "item"), None),
            P(("user", "item"), None),
        ),
        check_vma=False,
    )
```

profile of v0, /device:TPU:1, one launch (start us, length us, event | category | flops | bytes accessed | tf_op | source)
XLA Modules:
  0.0 494.1 jit_solution(14403094635809505106)
XLA Ops:
  7.2 6.1 %divide_reduce_fusion.2 = (f32[512]{0:T(512)}, f32[256]{0:T(256)}, bf16[512,256]{1,0:T(8,128)(2,1)}) fusion(f32[512,256]{1,0:T(8,128)} %param.18, f32[512,256]{1,0:T(8,128)} %param.19), kind=kLoop, calls=%fused_computation.56 | loop fusion | flops 10484992 | bytes 1313792 | tf_op jit(solution)/shard_map/reduce_sum | solution.py:95
  14.9 9.6 %fusion.12 = (bf16[1024,256]{1,0:T(8,128)(2,1)S(1)}, f32[1024]{0:T(1024)}) fusion(f32[1024,256]{1,0:T(8,128)} %param.17, f32[1024,256]{1,0:T(8,128)} %param.16), kind=kLoop, calls=%fused_computation.28 | loop fusion | flops 20708352 | bytes 2625536 | tf_op jit(solution)/shard_map/convert_element_type | solution.py:17
  24.4 44.0 %all-gather.2.cloned.1.call-done = bf16[8192,256]{1,0:T(8,128)(2,1)} async-done(((bf16[512,256]{1,0:T(8,128)(2,1)}), bf16[8192,256]{1,0:T(8,128)(2,1)}) %all-gather.2.cloned.1.call-update) | async-done | bytes 4194320 | tf_op jit(solution)/shard_map/all_gather | solution.py:35
  68.4 4.3 gather_fusion.2
  72.8 2.5 broadcast_in_dim.44
  75.2 256.8 %while.15 = (s32[]{:T(128)}, f32[8,128,256]{2,1,0:T(8,128)S(1)}, f32[32,128,256]{2,1,0:T(8,128)}, s32[256]{0:T(256)S(1)}, bf16[8,128,256]{2,1,0:T(8,128)(2,1)S(1...) while((s32[]{:T(128)}, f32[8,128,256]{2,1,0:T(8,128)S(1)}, ...), condition=%wide.region_3.0_spmd, body=%wide.region_0.3_spmd.sunk | while | flops 1635781120 | bytes 180366320 | solution.py:75
  75.3 2.8 gather_fusion
  78.1 4.4 gather_fusion.1
  82.5 4.8 fusion.39
  87.3 0.8 add_compare_fusion.2
  88.1 1.1 copy-done.3
  89.2 7.4 %convert_multiply_fusion.4 = f32[64,128,256]{2,1,0:T(8,128)} fusion(bf16[64,128,256]{2,1,0:T(8,128)(2,1)S(1)} %copy-done.1, bf16[64,128,256]{2,1,0:T(8,128)(2,1)S(1)} %copy-done.2, f32[64,128,128]{2,1,0:T(8,128)S(1)} %fusion.39, s32[256,128,128]{2,1,0:T(8,128)} %get-tuple-element.281, s32[]{:T(128)S(6)} %select_n.60, ...), kind=kOutput, calls=%fused_computation.7.clone.1 | convolution fusion | flops 547356672 | bytes 25165892 | tf_op jit(solution)/shard_map/while/body/eval_jaxpr/gef,gfk->gek/dot_general | solution.py:60
  96.6 12.4 %scatter_fusion = f32[8,128,256]{2,1,0:T(8,128)S(1)} fusion(f32[8,128,256]{2,1,0:T(8,128)S(1)} %get-tuple-element.264, s32[64]{0:T(128)S(1)} %get-tuple-element.248, f32[64,128,256]{2,1,0:T(8,128)} %convert_multiply_fusion.4), kind=kCustom, calls=%fused_computation.3.clone.1 | custom fusion | flops 2097152 | bytes 25166080 | tf_op jit(solution)/shard_map/while/body/eval_jaxpr/scatter-add | solution.py:66
  109.0 11.2 %convert_multiply_fusion.5 = f32[64,128,256]{2,1,0:T(8,128)} fusion(bf16[64,128,256]{2,1,0:T(8,128)(2,1)} %gather_fusion.1, bf16[64,128,256]{2,1,0:T(8,128)(2,1)} %gather_fusion, f32[64,128,128]{2,1,0:T(8,128)} %copy-done.3, s32[256,128,128]{2,1,0:T(8,128)} %get-tuple-element.281, s32[]{:T(128)S(6)} %select_n.60, pred[64]{0:T(512)(128)(4,1)S(1)} %add_compare_fusion.2), kind=kOutput, calls=%fused_computation.6.clone.1 | convolution fusion | flops 547356672 | bytes 25165892 | tf_op jit(solution)/shard_map/while/body/eval_jaxpr/gef,gek->gfk/dot_general | solution.py:63
  120.2 19.4 %scatter_fusion.1 = f32[32,128,256]{2,1,0:T(8,128)} fusion(f32[32,128,256]{2,1,0:T(8,128)} %get-tuple-element.265, s32[64]{0:T(128)S(1)} %get-tuple-element.249, f32[64,128,256]{2,1,0:T(8,128)} %convert_multiply_fusion.5), kind=kCustom, calls=%fused_computation.4.clone.1 | custom fusion | flops 2097152 | bytes 25166080 | tf_op jit(solution)/shard_map/while/body/eval_jaxpr/scatter-add | solution.py:67
  139.6 2.8 gather_fusion
  142.4 4.4 gather_fusion.1
  146.8 4.8 fusion.39
  151.6 0.8 add_compare_fusion.2
  152.4 1.1 copy-done.3
  153.5 7.4 %convert_multiply_fusion.4 = f32[64,128,256]{2,1,0:T(8,128)} fusion(bf16[64,128,256]{2,1,0:T(8,128)(2,1)S(1)} %copy-done.1, bf16[64,128,256]{2,1,0:T(8,128)(2,1)S(1)} %copy-done.2, f32[64,128,128]{2,1,0:T(8,128)S(1)} %fusion.39, s32[256,128,128]{2,1,0:T(8,128)} %get-tuple-element.281, s32[]{:T(128)S(6)} %select_n.60, ...), kind=kOutput, calls=%fused_computation.7.clone.1 | convolution fusion | flops 547356672 | bytes 25165892 | tf_op jit(solution)/shard_map/while/body/eval_jaxpr/gef,gfk->gek/dot_general | solution.py:60
  160.9 12.4 %scatter_fusion = f32[8,128,256]{2,1,0:T(8,128)S(1)} fusion(f32[8,128,256]{2,1,0:T(8,128)S(1)} %get-tuple-element.264, s32[64]{0:T(128)S(1)} %get-tuple-element.248, f32[64,128,256]{2,1,0:T(8,128)} %convert_multiply_fusion.4), kind=kCustom, calls=%fused_computation.3.clone.1 | custom fusion | flops 2097152 | bytes 25166080 | tf_op jit(solution)/shard_map/while/body/eval_jaxpr/scatter-add | solution.py:66
  173.3 11.2 %convert_multiply_fusion.5 = f32[64,128,256]{2,1,0:T(8,128)} fusion(bf16[64,128,256]{2,1,0:T(8,128)(2,1)} %gather_fusion.1, bf16[64,128,256]{2,1,0:T(8,128)(2,1)} %gather_fusion, f32[64,128,128]{2,1,0:T(8,128)} %copy-done.3, s32[256,128,128]{2,1,0:T(8,128)} %get-tuple-element.281, s32[]{:T(128)S(6)} %select_n.60, pred[64]{0:T(512)(128)(4,1)S(1)} %add_compare_fusion.2), kind=kOutput, calls=%fused_computation.6.clone.1 | convolution fusion | flops 547356672 | bytes 25165892 | tf_op jit(solution)/shard_map/while/body/eval_jaxpr/gef,gek->gfk/dot_general | solution.py:63
  184.5 19.3 %scatter_fusion.1 = f32[32,128,256]{2,1,0:T(8,128)} fusion(f32[32,128,256]{2,1,0:T(8,128)} %get-tuple-element.265, s32[64]{0:T(128)S(1)} %get-tuple-element.249, f32[64,128,256]{2,1,0:T(8,128)} %convert_multiply_fusion.5), kind=kCustom, calls=%fused_computation.4.clone.1 | custom fusion | flops 2097152 | bytes 25166080 | tf_op jit(solution)/shard_map/while/body/eval_jaxpr/scatter-add | solution.py:67
  203.9 2.8 gather_fusion
  206.7 4.4 gather_fusion.1
  211.1 4.9 fusion.39
  216.7 1.1 copy-done.3
  217.8 7.4 %convert_multiply_fusion.4 = f32[64,128,256]{2,1,0:T(8,128)} fusion(bf16[64,128,256]{2,1,0:T(8,128)(2,1)S(1)} %copy-done.1, bf16[64,128,256]{2,1,0:T(8,128)(2,1)S(1)} %copy-done.2, f32[64,128,128]{2,1,0:T(8,128)S(1)} %fusion.39, s32[256,128,128]{2,1,0:T(8,128)} %get-tuple-element.281, s32[]{:T(128)S(6)} %select_n.60, ...), kind=kOutput, calls=%fused_computation.7.clone.1 | convolution fusion | flops 547356672 | bytes 25165892 | tf_op jit(solution)/shard_map/while/body/eval_jaxpr/gef,gfk->gek/dot_general | solution.py:60
  225.2 12.4 %scatter_fusion = f32[8,128,256]{2,1,0:T(8,128)S(1)} fusion(f32[8,128,256]{2,1,0:T(8,128)S(1)} %get-tuple-element.264, s32[64]{0:T(128)S(1)} %get-tuple-element.248, f32[64,128,256]{2,1,0:T(8,128)} %convert_multiply_fusion.4), kind=kCustom, calls=%fused_computation.3.clone.1 | custom fusion | flops 2097152 | bytes 25166080 | tf_op jit(solution)/shard_map/while/body/eval_jaxpr/scatter-add | solution.py:66
  237.6 11.2 %convert_multiply_fusion.5 = f32[64,128,256]{2,1,0:T(8,128)} fusion(bf16[64,128,256]{2,1,0:T(8,128)(2,1)} %gather_fusion.1, bf16[64,128,256]{2,1,0:T(8,128)(2,1)} %gather_fusion, f32[64,128,128]{2,1,0:T(8,128)} %copy-done.3, s32[256,128,128]{2,1,0:T(8,128)} %get-tuple-element.281, s32[]{:T(128)S(6)} %select_n.60, pred[64]{0:T(512)(128)(4,1)S(1)} %add_compare_fusion.2), kind=kOutput, calls=%fused_computation.6.clone.1 | convolution fusion | flops 547356672 | bytes 25165892 | tf_op jit(solution)/shard_map/while/body/eval_jaxpr/gef,gek->gfk/dot_general | solution.py:63
  248.7 19.3 %scatter_fusion.1 = f32[32,128,256]{2,1,0:T(8,128)} fusion(f32[32,128,256]{2,1,0:T(8,128)} %get-tuple-element.265, s32[64]{0:T(128)S(1)} %get-tuple-element.249, f32[64,128,256]{2,1,0:T(8,128)} %convert_multiply_fusion.5), kind=kCustom, calls=%fused_computation.4.clone.1 | custom fusion | flops 2097152 | bytes 25166080 | tf_op jit(solution)/shard_map/while/body/eval_jaxpr/scatter-add | solution.py:67
  268.1 2.8 gather_fusion
  270.9 4.4 gather_fusion.1
  275.3 4.8 fusion.39
  281.0 1.1 copy-done.3
  282.1 7.4 %convert_multiply_fusion.4 = f32[64,128,256]{2,1,0:T(8,128)} fusion(bf16[64,128,256]{2,1,0:T(8,128)(2,1)S(1)} %copy-done.1, bf16[64,128,256]{2,1,0:T(8,128)(2,1)S(1)} %copy-done.2, f32[64,128,128]{2,1,0:T(8,128)S(1)} %fusion.39, s32[256,128,128]{2,1,0:T(8,128)} %get-tuple-element.281, s32[]{:T(128)S(6)} %select_n.60, ...), kind=kOutput, calls=%fused_computation.7.clone.1 | convolution fusion | flops 547356672 | bytes 25165892 | tf_op jit(solution)/shard_map/while/body/eval_jaxpr/gef,gfk->gek/dot_general | solution.py:60
  289.5 12.4 %scatter_fusion = f32[8,128,256]{2,1,0:T(8,128)S(1)} fusion(f32[8,128,256]{2,1,0:T(8,128)S(1)} %get-tuple-element.264, s32[64]{0:T(128)S(1)} %get-tuple-element.248, f32[64,128,256]{2,1,0:T(8,128)} %convert_multiply_fusion.4), kind=kCustom, calls=%fused_computation.3.clone.1 | custom fusion | flops 2097152 | bytes 25166080 | tf_op jit(solution)/shard_map/while/body/eval_jaxpr/scatter-add | solution.py:66
  301.8 11.2 %convert_multiply_fusion.5 = f32[64,128,256]{2,1,0:T(8,128)} fusion(bf16[64,128,256]{2,1,0:T(8,128)(2,1)} %gather_fusion.1, bf16[64,128,256]{2,1,0:T(8,128)(2,1)} %gather_fusion, f32[64,128,128]{2,1,0:T(8,128)} %copy-done.3, s32[256,128,128]{2,1,0:T(8,128)} %get-tuple-element.281, s32[]{:T(128)S(6)} %select_n.60, pred[64]{0:T(512)(128)(4,1)S(1)} %add_compare_fusion.2), kind=kOutput, calls=%fused_computation.6.clone.1 | convolution fusion | flops 547356672 | bytes 25165892 | tf_op jit(solution)/shard_map/while/body/eval_jaxpr/gef,gek->gfk/dot_general | solution.py:63
  313.0 19.0 %scatter_fusion.1 = f32[32,128,256]{2,1,0:T(8,128)} fusion(f32[32,128,256]{2,1,0:T(8,128)} %get-tuple-element.265, s32[64]{0:T(128)S(1)} %get-tuple-element.249, f32[64,128,256]{2,1,0:T(8,128)} %convert_multiply_fusion.5), kind=kCustom, calls=%fused_computation.4.clone.1 | custom fusion | flops 2097152 | bytes 25166080 | tf_op jit(solution)/shard_map/while/body/eval_jaxpr/scatter-add | solution.py:67
  332.0 1.0 copy-done
  333.2 4.3 broadcast_in_dim.45
  337.5 10.2 %scatter_fusion.2 = f32[64,128,256]{2,1,0:T(8,128)} fusion(f32[64,128,256]{2,1,0:T(8,128)} %broadcast_in_dim.45, s32[32]{0:T(128)S(1)} %copy-done.10, f32[32,128,256]{2,1,0:T(8,128)} %get-tuple-element.160), kind=kCustom, calls=%fused_computation.5 | custom fusion | flops 1048576 | bytes 12583040 | tf_op jit(solution)/shard_map/scatter-add | solution.py:79
  348.3 65.4 %psum.22 = f32[256]{0:T(256)S(1)} all-reduce(f32[256]{0:T(256)S(1)} %copy-done.8), channel_id=1, replica_groups=mesh['user'=16,'item'=8] {'user','item'}, use_global_device_ids=true, to_apply=%region_7.8 | all-reduce | flops 256 | bytes 2048 | tf_op jit(solution)/shard_map/psum | solution.py:32
  413.7 2.8 divide_reduce_fusion.1
  416.5 31.1 %psum.23 = f32[256]{0:T(256)S(1)} all-reduce(f32[256]{0:T(256)S(1)} %get-tuple-element.183), channel_id=1, replica_groups=mesh['user'=16,'item'=8] {'user'}, use_global_device_ids=true, to_apply=%region_12.13 | all-reduce | flops 256 | bytes 2048 | tf_op jit(solution)/shard_map/psum | solution.py:93
  447.6 34.5 %reduce-scatter.2.cloned.1.call-done = f32[512,256]{1,0:T(8,128)} async-done(((f32[8192,256]{1,0:T(8,128)}), f32[512,256]{1,0:T(8,128)}) %reduce-scatter.2.cloned.1.call-update) | async-done | bytes 524304 | tf_op jit(solution)/shard_map/reduce_scatter | solution.py:81
  482.1 5.4 %fusion.21 = (f32[512,256]{1,0:T(8,128)}, f32[512,256]{1,0:T(8,128)}) fusion(f32[512,256]{1,0:T(8,128)} %reduce-scatter.2.cloned.1.call-done, f32[256]{0:T(256)S(1)} %psum.23, f32[512]{0:T(512)S(1)} %add_divide_fusion.1), kind=kLoop, calls=%fused_computation.43 | loop fusion | flops 10223616 | bytes 1575936 | tf_op jit(solution)/shard_map/sub | solution.py:97
  (65 shorter events, 4.5 us)
Async XLA Ops:
  7.2 61.2 %all-gather.2.cloned.1.call-start = ((), (), s32[]{:S(2)}) async-start(), calls=%async_computation.1 | async-start | bytes 4456448 | tf_op jit(solution)/shard_map/all_gather | solution.py:35
  13.3 400.4 %all-reduce.2.cloned.1.call-start = ((), (), s32[]{:S(2)}) async-start(), calls=%async_computation.2 | async-start | bytes 2097152 | tf_op jit(solution)/shard_map/psum | solution.py:87
  14.3 0.6 copy-start.9
  68.4 6.8 %copy-start.6 = (s32[256]{0:T(256)S(1)}, s32[256]{0:T(256)}, u32[]{:S(2)}) copy-start(s32[256]{0:T(256)} %param.12) | copy-start | bytes 3076
  68.4 6.8 %copy-start.7 = (s32[256]{0:T(256)S(1)}, s32[256]{0:T(256)}, u32[]{:S(2)}) copy-start(s32[256]{0:T(256)} %param.13) | copy-start | bytes 3076
  82.5 6.8 %copy-start.1 = (bf16[64,128,256]{2,1,0:T(8,128)(2,1)S(1)}, bf16[64,128,256]{2,1,0:T(8,128)(2,1)}, u32[]{:S(2)}) copy-start(bf16[64,128,256]{2,1,0:T(8,128)(2,1)} %gather_fusion) | copy-start | bytes 12582916 | tf_op jit(solution)/shard_map/while
  82.5 6.8 %copy-start.2 = (bf16[64,128,256]{2,1,0:T(8,128)(2,1)S(1)}, bf16[64,128,256]{2,1,0:T(8,128)(2,1)}, u32[]{:S(2)}) copy-start(bf16[64,128,256]{2,1,0:T(8,128)(2,1)} %gather_fusion.1) | copy-start | bytes 12582916 | tf_op jit(solution)/shard_map/while
  87.3 1.9 copy-start.3
  146.8 6.8 %copy-start.1 = (bf16[64,128,256]{2,1,0:T(8,128)(2,1)S(1)}, bf16[64,128,256]{2,1,0:T(8,128)(2,1)}, u32[]{:S(2)}) copy-start(bf16[64,128,256]{2,1,0:T(8,128)(2,1)} %gather_fusion) | copy-start | bytes 12582916 | tf_op jit(solution)/shard_map/while
  146.8 6.8 %copy-start.2 = (bf16[64,128,256]{2,1,0:T(8,128)(2,1)S(1)}, bf16[64,128,256]{2,1,0:T(8,128)(2,1)}, u32[]{:S(2)}) copy-start(bf16[64,128,256]{2,1,0:T(8,128)(2,1)} %gather_fusion.1) | copy-start | bytes 12582916 | tf_op jit(solution)/shard_map/while
  151.6 1.9 copy-start.3
  211.0 6.8 %copy-start.1 = (bf16[64,128,256]{2,1,0:T(8,128)(2,1)S(1)}, bf16[64,128,256]{2,1,0:T(8,128)(2,1)}, u32[]{:S(2)}) copy-start(bf16[64,128,256]{2,1,0:T(8,128)(2,1)} %gather_fusion) | copy-start | bytes 12582916 | tf_op jit(solution)/shard_map/while
  211.0 6.8 %copy-start.2 = (bf16[64,128,256]{2,1,0:T(8,128)(2,1)S(1)}, bf16[64,128,256]{2,1,0:T(8,128)(2,1)}, u32[]{:S(2)}) copy-start(bf16[64,128,256]{2,1,0:T(8,128)(2,1)} %gather_fusion.1) | copy-start | bytes 12582916 | tf_op jit(solution)/shard_map/while
  215.9 1.9 copy-start.3
  275.3 6.8 %copy-start.1 = (bf16[64,128,256]{2,1,0:T(8,128)(2,1)S(1)}, bf16[64,128,256]{2,1,0:T(8,128)(2,1)}, u32[]{:S(2)}) copy-start(bf16[64,128,256]{2,1,0:T(8,128)(2,1)} %gather_fusion) | copy-start | bytes 12582916 | tf_op jit(solution)/shard_map/while
  275.3 6.8 %copy-start.2 = (bf16[64,128,256]{2,1,0:T(8,128)(2,1)S(1)}, bf16[64,128,256]{2,1,0:T(8,128)(2,1)}, u32[]{:S(2)}) copy-start(bf16[64,128,256]{2,1,0:T(8,128)(2,1)} %gather_fusion.1) | copy-start | bytes 12582916 | tf_op jit(solution)/shard_map/while
  280.1 1.9 copy-start.3
  332.0 1.0 copy-start
  333.0 149.1 %reduce-scatter.2.cloned.1.call-start = ((), (), s32[]{:S(2)}) async-start(), calls=%async_computation.3 | async-start | bytes 8912896 | tf_op jit(solution)/shard_map/reduce_scatter | solution.py:81
  333.2 4.3 copy-start.10
  347.7 0.6 copy-start.8
  347.7 66.0 %copy-start.5 = (f32[512]{0:T(512)S(1)}, f32[512]{0:T(512)}, u32[]{:S(2)}) copy-start(f32[512]{0:T(512)} %get-tuple-element.161) | copy-start | bytes 6148
  347.7 66.0 %copy-start.4 = (f32[1024]{0:T(1024)S(1)}, f32[1024]{0:T(1024)}, u32[]{:S(2)}) copy-start(f32[1024]{0:T(1024)} %get-tuple-element.189) | copy-start | bytes 12292
Sparse Core Ops, SparseCore 0:
  13.5 54.8 all-gather.1
  333.1 59.7 all-reduce.1
  396.3 85.7 reduce-scatter.1
where the time goes:
time: 496 us; the launch traced here: 494 us
  other arithmetic  165 us (33%)
  blocking collectives  96.5 us (19%)
  matrix products  93.6 us (19%)
  waiting for transfers between devices  78.6 us (16%)
  local copies, waits for them, and re-layouts  46.4 us (9%)
  between operations  13.8 us (3%)
    scatter-add x4, other arithmetic, add_group(): item_acc = item_acc.at[slot_index].add(item_term)  77 us
    psum x1, blocking collectives, shards(): item_total = lax.psum(jnp.sum(item_mean, axis=0), ('user', 'item'))  65.4 us
    scatter-add x4, other arithmetic, add_group(): user_acc = user_acc.at[user_index].add(user_term)  49.5 us
    dot_general x4, matrix products, add_group(): jnp.einsum('gef,gek->gfk', ratios, user_rows, preferred_element_type=jnp....  44.7 us
    all_gather x1, waiting for transfers between devices, shards(): shard_rows = lax.all_gather(item_gain, 'user', axis=0, tiled=True)  44 us
    reduce_scatter x1, waiting for transfers between devices, shards(): lax.psum_scatter(dense_sums.reshape(owners * item_blocks * tile_edge, fac...  34.5 us
    psum x1, blocking collectives, shards(): lax.psum(jnp.sum(user_shape_new / user_rate_new, axis=0), 'user')  31.1 us
    dot_general x4, matrix products, add_group(): jnp.einsum('gef,gfk->gek', ratios, item_rows, preferred_element_type=jnp....  29.5 us
  transfers between devices with their start and end apart: 3, of which 2 were waited for; matrix products, arithmetic and copies ran while one was open for 6% of the time, Pallas kernels for 0%

commit v1 on v0

v1 whole, which is shorter than its diff:
```python
import functools

import jax
import jax.numpy as jnp
from jax import lax
from jax.experimental import pallas as pl
from jax.experimental.pallas import tpu as pltpu
from jax.sharding import PartitionSpec as P

user_prior = 0.3
activity_prior = 0.3
activity_scale = 1.0
item_prior = 0.3
popularity_prior = 0.3
popularity_scale = 1.0

VMEM_BYTES = 60 << 20
EXTRA = 16
LANES = 128


def digamma_rest(x):
    w = x * (x + 3.0)
    steps = (2.0 * x + 3.0) * (2.0 * w + 2.0) / (w * (w + 2.0))
    inverse = 1.0 / (x + 4.0)
    z = inverse * inverse
    series = z * (1.0 / 12.0 - z * (1.0 / 120.0 - z * (1.0 / 252.0 - z * (1.0 / 240.0))))
    return steps + 0.5 * inverse + series


def digamma(x):
    return jnp.log(x + 4.0) - digamma_rest(x)


def gains_of(shape_values, rate_values, prior, strength):
    inverse_rate = 1.0 / rate_values
    gain = (shape_values + 4.0) * jnp.exp(-digamma_rest(shape_values)) * inverse_rate
    mean = shape_values * inverse_rate
    return gain.astype(jnp.bfloat16), strength / (prior + jnp.sum(mean, axis=1, keepdims=True)), mean


def item_gain_kernel(strength, touched_ref, shape_ref, rate_ref, gain_ref, level_ref, head_ref):
    turn = pl.program_id(0)
    gain_ref[...], level_ref[...], mean = gains_of(
        shape_ref[...], rate_ref[...], popularity_prior / popularity_scale, strength
    )
    devices, per_owner = touched_ref.shape
    total = jnp.broadcast_to(jnp.sum(mean, axis=0, keepdims=True), (devices, mean.shape[1]))

    @pl.when(turn == 0)
    def _():
        head_ref[:, pl.ds(0, per_owner)] = touched_ref[...].astype(jnp.float32)
        head_ref[:, pl.ds(LANES, mean.shape[1])] = total

    @pl.when(turn > 0)
    def _():
        head_ref[:, pl.ds(LANES, mean.shape[1])] += total


def item_gains(touched, item_shape, item_rate):
    rows, factors = item_shape.shape
    devices = touched.shape[0]
    step = rows // 2
    row_spec = pl.BlockSpec((step, factors), lambda r: (r, 0))
    return pl.pallas_call(
        functools.partial(item_gain_kernel, popularity_prior + factors * item_prior),
        grid=(rows // step,),
        in_specs=[pl.BlockSpec(touched.shape, lambda r: (0, 0)), row_spec, row_spec],
        out_specs=[
            row_spec,
            pl.BlockSpec((step, 1), lambda r: (r, 0)),
            pl.BlockSpec((devices, LANES + factors), lambda r: (0, 0)),
        ],
        out_shape=[
            jax.ShapeDtypeStruct((rows, factors), jnp.bfloat16),
            jax.ShapeDtypeStruct((rows, 1), jnp.float32),
            jax.ShapeDtypeStruct((devices, LANES + factors), jnp.float32),
        ],
        compiler_params=pltpu.CompilerParams(vmem_limit_bytes=VMEM_BYTES),
        cost_estimate=pl.CostEstimate(
            flops=40 * rows * factors, bytes_accessed=10 * rows * factors, transcendentals=4 * rows * factors
        ),
    )(touched, item_shape, item_rate)


def user_gain_kernel(strength, shape_ref, rate_ref, head_ref, gain_ref, level_ref, turned_ref, column_ref):
    gain, level_ref[...], _ = gains_of(shape_ref[...], rate_ref[...], activity_prior / activity_scale, strength)
    gain_ref[...] = gain
    turned_ref[...] = gain.T

    @pl.when(pl.program_id(0) == 0)
    def _():
        column_ref[...] = jnp.sum(head_ref[:, pl.ds(LANES, gain.shape[1])], axis=0, keepdims=True)


def user_gains(user_shape, user_rate, heads):
    rows, factors = user_shape.shape
    step = rows // 4
    row_spec = pl.BlockSpec((step, factors), lambda r: (r, 0))
    return pl.pallas_call(
        functools.partial(user_gain_kernel, activity_prior + factors * user_prior),
        grid=(rows // step,),
        in_specs=[row_spec, row_spec, pl.BlockSpec(heads.shape, lambda r: (0, 0))],
        out_specs=[
            row_spec,
            pl.BlockSpec((step, 1), lambda r: (r, 0)),
            pl.BlockSpec((factors, step), lambda r: (0, r)),
            pl.BlockSpec((1, factors), lambda r: (0, 0)),
        ],
        out_shape=[
            jax.ShapeDtypeStruct((rows, factors), jnp.bfloat16),
            jax.ShapeDtypeStruct((rows, 1), jnp.float32),
            jax.ShapeDtypeStruct((factors, rows), jnp.bfloat16),
            jax.ShapeDtypeStruct((1, factors), jnp.float32),
        ],
        compiler_params=pltpu.CompilerParams(vmem_limit_bytes=VMEM_BYTES),
        cost_estimate=pl.CostEstimate(
            flops=40 * rows * factors, bytes_accessed=12 * rows * factors, transcendentals=4 * rows * factors
        ),
    )(user_shape, user_rate, heads)


def pick_kernel(per_owner, head_ref, gain_ref, picked_ref):
    for device in range(head_ref.shape[0]):
        for place in range(per_owner):
            picked_ref[device * per_owner + place] = gain_ref[head_ref[device, place].astype(jnp.int32)]


def pick(heads, item_gain, edge, per_owner):
    items, factors = item_gain.shape
    devices = heads.shape[0]
    return pl.pallas_call(
        functools.partial(pick_kernel, per_owner),
        grid=(1,),
        in_specs=[
            pl.BlockSpec((devices, LANES), lambda step: (0, 0), memory_space=pltpu.SMEM),
            pl.BlockSpec((items // edge, edge, factors), lambda step: (0, 0, 0)),
        ],
        out_specs=pl.BlockSpec((devices * per_owner, edge, factors), lambda step: (0, 0, 0)),
        out_shape=jax.ShapeDtypeStruct((devices * per_owner, edge, factors), jnp.bfloat16),
        compiler_params=pltpu.CompilerParams(vmem_limit_bytes=VMEM_BYTES),
        cost_estimate=pl.CostEstimate(
            flops=0, bytes_accessed=2 * items * factors + 2 * devices * per_owner * edge * factors, transcendentals=0
        ),
    )(heads, item_gain.reshape(items // edge, edge, factors))


def dense_kernel(user_of, slot_of, live_ref, counts_ref, dense_ref, held_ref, arrived):
    depth, group = held_ref.shape[:2]
    live = live_ref[0]
    groups = (live + group - 1) // group

    def fetch(index):
        place = lax.rem(index, depth)
        return pltpu.make_async_copy(
            counts_ref.at[pl.ds(index * group, group)], held_ref.at[place], arrived.at[place]
        )

    for index in range(depth):

        @pl.when(index < groups)
        def _():
            fetch(index).start()

    def clear(slot, carry):
        dense_ref[slot] = jnp.zeros(dense_ref.shape[1:], dense_ref.dtype)
        return carry

    lax.fori_loop(0, dense_ref.shape[0], clear, 0)

    def add_group(index, carry):
        fetch(index).wait()
        place = lax.rem(index, depth)
        for offset in range(group):
            tile = index * group + offset

            @pl.when(tile < live)
            def _():
                user, slot = user_of[tile], slot_of[tile]
                dense_ref[slot, user] += held_ref[place, offset].astype(jnp.float32).astype(jnp.bfloat16)

        @pl.when(index + depth < groups)
        def _():
            fetch(index + depth).start()

        return carry

    lax.fori_loop(0, groups, add_group, 0)


def dense_counts(counts, tile_user, tile_slot, live_tiles, slot_count, user_blocks):
    tiles, edge, _ = counts.shape
    group = 8
    depth = min(8, tiles // group)
    dense_shape = (slot_count, user_blocks, edge, edge)
    return pl.pallas_call(
        dense_kernel,
        grid_spec=pltpu.PrefetchScalarGridSpec(
            num_scalar_prefetch=3,
            grid=(1,),
            in_specs=[pl.BlockSpec(memory_space=pl.ANY)],
            out_specs=pl.BlockSpec(dense_shape, lambda step, *_: (0, 0, 0, 0)),
            scratch_shapes=[
                pltpu.VMEM((depth, group, edge, edge), jnp.int32),
                pltpu.SemaphoreType.DMA((depth,)),
            ],
        ),
        out_shape=jax.ShapeDtypeStruct(dense_shape, jnp.bfloat16),
        compiler_params=pltpu.CompilerParams(vmem_limit_bytes=VMEM_BYTES),
        cost_estimate=pl.CostEstimate(
            flops=tiles * edge * edge, bytes_accessed=4 * counts.size + 2 * slot_count * user_blocks * edge * edge,
            transcendentals=0,
        ),
    )(tile_user, tile_slot, live_tiles, counts)


def split_rows(value, rows):
    high = value.astype(jnp.bfloat16).astype(jnp.float32)
    middle = (value - high).astype(jnp.bfloat16).astype(jnp.float32)
    low = value - high - middle
    row = lax.broadcasted_iota(jnp.int32, (rows, value.shape[1]), 0)
    block = jnp.where(row == 0, high, jnp.where(row == 1, middle, jnp.where(row == 2, low, 0.0)))
    return block.astype(jnp.bfloat16)


def sweep_kernel(
    prior_share, place_ref, dense_ref, items_ref, gain_ref, turned_ref, level_ref, total_ref, item_ref, *rest
):
    user_refs, acc_ref, ratio_ref = rest[:-2], rest[-2], rest[-1]
    turn = pl.program_id(0)
    per_step, touched_rows, factors = items_ref.shape
    slots, user_blocks, edge, _ = dense_ref.shape
    users = user_blocks * edge
    chunk = users // 2

    @pl.when(turn == 0)
    def _():
        acc_ref[...] = jnp.zeros_like(acc_ref)

    items = items_ref[...].reshape(per_step * touched_rows, factors)
    turned_items = items.T
    denominators = [
        jnp.dot(gain_ref[pl.ds(first, chunk), :], turned_items, preferred_element_type=jnp.float32)
        for first in range(0, users, chunk)
    ]
    for index, denominator in enumerate(denominators):
        blocks = pl.ds(index * (chunk // edge), chunk // edge)
        rows = pl.ds(index * chunk, chunk)
        counted = jnp.concatenate(
            [dense_ref[slot, blocks].reshape(chunk, edge) for slot in range(slots)], axis=1
        ).astype(jnp.float32)
        inverse = pl.reciprocal(denominator, approx=True)
        inverse *= 2.0 - denominator * inverse
        ratios = (counted * inverse).astype(jnp.bfloat16)
        ratio_ref[rows, :] = ratios
        acc_ref[rows, :] += jnp.dot(ratios, items, preferred_element_type=jnp.float32)
    sums = jnp.dot(turned_ref[...], ratio_ref[...], preferred_element_type=jnp.float32)
    sums = sums.astype(jnp.bfloat16).T
    for owner in range(per_step):
        item_ref[turn * per_step + owner, pl.ds(0, touched_rows), :] = sums[
            owner * touched_rows : (owner + 1) * touched_rows
        ]

    @pl.when(turn == pl.num_programs(0) - 1)
    def _():
        own = users // len(user_refs)
        part = jnp.zeros((1, factors), jnp.float32)
        for ahead, user_ref in enumerate(user_refs):
            target = (place_ref[0] + ahead) % len(user_refs)
            rows = pl.ds(pl.multiple_of(target * own, own), own)
            user_sums = acc_ref[rows, :]
            user_ref[...] = user_sums.astype(jnp.bfloat16)
            shape_share = prior_share + gain_ref[rows, :].astype(jnp.float32) * user_sums
            part += jnp.sum(shape_share / (level_ref[rows, :] + total_ref[...]), axis=0, keepdims=True)
        extra = split_rows(part, EXTRA)
        for owner in range(item_ref.shape[0]):
            item_ref[owner, pl.ds(touched_rows, EXTRA), :] = extra


def sweep(place, dense, items, user_gain, turned_gain, user_level, item_total, parts):
    owners, touched_rows, factors = items.shape
    users = user_gain.shape[0]
    user_blocks, edge = dense.shape[1:3]
    per_owner = touched_rows // edge
    per_step = 2
    own = users // parts
    whole = lambda turn, place_ref: (0, 0)
    out = pl.pallas_call(
        functools.partial(sweep_kernel, user_prior / parts),
        grid_spec=pltpu.PrefetchScalarGridSpec(
            num_scalar_prefetch=1,
            grid=(owners // per_step,),
            in_specs=[
                pl.BlockSpec(
                    (per_step * per_owner, user_blocks, edge, edge), lambda turn, place_ref: (turn, 0, 0, 0)
                ),
                pl.BlockSpec((per_step, touched_rows, factors), lambda turn, place_ref: (turn, 0, 0)),
                pl.BlockSpec((users, factors), whole),
                pl.BlockSpec((factors, users), whole),
                pl.BlockSpec((users, 1), whole),
                pl.BlockSpec((1, factors), whole),
            ],
            out_specs=[pl.BlockSpec((owners, touched_rows + EXTRA, factors), lambda turn, place_ref: (0, 0, 0))]
            + [pl.BlockSpec((own, factors), whole)] * parts,
            scratch_shapes=[
                pltpu.VMEM((users, factors), jnp.float32),
                pltpu.VMEM((users, per_step * touched_rows), jnp.bfloat16),
            ],
        ),
        out_shape=[jax.ShapeDtypeStruct((owners, touched_rows + EXTRA, factors), jnp.bfloat16)]
        + [jax.ShapeDtypeStruct((own, factors), jnp.bfloat16)] * parts,
        compiler_params=pltpu.CompilerParams(vmem_limit_bytes=VMEM_BYTES),
        cost_estimate=pl.CostEstimate(
            flops=6 * owners * touched_rows * users * factors,
            bytes_accessed=2 * dense.size + 4 * items.size + 4 * users * factors,
            transcendentals=owners * touched_rows * users,
        ),
    )(place, dense, items, user_gain, turned_gain, user_level, item_total)
    return out[0], out[1:]


def own_kernel(place_ref, gain_ref, *rest):
    sums_refs, sum_ref = rest[:-1], rest[-1]
    sums = jnp.zeros(gain_ref.shape, jnp.float32)
    for sums_ref in sums_refs:
        sums += sums_ref[...].astype(jnp.float32)
    sum_ref[...] = (gain_ref[...].astype(jnp.float32) * sums).astype(jnp.bfloat16)


def own_users(place, sums, user_gain):
    own, factors = sums[0].shape
    first = lambda step, place_ref: (0, 0)
    return pl.pallas_call(
        own_kernel,
        grid_spec=pltpu.PrefetchScalarGridSpec(
            num_scalar_prefetch=1,
            grid=(1,),
            in_specs=[pl.BlockSpec((own, factors), lambda step, place_ref: (place_ref[0], 0))]
            + [pl.BlockSpec((own, factors), first)] * len(sums),
            out_specs=pl.BlockSpec((own, factors), first),
        ),
        out_shape=jax.ShapeDtypeStruct((own, factors), jnp.bfloat16),
        compiler_params=pltpu.CompilerParams(vmem_limit_bytes=VMEM_BYTES),
        cost_estimate=pl.CostEstimate(
            flops=2 * len(sums) * own * factors, bytes_accessed=2 * len(sums) * own * factors, transcendentals=0
        ),
    )(place, user_gain, *sums)


def fold_kernel(sums_ref, part_ref):
    extra = sums_ref[0].astype(jnp.float32)
    for sender in range(1, sums_ref.shape[0]):
        extra += sums_ref[sender].astype(jnp.float32)
    part_ref[...] = jnp.sum(extra, axis=0, keepdims=True)


def fold(sums):
    senders, extended, factors = sums.shape
    return pl.pallas_call(
        fold_kernel,
        grid=(1,),
        in_specs=[pl.BlockSpec((senders, EXTRA, factors), lambda step: (0, extended // EXTRA - 1, 0))],
        out_specs=pl.BlockSpec((1, factors), lambda step: (0, 0)),
        out_shape=jax.ShapeDtypeStruct((1, factors), jnp.float32),
        compiler_params=pltpu.CompilerParams(vmem_limit_bytes=VMEM_BYTES // 2),
        cost_estimate=pl.CostEstimate(flops=0, bytes_accessed=2 * senders * EXTRA * factors, transcendentals=0),
    )(sums)


def item_kernel(per_owner, head_ref, sums_ref, gain_ref, level_ref, total_ref, shape_ref, elog_ref, acc_ref):
    edge = acc_ref.shape[1]
    user_total = jnp.sum(total_ref[...], axis=0, keepdims=True)
    acc_ref[...] = jnp.zeros_like(acc_ref)
    for sender in range(sums_ref.shape[0]):
        for place in range(per_owner):
            block = head_ref[sender, place].astype(jnp.int32)
            acc_ref[block] += sums_ref[sender, pl.ds(place * edge, edge), :].astype(jnp.float32)
    for block in range(acc_ref.shape[0]):
        rows = pl.ds(block * edge, edge)
        shape_new = item_prior + gain_ref[rows, :].astype(jnp.float32) * acc_ref[block]
        shape_ref[rows, :] = shape_new
        rate_new = level_ref[rows, :] + user_total
        elog_ref[rows, :] = digamma(shape_new) - jnp.log(rate_new)


def item_update(heads, sums, item_gain, item_level, user_parts, edge):
    items, factors = item_gain.shape
    senders, extended, _ = sums.shape
    per_owner = (extended - EXTRA) // edge
    whole = lambda step: (0, 0)
    return pl.pallas_call(
        functools.partial(item_kernel, per_owner),
        grid=(1,),
        in_specs=[
            pl.BlockSpec((senders, LANES), whole, memory_space=pltpu.SMEM),
            pl.BlockSpec(sums.shape, lambda step: (0, 0, 0)),
            pl.BlockSpec((items, factors), whole),
            pl.BlockSpec((items, 1), whole),
            pl.BlockSpec(user_parts.shape, whole),
        ],
        out_specs=[pl.BlockSpec((items, factors), whole)] * 2,
        scratch_shapes=[pltpu.VMEM((items // edge, edge, factors), jnp.float32)],
        out_shape=[jax.ShapeDtypeStruct((items, factors), jnp.float32)] * 2,
        compiler_params=pltpu.CompilerParams(vmem_limit_bytes=VMEM_BYTES // 2),
        cost_estimate=pl.CostEstimate(
            flops=40 * items * factors, bytes_accessed=2 * sums.size + 10 * items * factors,
            transcendentals=4 * items * factors,
        ),
    )(heads, sums, item_gain, item_level, user_parts)


def shards(
    counts, tile_user, tile_slot, live_tiles, touched, user_shape, user_rate, item_shape, item_rate
):
    edge = counts.shape[1]
    users, factors = user_shape.shape
    user_blocks = users // edge
    owners, per_owner = touched.shape
    columns = lax.axis_size("item")
    place = lax.axis_index("item").astype(jnp.int32).reshape(1)
    item_gain, item_level, heads = item_gains(touched, item_shape, item_rate)
    heads = lax.all_to_all(heads, "user", 0, 0, tiled=True)
    item_rows = pick(heads, item_gain, edge, per_owner).reshape(owners, per_owner * edge, factors)
    item_rows = lax.all_to_all(item_rows, "user", 0, 0, tiled=True)
    user_gain, user_level, turned_gain, column_total = user_gains(user_shape, user_rate, heads)
    item_total = jnp.sum(lax.all_gather(column_total, "item", axis=0, tiled=True), axis=0, keepdims=True)
    dense = dense_counts(counts, tile_user, tile_slot, live_tiles, owners * per_owner, user_blocks)
    item_sums, user_sums = sweep(
        place, dense, item_rows, user_gain, turned_gain, user_level, item_total, columns
    )
    item_sums = lax.all_to_all(item_sums, "user", 0, 0, tiled=True)
    user_sums = [user_sums[0]] + [
        lax.ppermute(user_sums[k], "item", [(j, (j + k) % columns) for j in range(columns)])
        for k in range(1, columns)
    ]
    user_sum = lax.all_gather(own_users(place, user_sums, user_gain), "item", axis=0, tiled=True)
    user_shape_new = user_prior + user_sum.astype(jnp.float32)
    user_rate_new = user_level + item_total
    user_parts = lax.all_gather(fold(item_sums), "item", axis=0, tiled=True)
    item_shape_new, item_elog = item_update(heads, item_sums, item_gain, item_level, user_parts, edge)
    return (user_shape_new, user_rate_new, item_shape_new, item_elog)


def solution(mesh):
    return jax.shard_map(
        shards,
        mesh=mesh,
        in_specs=(
            P(("user", "item"), None, None),
            P(("user", "item")),
            P(("user", "item")),
            P(("user", "item")),
            P(("user", "item"), None),
            P("user", None),
            P("user", None),
            P(("user", "item"), None),
            P(("user", "item"), None),
        ),
        out_specs=(
            P("user", None),
            P("user", None),
            P(("user", "item"), None),
            P(("user", "item"), None),
        ),
        check_vma=False,
    )
```

time: 496 us -> 124 us (0.25)
  other arithmetic: 165 us -> 3 us
  matrix products: 93.6 us -> 0 us
  waiting for transfers between devices: 78.6 us -> 7.67 us
  blocking collectives: 96.5 us -> 50.4 us
  local copies, waits for them, and re-layouts: 46.4 us -> 4.73 us
  Pallas kernels: 0 us -> 33.7 us
  starting transfers between devices: 0.3 us -> 21.3 us
  between operations: 13.8 us -> 1.48 us
    scatter-add x9 -> x0, other arithmetic: 137 us -> none  [the longest x4 77 us: add_group(): item_acc = item_acc.at[slot_index].add(item_term)]
    psum x2 -> x0, blocking collectives: 96.5 us -> none  [the longest x1 65.4 us: shards(): item_total = lax.psum(jnp.sum(item_mean, axis=0), ('user', 'item'))]
    dot_general x12 -> x0, matrix products: 93.6 us -> none  [the longest x4 44.7 us: add_group(): jnp.einsum('gef,gek->gfk', ratios, user_rows, preferred_element_type=jnp....]
    all_gather x1 -> x0, waiting for transfers between devices: 44 us -> none  [shards(): shard_rows = lax.all_gather(item_gain, 'user', axis=0, tiled=True)]
    all_gather x0 -> x3, blocking collectives: none -> 35.8 us  [the longest x1 13.2 us: shards(): lax.all_gather(own_users(place, user_sums, user_gain), 'item', axis=0, ti...]
    reduce_scatter x1 -> x0, waiting for transfers between devices: 34.5 us -> none  [shards(): lax.psum_scatter(dense_sums.reshape(owners * item_blocks * tile_edge, fac...]
    pallas_call x0 -> x8, Pallas kernels: none -> 33.7 us  [the longest x1 13.7 us: sweep(): pl.pallas_call(functools.partial(sweep_kernel, user_prior / parts), grid_...]
    gather x9 -> x0, local copies, waits for them, and re-layouts: 32.9 us -> none  [the longest x4 17.4 us: add_group(): item_rows = fetched[slot_index]]
  transfers between devices with their start and end apart: 3 -> 9, of which waited for: 2 -> 5; matrix products, arithmetic and copies ran while one was open for 6% -> 2% of each run, Pallas kernels for 0% -> 10%
where the time goes in v1:
time: 124 us; the launch traced here: 122 us
  blocking collectives  50.4 us (41%)
  Pallas kernels  33.7 us (27%)
  starting transfers between devices  21.3 us (17%)
  waiting for transfers between devices  7.67 us (6%)
  local copies, waits for them, and re-layouts  4.73 us (4%)
  other arithmetic  3 us (2%)
  between operations  1.48 us (1%)
    all_to_all x1, blocking collectives, shards(): heads = lax.all_to_all(heads, 'user', 0, 0, tiled=True)  14.7 us
    pallas_call x1, Pallas kernels, sweep(): pl.pallas_call(functools.partial(sweep_kernel, user_prior / parts), grid_...  13.7 us
    all_gather x1, blocking collectives, shards(): lax.all_gather(own_users(place, user_sums, user_gain), 'item', axis=0, ti...  13.2 us
    all_gather x1, blocking collectives, shards(): lax.all_gather(column_total, 'item', axis=0, tiled=True)  13 us
    ppermute x7, starting transfers between devices, shards(): lax.ppermute(user_sums[k], 'item', [(j, (j + k) % columns) for j in range...  9.83 us
    all_gather x1, blocking collectives, shards(): user_parts = lax.all_gather(fold(item_sums), 'item', axis=0, tiled=True)  9.63 us
    all_to_all x1, starting transfers between devices, shards(): item_sums = lax.all_to_all(item_sums, 'user', 0, 0, tiled=True)  7.75 us
    pallas_call x1, Pallas kernels, dense_counts(): pl.pallas_call(dense_kernel, grid_spec=pltpu.PrefetchScalarGridSpec(num_s...  6.31 us
  transfers between devices with their start and end apart: 9, of which 5 were waited for; matrix products, arithmetic and copies ran while one was open for 2% of the time, Pallas kernels for 10%

profile of v1, /device:TPU:1, one launch (start us, length us, event | category | flops | bytes accessed | tf_op | source)
XLA Modules:
  0.0 122.3 jit_solution(15841619370500302827)
XLA Ops:
  0.6 1.4 %copy.15.touched_ref = s32[16,2]{1,0:T(8,128)} copy(s32[16,2]{0,1:T(2,128)} %param.13) | data formatting | bytes 256 | tf_op args[4]
  2.0 2.5 %shard_map.120 = (bf16[512,256]{1,0:T(8,128)(2,1)}, f32[512,1]{1,0:T(8,128)}, f32[16,384]{1,0:T(8,128)}) custom-call(s32[16,2]{1,0:T(8,128)} %copy.15.touched_ref, f32[512,256]{1,0:T(8,128)} %shape_ref.2, f32[512,256]{1,0:T(8,128)} %rate_ref.2), custom_call_target="tpu_custom_call" | custom-call | flops 5242880 | bytes 1310720 | tf_op jit(solution)/shard_map/pallas_call | solution.py:65
  4.4 0.8 copy.16
  5.2 14.7 %all_to_all.21 = f32[16,1,384]{2,1,0:T(1,128)S(1)} all-to-all(f32[16,1,384]{2,1,0:T(1,128)S(1)} %copy.16), channel_id=1, replica_groups=mesh['user'=16,'item'=8] {'user'}, dimensions={0} | all-to-all | bytes 49152 | tf_op jit(solution)/shard_map/all_to_all | solution.py:422
  19.9 0.6 copy.21
  20.5 2.5 %shard_map.123 = bf16[32,128,256]{2,1,0:T(8,128)(2,1)} custom-call(f32[16,384]{1,0:T(8,128)} %bitcast.14, bf16[4,128,256]{2,1,0:T(8,128)(2,1)} %bitcast.13), custom_call_target="tpu_custom_call" | custom-call | bytes 2359296 | tf_op jit(solution)/shard_map/pallas_call | solution.py:132
  23.0 3.7 %all-to-all-start.1 = ((bf16[16,256,256]{2,1,0:T(8,128)(2,1)}), bf16[16,256,256]{2,1,0:T(8,128)(2,1)S(1)}, u32[]{:S(2)}, u32[]{:S(2)}) async-start(bf16[16,256,256]{2,1,0:T(8,128)(2,1)} %bitcast.19), calls=%async_computation.1 | async-start | bytes 4194304 | tf_op jit(solution)/shard_map/all_to_all | solution.py:424
  27.3 6.3 %shard_map.122.dense_ref = bf16[32,8,128,128]{3,2,1,0:T(8,128)(2,1)} custom-call(s32[256]{0:T(256)} %user_of.1, s32[256]{0:T(256)} %slot_of.1, s32[1]{0:T(128)S(6)} %copy.23.live_ref, s32[256,128,128]{2,1,0:T(8,128)} %counts_ref.1), custom_call_target="tpu_custom_call" | custom-call | flops 4194304 | bytes 25165824 | tf_op jit(solution)/shard_map/pallas_call | solution.py:196
  33.7 4.3 %shard_map.121 = (bf16[1024,256]{1,0:T(8,128)(2,1)}, f32[1024,1]{1,0:T(8,128)}, bf16[256,1024]{1,0:T(8,128)(2,1)}, f32[1,256]{1,0:T(1,128)}) custom-call(f32[1024,256]{1,0:T(8,128)} %shape_ref.3, f32[1024,256]{1,0:T(8,128)} %rate_ref.3, f32[16,384]{1,0:T(8,128)} %bitcast.15), custom_call_target="tpu_custom_call" | custom-call | flops 10485760 | bytes 3145728 | tf_op jit(solution)/shard_map/pallas_call | solution.py:100
  38.0 13.0 %all-gather = f32[8,1,256]{2,1,0:T(1,128)S(1)} all-gather(f32[1,1,256]{2,1,0:T(1,128)} %bitcast.22), channel_id=1, replica_groups=mesh['user'=16,'item'=8] {'item'}, dimensions={0}, use_global_device_ids=true | all-gather | bytes 9216 | tf_op jit(solution)/shard_map/all_gather | solution.py:426
  50.9 0.6 reduce_sum.9
  51.5 2.0 %all-to-all-done.1.items_ref = bf16[16,256,256]{2,1,0:T(8,128)(2,1)S(1)} async-done(((bf16[16,256,256]{2,1,0:T(8,128)(2,1)}), bf16[16,256,256]{2,1,0:T(8,128)(2,1)S(1)}, u32[]{:S(2)}, u32[]{:S(2)}) %all-to-all-start.1) | async-done | bytes 2097184 | tf_op jit(solution)/shard_map/all_to_all | solution.py:424
  53.5 1.4 %copy-done.3 = bf16[16,256,256]{2,1,0:T(8,128)(2,1)} copy-done((bf16[16,256,256]{2,1,0:T(8,128)(2,1)}, bf16[16,256,256]{2,1,0:T(8,128)(2,1)S(1)}, u32[]{:S(2)}) %copy-start.3) | copy-done | bytes 2097176
  54.8 13.7 %shard_map.124 = (bf16[16,272,256]{2,1,0:T(8,128)(2,1)}, bf16[128,256]{1,0:T(8,128)(2,1)}, bf16[128,256]{1,0:T(8,128)(2,1)}, bf16[128,256]{1,0:T(8,128)(2,1)}, b...) custom-call(s32[1]{0:T(128)} %bitcast.place_ref, ...), custom_call_target="tpu_custom_call" | custom-call | flops 6442450944 | bytes 13631488 | tf_op jit(solution)/shard_map/pallas_call | solution.py:288
  68.5 0.0 copy-start.19
  68.5 0.0 copy-start.18
  68.5 0.0 copy-start.4
  68.5 0.0 copy-start.17
  68.5 0.0 copy-start.16
  68.6 0.0 copy-start.15
  68.6 7.7 %all-to-all-start.2 = ((bf16[16,272,256]{2,1,0:T(8,128)(2,1)}), bf16[16,272,256]{2,1,0:T(8,128)(2,1)S(1)}, u32[]{:S(2)}, u32[]{:S(2)}) async-start(bf16[16,272,256]{2,1,0:T(8,128)(2,1)} %get-tuple-element.36), calls=%async_computation.2 | async-start | bytes 4456448 | tf_op jit(solution)/shard_map/all_to_all | solution.py:431
  76.4 2.0 %collective-permute-start = (bf16[128,256]{1,0:T(8,128)(2,1)S(1)}, bf16[128,256]{1,0:T(8,128)(2,1)S(1)}, u32[]{:S(2)}, u32[]{:S(2)}) collective-permute-start(bf16[128,256]{1,0:T(8,128)(2,1)S(1)} %copy-done.19), channel_id=1, source_target_pairs={{0,1},{1,2},{2,3},{3,4},{4,5},{5,6},{6,7},{7,0},{8,9},{9,10},{10,1... | collective-permute-start | bytes 196616 | tf_op jit(solution)/shard_map/ppermute | solution.py:433
  78.4 1.3 %collective-permute-start.1 = (bf16[128,256]{1,0:T(8,128)(2,1)S(1)}, bf16[128,256]{1,0:T(8,128)(2,1)S(1)}, u32[]{:S(2)}, u32[]{:S(2)}) collective-permute-start(bf16[128,256]{1,0:T(8,128)(2,1)S(1)} %copy-done.18), channel_id=1, source_target_pairs={{0,2},{1,3},{2,4},{3,5},{4,6},{5,7},{6,0},{7,1},{8,10},{9,11},{10,... | collective-permute-start | bytes 196616 | tf_op jit(solution)/shard_map/ppermute | solution.py:433
  79.7 0.2 reduce.1
  79.9 0.0 copy-done.17
  79.9 1.8 %collective-permute-start.2 = (bf16[128,256]{1,0:T(8,128)(2,1)S(1)}, bf16[128,256]{1,0:T(8,128)(2,1)S(1)}, u32[]{:S(2)}, u32[]{:S(2)}) collective-permute-start(bf16[128,256]{1,0:T(8,128)(2,1)S(1)} %copy-done.17), channel_id=1, source_target_pairs={{0,3},{1,4},{2,5},{3,6},{4,7},{5,0},{6,1},{7,2},{8,11},{9,12},{10,... | collective-permute-start | bytes 196616 | tf_op jit(solution)/shard_map/ppermute | solution.py:433
  81.6 0.4 collective-permute-start.3
  82.0 1.9 %collective-permute-start.4 = (bf16[128,256]{1,0:T(8,128)(2,1)S(1)}, bf16[128,256]{1,0:T(8,128)(2,1)S(1)}, u32[]{:S(2)}, u32[]{:S(2)}) collective-permute-start(bf16[128,256]{1,0:T(8,128)(2,1)S(1)} %copy-done.15), channel_id=1, source_target_pairs={{0,5},{1,6},{2,7},{3,0},{4,1},{5,2},{6,3},{7,4},{8,13},{9,14},{10,... | collective-permute-start | bytes 196616 | tf_op jit(solution)/shard_map/ppermute | solution.py:433
  83.9 0.0 collective-permute-done.rest_1_
  83.9 0.9 collective-permute-start.5
  84.8 0.0 collective-permute-done.1.rest_2_
  84.8 0.0 copy-done.13
  84.8 1.6 %collective-permute-start.6 = (bf16[128,256]{1,0:T(8,128)(2,1)S(1)}, bf16[128,256]{1,0:T(8,128)(2,1)S(1)}, u32[]{:S(2)}, u32[]{:S(2)}) collective-permute-start(bf16[128,256]{1,0:T(8,128)(2,1)S(1)} %copy-done.13), channel_id=1, source_target_pairs={{0,7},{1,0},{2,1},{3,2},{4,3},{5,4},{6,5},{7,6},{8,15},{9,8},{10,9... | collective-permute-start | bytes 196616 | tf_op jit(solution)/shard_map/ppermute | solution.py:433
  86.4 0.0 copy-done.12
  86.4 1.2 broadcast_add_fusion
  87.6 0.0 collective-permute-done.2.rest_3_
  87.6 0.0 collective-permute-done.3.rest_4_
  87.6 0.3 collective-permute-done.4.rest_5_
  88.0 0.1 collective-permute-done.5.rest_6_
  88.1 1.5 %collective-permute-done.6.rest_7_ = bf16[128,256]{1,0:T(8,128)(2,1)S(1)} collective-permute-done((bf16[128,256]{1,0:T(8,128)(2,1)S(1)}, bf16[128,256]{1,0:T(8,128)(2,1)S(1)}, u32[]{:S(2)}, u32[]{:S(2)}) %collective-permute-start.6) | collective-permute-done | bytes 65568 | tf_op jit(solution)/shard_map/ppermute | solution.py:433
  89.6 0.0 copy-done.5
  89.7 0.6 copy-done.11
  90.3 1.8 %shard_map.125 = bf16[128,256]{1,0:T(8,128)(2,1)} custom-call(s32[1]{0:T(128)} %bitcast.place_ref, bf16[1024,256]{1,0:T(8,128)(2,1)} %get-tuple-element.23.gain_ref, bf16[128,256]{1,0:T(8,128)(2,1)} %get-tuple-element.28.rest_0_, bf16[128,256]{1,0:T(8,128)(2,1)} %copy-done.5, bf16[128,256]{1,0:T(8,128)(2,1)} %copy-done.6, bf16[128,256]{1,0:T(8,128)(2,1)} %copy-done.7, ...), custom_call_target="tpu_custom_call" | custom-call | flops 524288 | bytes 524288 | tf_op jit(solution)/shard_map/pallas_call | solution.py:333
  92.1 13.2 %all_gather.10 = bf16[1024,256]{1,0:T(8,128)(2,1)S(1)} all-gather(bf16[128,256]{1,0:T(8,128)(2,1)} %shard_map.125), channel_id=1, replica_groups=mesh['user'=16,'item'=8] {'item'}, dimensions={0}, use_global_device_ids=true | all-gather | bytes 589824 | tf_op jit(solution)/shard_map/all_gather | solution.py:436
  105.2 1.1 convert_add_fusion
  106.3 3.7 %all-to-all-done.2.sums_ref = bf16[16,272,256]{2,1,0:T(8,128)(2,1)S(1)} async-done(((bf16[16,272,256]{2,1,0:T(8,128)(2,1)}), bf16[16,272,256]{2,1,0:T(8,128)(2,1)S(1)}, u32[]{:S(2)}, u32[]{:S(2)}) %all-to-all-start.2) | async-done | bytes 2228256 | tf_op jit(solution)/shard_map/all_to_all | solution.py:431
  110.0 9.6 %all-gather.1 = f32[8,1,256]{2,1,0:T(1,128)S(1)} all-gather(f32[1,1,256]{2,1,0:T(1,128)S(1)} %bitcast.18), channel_id=1, replica_groups=mesh['user'=16,'item'=8] {'item'}, dimensions={0}, use_global_device_ids=true | all-gather | bytes 9216 | tf_op jit(solution)/shard_map/all_gather | solution.py:439
  119.7 2.7 %shard_map.127 = (f32[512,256]{1,0:T(8,128)}, f32[512,256]{1,0:T(8,128)}) custom-call(f32[16,384]{1,0:T(8,128)S(1)} %bitcast.16, bf16[16,272,256]{2,1,0:T(8,128)(2,1)S(1)} %all-to-all-done.2.sums_ref, bf16[512,256]{1,0:T(8,128)(2,1)S(1)} %copy-done, f32[512,1]{1,0:T(8,128)S(1)} %copy-done.2, f32[8,256]{1,0:T(8,128)S(1)} %bitcast.17), custom_call_target="tpu_custom_call" | custom-call | flops 5242880 | bytes 3538944 | tf_op jit(solution)/shard_map/pallas_call | solution.py:391
  (30 shorter events, 0.1 us)
Async XLA Ops:
  23.0 30.5 %all-to-all-start.1 = ((bf16[16,256,256]{2,1,0:T(8,128)(2,1)}), bf16[16,256,256]{2,1,0:T(8,128)(2,1)S(1)}, u32[]{:S(2)}, u32[]{:S(2)}) async-start(bf16[16,256,256]{2,1,0:T(8,128)(2,1)} %bitcast.19), calls=%async_computation.1 | async-start | bytes 4194304 | tf_op jit(solution)/shard_map/all_to_all | solution.py:424
  53.5 1.4 %copy-start.3 = (bf16[16,256,256]{2,1,0:T(8,128)(2,1)}, bf16[16,256,256]{2,1,0:T(8,128)(2,1)S(1)}, u32[]{:S(2)}) copy-start(bf16[16,256,256]{2,1,0:T(8,128)(2,1)S(1)} %all-to-all-done.1.items_ref) | copy-start | bytes 6291460
  68.5 7.9 %copy-start.19 = (bf16[128,256]{1,0:T(8,128)(2,1)S(1)}, bf16[128,256]{1,0:T(8,128)(2,1)}, u32[]{:S(2)}) copy-start(bf16[128,256]{1,0:T(8,128)(2,1)} %get-tuple-element.29) | copy-start | bytes 196612
  68.5 9.8 %copy-start.18 = (bf16[128,256]{1,0:T(8,128)(2,1)S(1)}, bf16[128,256]{1,0:T(8,128)(2,1)}, u32[]{:S(2)}) copy-start(bf16[128,256]{1,0:T(8,128)(2,1)} %get-tuple-element.30) | copy-start | bytes 196612
  68.5 11.1 %copy-start.4 = (f32[1024,1]{1,0:T(8,128)S(1)}, f32[1024,1]{1,0:T(8,128)}, u32[]{:S(2)}) copy-start(f32[1024,1]{1,0:T(8,128)} %get-tuple-element.26.level_ref) | copy-start | bytes 12292
  68.5 11.3 %copy-start.17 = (bf16[128,256]{1,0:T(8,128)(2,1)S(1)}, bf16[128,256]{1,0:T(8,128)(2,1)}, u32[]{:S(2)}) copy-start(bf16[128,256]{1,0:T(8,128)(2,1)} %get-tuple-element.31) | copy-start | bytes 196612
  68.5 13.1 %copy-start.16 = (bf16[128,256]{1,0:T(8,128)(2,1)S(1)}, bf16[128,256]{1,0:T(8,128)(2,1)}, u32[]{:S(2)}) copy-start(bf16[128,256]{1,0:T(8,128)(2,1)} %get-tuple-element.32) | copy-start | bytes 196612
  68.6 13.4 %copy-start.15 = (bf16[128,256]{1,0:T(8,128)(2,1)S(1)}, bf16[128,256]{1,0:T(8,128)(2,1)}, u32[]{:S(2)}) copy-start(bf16[128,256]{1,0:T(8,128)(2,1)} %get-tuple-element.33) | copy-start | bytes 196612
  68.6 15.3 %copy-start.14 = (bf16[128,256]{1,0:T(8,128)(2,1)S(1)}, bf16[128,256]{1,0:T(8,128)(2,1)}, u32[]{:S(2)}) copy-start(bf16[128,256]{1,0:T(8,128)(2,1)} %get-tuple-element.34) | copy-start | bytes 196612
  68.6 16.3 %copy-start.13 = (bf16[128,256]{1,0:T(8,128)(2,1)S(1)}, bf16[128,256]{1,0:T(8,128)(2,1)}, u32[]{:S(2)}) copy-start(bf16[128,256]{1,0:T(8,128)(2,1)} %get-tuple-element.35) | copy-start | bytes 196612
  68.6 17.9 %copy-start.12 = (f32[256]{0:T(256)S(1)}, f32[256]{0:T(256)}, u32[]{:S(2)}) copy-start(f32[256]{0:T(256)} %reduce_sum.9) | copy-start | bytes 3076
  68.6 41.4 %all-to-all-start.2 = ((bf16[16,272,256]{2,1,0:T(8,128)(2,1)}), bf16[16,272,256]{2,1,0:T(8,128)(2,1)S(1)}, u32[]{:S(2)}, u32[]{:S(2)}) async-start(bf16[16,272,256]{2,1,0:T(8,128)(2,1)} %get-tuple-element.36), calls=%async_computation.2 | async-start | bytes 4456448 | tf_op jit(solution)/shard_map/all_to_all | solution.py:431
  76.4 7.5 %collective-permute-start = (bf16[128,256]{1,0:T(8,128)(2,1)S(1)}, bf16[128,256]{1,0:T(8,128)(2,1)S(1)}, u32[]{:S(2)}, u32[]{:S(2)}) collective-permute-start(bf16[128,256]{1,0:T(8,128)(2,1)S(1)} %copy-done.19), channel_id=1, source_target_pairs={{0,1},{1,2},{2,3},{3,4},{4,5},{5,6},{6,7},{7,0},{8,9},{9,10},{10,1... | collective-permute-start | bytes 196616 | tf_op jit(solution)/shard_map/ppermute | solution.py:433
  78.4 6.5 %collective-permute-start.1 = (bf16[128,256]{1,0:T(8,128)(2,1)S(1)}, bf16[128,256]{1,0:T(8,128)(2,1)S(1)}, u32[]{:S(2)}, u32[]{:S(2)}) collective-permute-start(bf16[128,256]{1,0:T(8,128)(2,1)S(1)} %copy-done.18), channel_id=1, source_target_pairs={{0,2},{1,3},{2,4},{3,5},{4,6},{5,7},{6,0},{7,1},{8,10},{9,11},{10,... | collective-permute-start | bytes 196616 | tf_op jit(solution)/shard_map/ppermute | solution.py:433
  79.9 7.7 %collective-permute-start.2 = (bf16[128,256]{1,0:T(8,128)(2,1)S(1)}, bf16[128,256]{1,0:T(8,128)(2,1)S(1)}, u32[]{:S(2)}, u32[]{:S(2)}) collective-permute-start(bf16[128,256]{1,0:T(8,128)(2,1)S(1)} %copy-done.17), channel_id=1, source_target_pairs={{0,3},{1,4},{2,5},{3,6},{4,7},{5,0},{6,1},{7,2},{8,11},{9,12},{10,... | collective-permute-start | bytes 196616 | tf_op jit(solution)/shard_map/ppermute | solution.py:433
  81.6 6.0 %collective-permute-start.3 = (bf16[128,256]{1,0:T(8,128)(2,1)S(1)}, bf16[128,256]{1,0:T(8,128)(2,1)S(1)}, u32[]{:S(2)}, u32[]{:S(2)}) collective-permute-start(bf16[128,256]{1,0:T(8,128)(2,1)S(1)} %copy-done.16), channel_id=1, source_target_pairs={{0,4},{1,5},{2,6},{3,7},{4,0},{5,1},{6,2},{7,3},{8,12},{9,13},{10,... | collective-permute-start | bytes 196616 | tf_op jit(solution)/shard_map/ppermute | solution.py:433
  82.0 6.0 %collective-permute-start.4 = (bf16[128,256]{1,0:T(8,128)(2,1)S(1)}, bf16[128,256]{1,0:T(8,128)(2,1)S(1)}, u32[]{:S(2)}, u32[]{:S(2)}) collective-permute-start(bf16[128,256]{1,0:T(8,128)(2,1)S(1)} %copy-done.15), channel_id=1, source_target_pairs={{0,5},{1,6},{2,7},{3,0},{4,1},{5,2},{6,3},{7,4},{8,13},{9,14},{10,... | collective-permute-start | bytes 196616 | tf_op jit(solution)/shard_map/ppermute | solution.py:433
  83.9 5.7 %copy-start.5 = (bf16[128,256]{1,0:T(8,128)(2,1)}, bf16[128,256]{1,0:T(8,128)(2,1)S(1)}, u32[]{:S(2)}) copy-start(bf16[128,256]{1,0:T(8,128)(2,1)S(1)} %collective-permute-done.rest_1_) | copy-start | bytes 196612
  83.9 4.2 %collective-permute-start.5 = (bf16[128,256]{1,0:T(8,128)(2,1)S(1)}, bf16[128,256]{1,0:T(8,128)(2,1)S(1)}, u32[]{:S(2)}, u32[]{:S(2)}) collective-permute-start(bf16[128,256]{1,0:T(8,128)(2,1)S(1)} %copy-done.14), channel_id=1, source_target_pairs={{0,6},{1,7},{2,0},{3,1},{4,2},{5,3},{6,4},{7,5},{8,14},{9,15},{10,... | collective-permute-start | bytes 196616 | tf_op jit(solution)/shard_map/ppermute | solution.py:433
  84.8 4.8 %copy-start.6 = (bf16[128,256]{1,0:T(8,128)(2,1)}, bf16[128,256]{1,0:T(8,128)(2,1)S(1)}, u32[]{:S(2)}) copy-start(bf16[128,256]{1,0:T(8,128)(2,1)S(1)} %collective-permute-done.1.rest_2_) | copy-start | bytes 196612
  84.8 4.8 %collective-permute-start.6 = (bf16[128,256]{1,0:T(8,128)(2,1)S(1)}, bf16[128,256]{1,0:T(8,128)(2,1)S(1)}, u32[]{:S(2)}, u32[]{:S(2)}) collective-permute-start(bf16[128,256]{1,0:T(8,128)(2,1)S(1)} %copy-done.13), channel_id=1, source_target_pairs={{0,7},{1,0},{2,1},{3,2},{4,3},{5,4},{6,5},{7,6},{8,15},{9,8},{10,9... | collective-permute-start | bytes 196616 | tf_op jit(solution)/shard_map/ppermute | solution.py:433
  87.6 2.0 %copy-start.7 = (bf16[128,256]{1,0:T(8,128)(2,1)}, bf16[128,256]{1,0:T(8,128)(2,1)S(1)}, u32[]{:S(2)}) copy-start(bf16[128,256]{1,0:T(8,128)(2,1)S(1)} %collective-permute-done.2.rest_3_) | copy-start | bytes 196612
  87.6 2.0 %copy-start.8 = (bf16[128,256]{1,0:T(8,128)(2,1)}, bf16[128,256]{1,0:T(8,128)(2,1)S(1)}, u32[]{:S(2)}) copy-start(bf16[128,256]{1,0:T(8,128)(2,1)S(1)} %collective-permute-done.3.rest_4_) | copy-start | bytes 196612
  88.0 1.7 %copy-start.9 = (bf16[128,256]{1,0:T(8,128)(2,1)}, bf16[128,256]{1,0:T(8,128)(2,1)S(1)}, u32[]{:S(2)}) copy-start(bf16[128,256]{1,0:T(8,128)(2,1)S(1)} %collective-permute-done.4.rest_5_) | copy-start | bytes 196612
  88.1 1.6 %copy-start.10 = (bf16[128,256]{1,0:T(8,128)(2,1)}, bf16[128,256]{1,0:T(8,128)(2,1)S(1)}, u32[]{:S(2)}) copy-start(bf16[128,256]{1,0:T(8,128)(2,1)S(1)} %collective-permute-done.5.rest_6_) | copy-start | bytes 196612
  89.6 0.6 copy-start.11
  92.0 27.6 %copy-start = (bf16[512,256]{1,0:T(8,128)(2,1)S(1)}, bf16[512,256]{1,0:T(8,128)(2,1)}, u32[]{:S(2)}) copy-start(bf16[512,256]{1,0:T(8,128)(2,1)} %get-tuple-element.24.gain_ref) | copy-start | bytes 786436
  92.1 27.6 %copy-start.1 = (f32[16,1,384]{2,0,1:T(8,128)S(1)}, f32[16,1,384]{2,0,1:T(8,128)}, u32[]{:S(2)}) copy-start(f32[16,1,384]{2,0,1:T(8,128)} %copy.21) | copy-start | bytes 73732
  92.1 27.6 %copy-start.2 = (f32[512,1]{1,0:T(8,128)S(1)}, f32[512,1]{1,0:T(8,128)}, u32[]{:S(2)}) copy-start(f32[512,1]{1,0:T(8,128)} %get-tuple-element.37.level_ref) | copy-start | bytes 6148

commit v2 on v1

--- a/solution.py
+++ b/solution.py
@@ -15,6 +15,7 @@
 popularity_scale = 1.0
 
 VMEM_BYTES = 60 << 20
+SWEEP_BYTES = 54 << 20
 EXTRA = 16
 LANES = 128
 
@@ -44,43 +45,45 @@
     gain_ref[...], level_ref[...], mean = gains_of(
         shape_ref[...], rate_ref[...], popularity_prior / popularity_scale, strength
     )
-    devices, per_owner = touched_ref.shape
-    total = jnp.broadcast_to(jnp.sum(mean, axis=0, keepdims=True), (devices, mean.shape[1]))
+    per_owner, devices = touched_ref.shape
+    factors = mean.shape[1]
+    total = jnp.broadcast_to(jnp.sum(mean, axis=0).reshape(1, 1, factors), (devices, 1, factors))
 
     @pl.when(turn == 0)
     def _():
-        head_ref[:, pl.ds(0, per_owner)] = touched_ref[...].astype(jnp.float32)
-        head_ref[:, pl.ds(LANES, mean.shape[1])] = total
-
-    @pl.when(turn > 0)
-    def _():
-        head_ref[:, pl.ds(LANES, mean.shape[1])] += total
+        head_ref[...] = jnp.zeros_like(head_ref)
+        for place in range(per_owner):
+            blocks = touched_ref[pl.ds(place, 1), :].astype(jnp.float32).reshape(1, 1, devices)
+            head_ref[:, :, pl.ds(place * LANES, devices)] = jnp.broadcast_to(blocks, (devices, 1, devices))
+
+    head_ref[:, :, pl.ds(per_owner * LANES, factors)] += total
 
 
 def item_gains(touched, item_shape, item_rate):
     rows, factors = item_shape.shape
-    devices = touched.shape[0]
+    devices, per_owner = touched.shape
     step = rows // 2
     row_spec = pl.BlockSpec((step, factors), lambda r: (r, 0))
+    head_shape = (devices, 1, per_owner * LANES + factors)
     return pl.pallas_call(
         functools.partial(item_gain_kernel, popularity_prior + factors * item_prior),
         grid=(rows // step,),
-        in_specs=[pl.BlockSpec(touched.shape, lambda r: (0, 0)), row_spec, row_spec],
+        in_specs=[pl.BlockSpec((per_owner, devices), lambda r: (0, 0)), row_spec, row_spec],
         out_specs=[
             row_spec,
             pl.BlockSpec((step, 1), lambda r: (r, 0)),
-            pl.BlockSpec((devices, LANES + factors), lambda r: (0, 0)),
+            pl.BlockSpec(head_shape, lambda r: (0, 0, 0)),
         ],
         out_shape=[
             jax.ShapeDtypeStruct((rows, factors), jnp.bfloat16),
             jax.ShapeDtypeStruct((rows, 1), jnp.float32),
-            jax.ShapeDtypeStruct((devices, LANES + factors), jnp.float32),
+            jax.ShapeDtypeStruct(head_shape, jnp.float32),
         ],
         compiler_params=pltpu.CompilerParams(vmem_limit_bytes=VMEM_BYTES),
         cost_estimate=pl.CostEstimate(
             flops=40 * rows * factors, bytes_accessed=10 * rows * factors, transcendentals=4 * rows * factors
         ),
-    )(touched, item_shape, item_rate)
+    )(touched.T, item_shape, item_rate)
 
 
 def user_gain_kernel(strength, shape_ref, rate_ref, head_ref, gain_ref, level_ref, turned_ref, column_ref):
@@ -90,7 +93,9 @@
 
     @pl.when(pl.program_id(0) == 0)
     def _():
-        column_ref[...] = jnp.sum(head_ref[:, pl.ds(LANES, gain.shape[1])], axis=0, keepdims=True)
+        factors = gain.shape[1]
+        means = head_ref[:, :, pl.ds(head_ref.shape[2] - factors, factors)]
+        column_ref[...] = jnp.sum(means, axis=0).reshape(1, factors)
 
 
 def user_gains(user_shape, user_rate, heads):
@@ -100,7 +105,7 @@
     return pl.pallas_call(
         functools.partial(user_gain_kernel, activity_prior + factors * user_prior),
         grid=(rows // step,),
-        in_specs=[row_spec, row_spec, pl.BlockSpec(heads.shape, lambda r: (0, 0))],
+        in_specs=[row_spec, row_spec, pl.BlockSpec(heads.shape, lambda r: (0, 0, 0))],
         out_specs=[
             row_spec,
             pl.BlockSpec((step, 1), lambda r: (r, 0)),
@@ -120,32 +125,48 @@
     )(user_shape, user_rate, heads)
 
 
-def pick_kernel(per_owner, head_ref, gain_ref, picked_ref):
+def pick_kernel(per_owner, seat_ref, head_ref, gain_ref, picked_ref, sent):
+    edge = gain_ref.shape[1]
+    copies = []
     for device in range(head_ref.shape[0]):
         for place in range(per_owner):
-            picked_ref[device * per_owner + place] = gain_ref[head_ref[device, place].astype(jnp.int32)]
-
-
-def pick(heads, item_gain, edge, per_owner):
+            block = head_ref[device, 0, place * LANES + seat_ref[0]].astype(jnp.int32)
+            copies.append(
+                pltpu.make_async_copy(
+                    gain_ref.at[block],
+                    picked_ref.at[device, pl.ds(place * edge, edge)],
+                    sent.at[device * per_owner + place],
+                )
+            )
+            copies[-1].start()
+    for copy in copies:
+        copy.wait()
+
+
+def pick(seat, heads, item_gain, edge, per_owner):
     items, factors = item_gain.shape
     devices = heads.shape[0]
     return pl.pallas_call(
         functools.partial(pick_kernel, per_owner),
-        grid=(1,),
-        in_specs=[
-            pl.BlockSpec((devices, LANES), lambda step: (0, 0), memory_space=pltpu.SMEM),
-            pl.BlockSpec((items // edge, edge, factors), lambda step: (0, 0, 0)),
-        ],
-        out_specs=pl.BlockSpec((devices * per_owner, edge, factors), lambda step: (0, 0, 0)),
-        out_shape=jax.ShapeDtypeStruct((devices * per_owner, edge, factors), jnp.bfloat16),
+        grid_spec=pltpu.PrefetchScalarGridSpec(
+            num_scalar_prefetch=1,
+            grid=(1,),
+            in_specs=[
+                pl.BlockSpec(heads.shape, lambda step, seat_ref: (0, 0, 0), memory_space=pltpu.SMEM),
+                pl.BlockSpec((items // edge, edge, factors), lambda step, seat_ref: (0, 0, 0)),
+            ],
+            out_specs=pl.BlockSpec(memory_space=pl.ANY),
+            scratch_shapes=[pltpu.SemaphoreType.DMA((devices * per_owner,))],
+        ),
+        out_shape=jax.ShapeDtypeStruct((devices, per_owner * edge, factors), jnp.bfloat16),
         compiler_params=pltpu.CompilerParams(vmem_limit_bytes=VMEM_BYTES),
         cost_estimate=pl.CostEstimate(
             flops=0, bytes_accessed=2 * items * factors + 2 * devices * per_owner * edge * factors, transcendentals=0
         ),
-    )(heads, item_gain.reshape(items // edge, edge, factors))
-
-
-def dense_kernel(user_of, slot_of, live_ref, counts_ref, dense_ref, held_ref, arrived):
+    )(seat, heads, item_gain.reshape(items // edge, edge, factors))
+
+
+def dense_kernel(user_of, slot_of, live_ref, counts_ref, after_ref, dense_ref, held_ref, arrived):
     depth, group = held_ref.shape[:2]
     live = live_ref[0]
     groups = (live + group - 1) // group
@@ -188,7 +209,7 @@
     lax.fori_loop(0, groups, add_group, 0)
 
 
-def dense_counts(counts, tile_user, tile_slot, live_tiles, slot_count, user_blocks):
+def dense_counts(counts, tile_user, tile_slot, live_tiles, slot_count, user_blocks, after):
     tiles, edge, _ = counts.shape
     group = 8
     depth = min(8, tiles // group)
@@ -198,7 +219,7 @@
         grid_spec=pltpu.PrefetchScalarGridSpec(
             num_scalar_prefetch=3,
             grid=(1,),
-            in_specs=[pl.BlockSpec(memory_space=pl.ANY)],
+            in_specs=[pl.BlockSpec(memory_space=pl.ANY), pl.BlockSpec(after.shape, lambda step, *_: (0, 0))],
             out_specs=pl.BlockSpec(dense_shape, lambda step, *_: (0, 0, 0, 0)),
             scratch_shapes=[
                 pltpu.VMEM((depth, group, edge, edge), jnp.int32),
@@ -211,7 +232,7 @@
             flops=tiles * edge * edge, bytes_accessed=4 * counts.size + 2 * slot_count * user_blocks * edge * edge,
             transcendentals=0,
         ),
-    )(tile_user, tile_slot, live_tiles, counts)
+    )(tile_user, tile_slot, live_tiles, counts, after)
 
 
 def split_rows(value, rows):
@@ -226,43 +247,63 @@
 def sweep_kernel(
     prior_share, place_ref, dense_ref, items_ref, gain_ref, turned_ref, level_ref, total_ref, item_ref, *rest
 ):
-    user_refs, acc_ref, ratio_ref = rest[:-2], rest[-2], rest[-1]
+    user_refs, (acc_ref, early_ref, late_ref, held_ref) = rest[:-4], rest[-4:]
     turn = pl.program_id(0)
     per_step, touched_rows, factors = items_ref.shape
     slots, user_blocks, edge, _ = dense_ref.shape
     users = user_blocks * edge
+    pair = per_step // 2
     chunk = users // 2
+
+    def items_of(half):
+        return items_ref[pl.ds(half * pair, pair)].reshape(pair * touched_rows, factors)
+
+    def denominators(half):
+        turned_items = items_of(half).T
+        return [
+            jnp.dot(gain_ref[pl.ds(first, chunk), :], turned_items, preferred_element_type=jnp.float32)
+            for first in range(0, users, chunk)
+        ]
+
+    def put_ratios(half, parts, ratio_ref):
+        for index, denominator in enumerate(parts):
+            blocks = pl.ds(index * (chunk // edge), chunk // edge)
+            first = half * (slots // 2)
+            counted = jnp.concatenate(
+                [dense_ref[slot, blocks].reshape(chunk, edge) for slot in range(first, first + slots // 2)], axis=1
+            ).astype(jnp.float32)
+            inverse = pl.reciprocal(denominator, approx=True)
+            inverse *= 2.0 - denominator * inverse
+            ratio_ref[pl.ds(index * chunk, chunk), :] = (counted * inverse).astype(jnp.bfloat16)
+
+    def add_products(ratio_ref, items, owner):
+        for first in range(0, users, chunk):
+            rows = pl.ds(first, chunk)
+            acc_ref[rows, :] += jnp.dot(ratio_ref[rows, :], items, preferred_element_type=jnp.float32)
+        sums = jnp.dot(turned_ref[...], ratio_ref[...], preferred_element_type=jnp.float32)
+        sums = sums.astype(jnp.bfloat16).T
+        for index in range(pair):
+            item_ref[owner + index, pl.ds(0, touched_rows), :] = sums[
+                index * touched_rows : (index + 1) * touched_rows
+            ]
 
     @pl.when(turn == 0)
     def _():
         acc_ref[...] = jnp.zeros_like(acc_ref)
-
-    items = items_ref[...].reshape(per_step * touched_rows, factors)
-    turned_items = items.T
-    denominators = [
-        jnp.dot(gain_ref[pl.ds(first, chunk), :], turned_items, preferred_element_type=jnp.float32)
-        for first in range(0, users, chunk)
-    ]
-    for index, denominator in enumerate(denominators):
-        blocks = pl.ds(index * (chunk // edge), chunk // edge)
-        rows = pl.ds(index * chunk, chunk)
-        counted = jnp.concatenate(
-            [dense_ref[slot, blocks].reshape(chunk, edge) for slot in range(slots)], axis=1
-        ).astype(jnp.float32)
-        inverse = pl.reciprocal(denominator, approx=True)
-        inverse *= 2.0 - denominator * inverse
-        ratios = (counted * inverse).astype(jnp.bfloat16)
-        ratio_ref[rows, :] = ratios
-        acc_ref[rows, :] += jnp.dot(ratios, items, preferred_element_type=jnp.float32)
-    sums = jnp.dot(turned_ref[...], ratio_ref[...], preferred_element_type=jnp.float32)
-    sums = sums.astype(jnp.bfloat16).T
-    for owner in range(per_step):
-        item_ref[turn * per_step + owner, pl.ds(0, touched_rows), :] = sums[
-            owner * touched_rows : (owner + 1) * touched_rows
-        ]
+        late_ref[...] = jnp.zeros_like(late_ref)
+        held_ref[...] = jnp.zeros_like(held_ref)
+
+    early = denominators(0)
+    add_products(late_ref, held_ref[...], jnp.maximum(turn * per_step - pair, pair))
+    put_ratios(0, early, early_ref)
+    late = denominators(1)
+    add_products(early_ref, items_of(0), turn * per_step)
+    put_ratios(1, late, late_ref)
+    held_ref[...] = items_of(1)
 
     @pl.when(turn == pl.num_programs(0) - 1)
     def _():
+        add_products(late_ref, held_ref[...], turn * per_step + pair)
         own = users // len(user_refs)
         part = jnp.zeros((1, factors), jnp.float32)
         for ahead, user_ref in enumerate(user_refs):
@@ -282,7 +323,7 @@
     users = user_gain.shape[0]
     user_blocks, edge = dense.shape[1:3]
     per_owner = touched_rows // edge
-    per_step = 2
+    per_step = 4
     own = users // parts
     whole = lambda turn, place_ref: (0, 0)
     out = pl.pallas_call(
@@ -304,12 +345,14 @@
             + [pl.BlockSpec((own, factors), whole)] * parts,
             scratch_shapes=[
                 pltpu.VMEM((users, factors), jnp.float32),
-                pltpu.VMEM((users, per_step * touched_rows), jnp.bfloat16),
+                pltpu.VMEM((users, per_step // 2 * touched_rows), jnp.bfloat16),
+                pltpu.VMEM((users, per_step // 2 * touched_rows), jnp.bfloat16),
+                pltpu.VMEM((per_step // 2 * touched_rows, factors), jnp.bfloat16),
             ],
         ),
         out_shape=[jax.ShapeDtypeStruct((owners, touched_rows + EXTRA, factors), jnp.bfloat16)]
         + [jax.ShapeDtypeStruct((own, factors), jnp.bfloat16)] * parts,
-        compiler_params=pltpu.CompilerParams(vmem_limit_bytes=VMEM_BYTES),
+        compiler_params=pltpu.CompilerParams(vmem_limit_bytes=SWEEP_BYTES),
         cost_estimate=pl.CostEstimate(
             flops=6 * owners * touched_rows * users * factors,
             bytes_accessed=2 * dense.size + 4 * items.size + 4 * users * factors,
@@ -351,62 +394,85 @@
     extra = sums_ref[0].astype(jnp.float32)
     for sender in range(1, sums_ref.shape[0]):
         extra += sums_ref[sender].astype(jnp.float32)
-    part_ref[...] = jnp.sum(extra, axis=0, keepdims=True)
-
-
-def fold(sums):
+    part_ref[...] = jnp.broadcast_to(jnp.sum(extra, axis=0).reshape(1, 1, -1), part_ref.shape)
+
+
+def fold(sums, copies):
     senders, extended, factors = sums.shape
     return pl.pallas_call(
         fold_kernel,
         grid=(1,),
         in_specs=[pl.BlockSpec((senders, EXTRA, factors), lambda step: (0, extended // EXTRA - 1, 0))],
-        out_specs=pl.BlockSpec((1, factors), lambda step: (0, 0)),
-        out_shape=jax.ShapeDtypeStruct((1, factors), jnp.float32),
+        out_specs=pl.BlockSpec((copies, 1, factors), lambda step: (0, 0, 0)),
+        out_shape=jax.ShapeDtypeStruct((copies, 1, factors), jnp.float32),
         compiler_params=pltpu.CompilerParams(vmem_limit_bytes=VMEM_BYTES // 2),
         cost_estimate=pl.CostEstimate(flops=0, bytes_accessed=2 * senders * EXTRA * factors, transcendentals=0),
     )(sums)
 
 
-def item_kernel(per_owner, head_ref, sums_ref, gain_ref, level_ref, total_ref, shape_ref, elog_ref, acc_ref):
+def shape_kernel(per_owner, seat_ref, head_ref, sums_ref, gain_ref, shape_ref, digamma_ref, acc_ref):
     edge = acc_ref.shape[1]
-    user_total = jnp.sum(total_ref[...], axis=0, keepdims=True)
     acc_ref[...] = jnp.zeros_like(acc_ref)
     for sender in range(sums_ref.shape[0]):
         for place in range(per_owner):
-            block = head_ref[sender, place].astype(jnp.int32)
+            block = head_ref[sender, 0, place * LANES + seat_ref[0]].astype(jnp.int32)
             acc_ref[block] += sums_ref[sender, pl.ds(place * edge, edge), :].astype(jnp.float32)
     for block in range(acc_ref.shape[0]):
         rows = pl.ds(block * edge, edge)
         shape_new = item_prior + gain_ref[rows, :].astype(jnp.float32) * acc_ref[block]
         shape_ref[rows, :] = shape_new
-        rate_new = level_ref[rows, :] + user_total
-        elog_ref[rows, :] = digamma(shape_new) - jnp.log(rate_new)
-
-
-def item_update(heads, sums, item_gain, item_level, user_parts, edge):
+        digamma_ref[rows, :] = digamma(shape_new)
+
+
+def item_shapes(seat, heads, sums, item_gain, edge, per_owner):
     items, factors = item_gain.shape
-    senders, extended, _ = sums.shape
-    per_owner = (extended - EXTRA) // edge
-    whole = lambda step: (0, 0)
-    return pl.pallas_call(
-        functools.partial(item_kernel, per_owner),
-        grid=(1,),
-        in_specs=[
-            pl.BlockSpec((senders, LANES), whole, memory_space=pltpu.SMEM),
-            pl.BlockSpec(sums.shape, lambda step: (0, 0, 0)),
-            pl.BlockSpec((items, factors), whole),
-            pl.BlockSpec((items, 1), whole),
-            pl.BlockSpec(user_parts.shape, whole),
-        ],
-        out_specs=[pl.BlockSpec((items, factors), whole)] * 2,
-        scratch_shapes=[pltpu.VMEM((items // edge, edge, factors), jnp.float32)],
+    whole = lambda step, seat_ref: (0, 0)
+    return pl.pallas_call(
+        functools.partial(shape_kernel, per_owner),
+        grid_spec=pltpu.PrefetchScalarGridSpec(
+            num_scalar_prefetch=1,
+            grid=(1,),
+            in_specs=[
+                pl.BlockSpec(heads.shape, lambda step, seat_ref: (0, 0, 0), memory_space=pltpu.SMEM),
+                pl.BlockSpec(sums.shape, lambda step, seat_ref: (0, 0, 0)),
+                pl.BlockSpec((items, factors), whole),
+            ],
+            out_specs=[pl.BlockSpec((items, factors), whole)] * 2,
+            scratch_shapes=[pltpu.VMEM((items // edge, edge, factors), jnp.float32)],
+        ),
         out_shape=[jax.ShapeDtypeStruct((items, factors), jnp.float32)] * 2,
         compiler_params=pltpu.CompilerParams(vmem_limit_bytes=VMEM_BYTES // 2),
         cost_estimate=pl.CostEstimate(
             flops=40 * items * factors, bytes_accessed=2 * sums.size + 10 * items * factors,
-            transcendentals=4 * items * factors,
-        ),
-    )(heads, sums, item_gain, item_level, user_parts)
+            transcendentals=3 * items * factors,
+        ),
+    )(seat, heads, sums, item_gain)
+
+
+def elog_kernel(digamma_ref, level_ref, parts_ref, elog_ref):
+    user_total = jnp.sum(parts_ref[...], axis=0)
+    elog_ref[...] = digamma_ref[...] - jnp.log(level_ref[...] + user_total)
+
+
+def item_elogs(digammas, item_level, user_parts):
+    items, factors = digammas.shape
+    step = items // 2
+    row_spec = pl.BlockSpec((step, factors), lambda r: (r, 0))
+    return pl.pallas_call(
+        elog_kernel,
+        grid=(items // step,),
+        in_specs=[
+            row_spec,
+            pl.BlockSpec((step, 1), lambda r: (r, 0)),
+            pl.BlockSpec(user_parts.shape, lambda r: (0, 0, 0)),
+        ],
+        out_specs=row_spec,
+        out_shape=jax.ShapeDtypeStruct((items, factors), jnp.float32),
+        compiler_params=pltpu.CompilerParams(vmem_limit_bytes=VMEM_BYTES // 2),
+        cost_estimate=pl.CostEstimate(
+            flops=2 * items * factors, bytes_accessed=8 * items * factors, transcendentals=items * factors
+        ),
+    )(digammas, item_level, user_parts)
 
 
 def shards(
@@ -418,17 +484,19 @@
     owners, per_owner = touched.shape
     columns = lax.axis_size("item")
     place = lax.axis_index("item").astype(jnp.int32).reshape(1)
+    seat = lax.axis_index("user").astype(jnp.int32).reshape(1)
     item_gain, item_level, heads = item_gains(touched, item_shape, item_rate)
-    heads = lax.all_to_all(heads, "user", 0, 0, tiled=True)
-    item_rows = pick(heads, item_gain, edge, per_owner).reshape(owners, per_owner * edge, factors)
-    item_rows = lax.all_to_all(item_rows, "user", 0, 0, tiled=True)
+    heads = lax.all_to_all(heads, "user", 0, 0)
+    item_rows = lax.all_to_all(pick(seat, heads, item_gain, edge, per_owner), "user", 0, 0)
     user_gain, user_level, turned_gain, column_total = user_gains(user_shape, user_rate, heads)
     item_total = jnp.sum(lax.all_gather(column_total, "item", axis=0, tiled=True), axis=0, keepdims=True)
-    dense = dense_counts(counts, tile_user, tile_slot, live_tiles, owners * per_owner, user_blocks)
+    dense = dense_counts(
+        counts, tile_user, tile_slot, live_tiles, owners * per_owner, user_blocks, item_total
+    )
     item_sums, user_sums = sweep(
         place, dense, item_rows, user_gain, turned_gain, user_level, item_total, columns
     )
-    item_sums = lax.all_to_all(item_sums, "user", 0, 0, tiled=True)
+    item_sums = lax.all_to_all(item_sums, "user", 0, 0)
     user_sums = [user_sums[0]] + [
         lax.ppermute(user_sums[k], "item", [(j, (j + k) % columns) for j in range(columns)])
         for k in range(1, columns)
@@ -436,8 +504,9 @@
     user_sum = lax.all_gather(own_users(place, user_sums, user_gain), "item", axis=0, tiled=True)
     user_shape_new = user_prior + user_sum.astype(jnp.float32)
     user_rate_new = user_level + item_total
-    user_parts = lax.all_gather(fold(item_sums), "item", axis=0, tiled=True)
-    item_shape_new, item_elog = item_update(heads, item_sums, item_gain, item_level, user_parts, edge)
+    user_parts = lax.all_to_all(fold(item_sums, columns), "item", 0, 0)
+    item_shape_new, digammas = item_shapes(seat, heads, item_sums, item_gain, edge, per_owner)
+    item_elog = item_elogs(digammas, item_level, user_parts)
     return (user_shape_new, user_rate_new, item_shape_new, item_elog)
 
 

time: 124 us -> 120 us (0.968); the launches traced: 122 us -> 121 us
  blocking collectives: 50.4 us -> 26.5 us
  starting transfers between devices: 21.3 us -> 34.6 us
  waiting for transfers between devices: 7.67 us -> 16.4 us
  Pallas kernels: 33.7 us -> 36.6 us
  local copies, waits for them, and re-layouts: 4.73 us -> 2.67 us
    all_to_all x2 -> x4, starting transfers between devices: 11.5 us -> 26.7 us  [the longest x1 9.54 us: shards(): item_sums = lax.all_to_all(item_sums, 'user', 0, 0)]
    all_to_all x1 -> x0, blocking collectives: 14.7 us -> none  [shards(): heads = lax.all_to_all(heads, 'user', 0, 0, tiled=True)]
    all_gather x1 -> x0, blocking collectives: 9.63 us -> none  [shards(): user_parts = lax.all_gather(fold(item_sums), 'item', axis=0, tiled=True)]
    all_to_all x2 -> x4, waiting for transfers between devices: 5.65 us -> 13.6 us  [the longest x1 6.47 us: shards(): heads = lax.all_to_all(heads, 'user', 0, 0)]
    ppermute x7, starting transfers between devices: 9.83 us -> 7.9 us  [shards(): lax.ppermute(user_sums[k], 'item', [(j, (j + k) % columns) for j in range...]
    pallas_call x2 -> x3, Pallas kernels: 5.15 us -> 6.56 us  [the longest x1 2.86 us: pick(): pl.pallas_call(functools.partial(pick_kernel, per_owner), grid_spec=pltpu...]
    unnamed x43 -> x42, local copies, waits for them, and re-layouts: 3.96 us -> 2.67 us
    pallas_call x1, Pallas kernels: 6.31 us -> 7.58 us  [dense_counts(): pl.pallas_call(dense_kernel, grid_spec=pltpu.PrefetchScalarGridSpec(num_s...]
  transfers between devices with their start and end apart: 9 -> 11, of which waited for: 5 -> 8; matrix products, arithmetic and copies ran while one was open for 2% -> 3% of each run, Pallas kernels for 10% -> 14%
where the time goes in v2:
time: 120 us; the launch traced here: 121 us
  Pallas kernels  36.6 us (30%)
  starting transfers between devices  34.6 us (29%)
  blocking collectives  26.5 us (22%)
  waiting for transfers between devices  16.4 us (14%)
  other arithmetic  3.04 us (3%)
  local copies, waits for them, and re-layouts  2.67 us (2%)
  between operations  1.5 us (1%)
    all_gather x1, blocking collectives, shards(): lax.all_gather(own_users(place, user_sums, user_gain), 'item', axis=0, ti...  13.5 us
    pallas_call x1, Pallas kernels, sweep(): pl.pallas_call(functools.partial(sweep_kernel, user_prior / parts), grid_...  13.2 us
    all_gather x1, blocking collectives, shards(): lax.all_gather(column_total, 'item', axis=0, tiled=True)  12.9 us
    all_to_all x1, starting transfers between devices, shards(): item_sums = lax.all_to_all(item_sums, 'user', 0, 0)  9.54 us
    all_to_all x1, starting transfers between devices, shards(): heads = lax.all_to_all(heads, 'user', 0, 0)  8.43 us
    ppermute x7, starting transfers between devices, shards(): lax.ppermute(user_sums[k], 'item', [(j, (j + k) % columns) for j in range...  7.9 us
    pallas_call x1, Pallas kernels, dense_counts(): pl.pallas_call(dense_kernel, grid_spec=pltpu.PrefetchScalarGridSpec(num_s...  7.58 us
    all_to_all x1, waiting for transfers between devices, shards(): heads = lax.all_to_all(heads, 'user', 0, 0)  6.47 us
  transfers between devices with their start and end apart: 11, of which 8 were waited for; matrix products, arithmetic and copies ran while one was open for 3% of the time, Pallas kernels for 14%

profile of v2, /device:TPU:1, one launch (start us, length us, event | category | flops | bytes accessed | tf_op | source)
XLA Modules:
  0.0 121.2 jit_solution(9719446908761515189)
XLA Ops:
  0.6 2.5 %shard_map.120 = (bf16[512,256]{1,0:T(8,128)(2,1)}, f32[512,1]{1,0:T(8,128)}, f32[16,1,512]{2,1,0:T(1,128)}) custom-call(s32[2,16]{1,0:T(2,128)} %bitcast.9, f32[512,256]{1,0:T(8,128)} %shape_ref.2, f32[512,256]{1,0:T(8,128)} %rate_ref.2), custom_call_target="tpu_custom_call" | custom-call | flops 5242880 | bytes 1310720 | tf_op jit(solution)/shard_map/pallas_call | solution.py:68
  3.2 8.4 %all-to-all-start = ((f32[16,1,512]{2,1,0:T(1,128)}), f32[16,1,512]{2,1,0:T(1,128)S(1)}, u32[]{:S(2)}, u32[]{:S(2)}) async-start(f32[16,1,512]{2,1,0:T(1,128)} %get-tuple-element.22), calls=%async_computation | async-start | bytes 65536 | tf_op jit(solution)/shard_map/all_to_all | solution.py:489
  11.6 6.5 %all-to-all-done.head_ref = f32[16,1,512]{2,1,0:T(1,128)S(1)} async-done(((f32[16,1,512]{2,1,0:T(1,128)}), f32[16,1,512]{2,1,0:T(1,128)S(1)}, u32[]{:S(2)}, u32[]{:S(2)}) %all-to-all-start) | async-done | bytes 32800 | tf_op jit(solution)/shard_map/all_to_all | solution.py:489
  18.1 0.6 copy-done.1
  18.7 2.9 %shard_map.123 = bf16[16,256,256]{2,1,0:T(8,128)(2,1)} custom-call(s32[1]{0:T(128)} %bitcast.4.seat_ref, f32[16,1,512]{2,1,0:T(1,128)} %copy-done.1, bf16[4,128,256]{2,1,0:T(8,128)(2,1)} %bitcast.6), custom_call_target="tpu_custom_call" | custom-call | bytes 2359296 | tf_op jit(solution)/shard_map/pallas_call | solution.py:149
  21.6 3.7 %all-to-all-start.1 = ((bf16[16,256,256]{2,1,0:T(8,128)(2,1)}), bf16[16,256,256]{2,1,0:T(8,128)(2,1)S(1)}, u32[]{:S(2)}, u32[]{:S(2)}) async-start(bf16[16,256,256]{2,1,0:T(8,128)(2,1)} %shard_map.123), calls=%async_computation.1 | async-start | bytes 4194304 | tf_op jit(solution)/shard_map/all_to_all | solution.py:490
  26.0 4.3 %shard_map.121 = (bf16[1024,256]{1,0:T(8,128)(2,1)}, f32[1024,1]{1,0:T(8,128)}, bf16[256,1024]{1,0:T(8,128)(2,1)}, f32[1,256]{1,0:T(1,128)}) custom-call(f32[1024,256]{1,0:T(8,128)} %shape_ref.3, f32[1024,256]{1,0:T(8,128)} %rate_ref.3, f32[16,1,512]{2,1,0:T(1,128)} %copy-done.1), custom_call_target="tpu_custom_call" | custom-call | flops 10485760 | bytes 3145728 | tf_op jit(solution)/shard_map/pallas_call | solution.py:105
  30.3 12.9 %all-gather = f32[8,1,256]{2,1,0:T(1,128)S(1)} all-gather(f32[1,1,256]{2,1,0:T(1,128)} %bitcast.10), channel_id=1, replica_groups=mesh['user'=16,'item'=8] {'item'}, dimensions={0}, use_global_device_ids=true | all-gather | bytes 9216 | tf_op jit(solution)/shard_map/all_gather | solution.py:492
  43.2 0.6 reduce_sum.9
  43.8 7.6 %shard_map.122.dense_ref = bf16[32,8,128,128]{3,2,1,0:T(8,128)(2,1)} custom-call(s32[256]{0:T(256)} %user_of.1, s32[256]{0:T(256)} %slot_of.1, s32[1]{0:T(128)S(6)} %copy.13.live_ref, s32[256,128,128]{2,1,0:T(8,128)} %counts_ref.1, f32[1,256]{1,0:T(1,128)} %bitcast.7), custom_call_target="tpu_custom_call" | custom-call | flops 4194304 | bytes 25165824 | tf_op jit(solution)/shard_map/pallas_call | solution.py:217
  51.4 0.8 all-to-all-done.1.items_ref
  52.2 1.4 %copy-done.4 = bf16[16,256,256]{2,1,0:T(8,128)(2,1)} copy-done((bf16[16,256,256]{2,1,0:T(8,128)(2,1)}, bf16[16,256,256]{2,1,0:T(8,128)(2,1)S(1)}, u32[]{:S(2)}) %copy-start.4) | copy-done | bytes 2097176
  53.6 13.2 %shard_map.124 = (bf16[16,272,256]{2,1,0:T(8,128)(2,1)}, bf16[128,256]{1,0:T(8,128)(2,1)}, bf16[128,256]{1,0:T(8,128)(2,1)}, bf16[128,256]{1,0:T(8,128)(2,1)}, b...) custom-call(s32[1]{0:T(128)} %bitcast.place_ref, ...), custom_call_target="tpu_custom_call" | custom-call | flops 6442450944 | bytes 13631488 | tf_op jit(solution)/shard_map/pallas_call | solution.py:329
  66.8 0.0 copy-start.20
  66.8 0.0 copy-start.19
  66.8 0.0 copy-start.5
  66.9 9.5 %all-to-all-start.2 = ((bf16[16,272,256]{2,1,0:T(8,128)(2,1)}), bf16[16,272,256]{2,1,0:T(8,128)(2,1)S(1)}, u32[]{:S(2)}, u32[]{:S(2)}) async-start(bf16[16,272,256]{2,1,0:T(8,128)(2,1)} %get-tuple-element.36), calls=%async_computation.2 | async-start | bytes 4456448 | tf_op jit(solution)/shard_map/all_to_all | solution.py:499
  76.4 0.1 collective-permute-start
  76.5 0.0 copy-done.19
  76.5 1.3 %collective-permute-start.1 = (bf16[128,256]{1,0:T(8,128)(2,1)S(1)}, bf16[128,256]{1,0:T(8,128)(2,1)S(1)}, u32[]{:S(2)}, u32[]{:S(2)}) collective-permute-start(bf16[128,256]{1,0:T(8,128)(2,1)S(1)} %copy-done.19), channel_id=1, source_target_pairs={{0,2},{1,3},{2,4},{3,5},{4,6},{5,7},{6,0},{7,1},{8,10},{9,11},{10,... | collective-permute-start | bytes 196616 | tf_op jit(solution)/shard_map/ppermute | solution.py:501
  77.8 0.2 reduce.1
  78.0 1.8 %collective-permute-start.2 = (bf16[128,256]{1,0:T(8,128)(2,1)S(1)}, bf16[128,256]{1,0:T(8,128)(2,1)S(1)}, u32[]{:S(2)}, u32[]{:S(2)}) collective-permute-start(bf16[128,256]{1,0:T(8,128)(2,1)S(1)} %copy-done.18), channel_id=1, source_target_pairs={{0,3},{1,4},{2,5},{3,6},{4,7},{5,0},{6,1},{7,2},{8,11},{9,12},{10,... | collective-permute-start | bytes 196616 | tf_op jit(solution)/shard_map/ppermute | solution.py:501
  79.8 0.0 copy-done.17
  79.8 1.5 %collective-permute-start.3 = (bf16[128,256]{1,0:T(8,128)(2,1)S(1)}, bf16[128,256]{1,0:T(8,128)(2,1)S(1)}, u32[]{:S(2)}, u32[]{:S(2)}) collective-permute-start(bf16[128,256]{1,0:T(8,128)(2,1)S(1)} %copy-done.17), channel_id=1, source_target_pairs={{0,4},{1,5},{2,6},{3,7},{4,0},{5,1},{6,2},{7,3},{8,12},{9,13},{10,... | collective-permute-start | bytes 196616 | tf_op jit(solution)/shard_map/ppermute | solution.py:501
  81.3 0.0 copy-done.16
  81.3 2.5 %collective-permute-start.4 = (bf16[128,256]{1,0:T(8,128)(2,1)S(1)}, bf16[128,256]{1,0:T(8,128)(2,1)S(1)}, u32[]{:S(2)}, u32[]{:S(2)}) collective-permute-start(bf16[128,256]{1,0:T(8,128)(2,1)S(1)} %copy-done.16), channel_id=1, source_target_pairs={{0,5},{1,6},{2,7},{3,0},{4,1},{5,2},{6,3},{7,4},{8,13},{9,14},{10,... | collective-permute-start | bytes 196616 | tf_op jit(solution)/shard_map/ppermute | solution.py:501
  83.9 0.0 collective-permute-done.rest_1_
  83.9 0.1 collective-permute-start.5
  84.0 0.0 collective-permute-done.1.rest_2_
  84.0 0.6 collective-permute-start.6
  84.6 1.2 broadcast_add_fusion
  85.8 0.1 collective-permute-done.2.rest_3_
  85.9 0.0 collective-permute-done.3.rest_4_
  85.9 0.9 collective-permute-done.4.rest_5_
  86.8 1.2 collective-permute-done.5.rest_6_
  88.0 0.6 collective-permute-done.6.rest_7_
  88.6 0.0 copy-done.7
  88.6 0.0 copy-done.11
  88.6 0.6 copy-done.12
  89.2 1.8 %shard_map.125 = bf16[128,256]{1,0:T(8,128)(2,1)} custom-call(s32[1]{0:T(128)} %bitcast.place_ref, bf16[1024,256]{1,0:T(8,128)(2,1)} %get-tuple-element.23.gain_ref, bf16[128,256]{1,0:T(8,128)(2,1)} %get-tuple-element.28.rest_0_, bf16[128,256]{1,0:T(8,128)(2,1)} %copy-done.6, bf16[128,256]{1,0:T(8,128)(2,1)} %copy-done.7, bf16[128,256]{1,0:T(8,128)(2,1)} %copy-done.8, ...), custom_call_target="tpu_custom_call" | custom-call | flops 524288 | bytes 524288 | tf_op jit(solution)/shard_map/pallas_call | solution.py:376
  91.0 13.5 %all_gather.7 = bf16[1024,256]{1,0:T(8,128)(2,1)S(1)} all-gather(bf16[128,256]{1,0:T(8,128)(2,1)} %shard_map.125), channel_id=1, replica_groups=mesh['user'=16,'item'=8] {'item'}, dimensions={0}, use_global_device_ids=true | all-gather | bytes 589824 | tf_op jit(solution)/shard_map/all_gather | solution.py:504
  104.5 5.5 %all-to-all-done.2.sums_ref = bf16[16,272,256]{2,1,0:T(8,128)(2,1)S(1)} async-done(((bf16[16,272,256]{2,1,0:T(8,128)(2,1)}), bf16[16,272,256]{2,1,0:T(8,128)(2,1)S(1)}, u32[]{:S(2)}, u32[]{:S(2)}) %all-to-all-start.2) | async-done | bytes 2228256 | tf_op jit(solution)/shard_map/all_to_all | solution.py:499
  110.1 0.6 shard_map.127
  110.7 5.0 %all-to-all-start.3 = ((f32[8,1,256]{2,1,0:T(1,128)}), f32[8,1,256]{2,1,0:T(1,128)S(1)}, u32[]{:S(2)}, u32[]{:S(2)}) async-start(f32[8,1,256]{2,1,0:T(1,128)} %shard_map.127), calls=%async_computation.3 | async-start | bytes 16384 | tf_op jit(solution)/shard_map/all_to_all | solution.py:507
  115.7 1.1 convert_add_fusion
  116.7 2.8 %shard_map.126 = (f32[512,256]{1,0:T(8,128)}, f32[512,256]{1,0:T(8,128)S(1)}) custom-call(s32[1]{0:T(128)} %bitcast.4.seat_ref, f32[16,1,512]{2,1,0:T(1,128)S(1)} %copy-done.2, bf16[16,272,256]{2,1,0:T(8,128)(2,1)S(1)} %all-to-all-done.2.sums_ref, bf16[512,256]{1,0:T(8,128)(2,1)S(1)} %copy-done), custom_call_target="tpu_custom_call" | custom-call | flops 5242880 | bytes 3538944 | tf_op jit(solution)/shard_map/pallas_call | solution.py:430
  119.5 0.8 all-to-all-done.3.parts_ref
  120.3 0.9 shard_map.128
  (31 shorter events, 0.1 us)
Async XLA Ops:
  3.2 14.9 %all-to-all-start = ((f32[16,1,512]{2,1,0:T(1,128)}), f32[16,1,512]{2,1,0:T(1,128)S(1)}, u32[]{:S(2)}, u32[]{:S(2)}) async-start(f32[16,1,512]{2,1,0:T(1,128)} %get-tuple-element.22), calls=%async_computation | async-start | bytes 65536 | tf_op jit(solution)/shard_map/all_to_all | solution.py:489
  18.1 0.6 copy-start.1
  21.6 30.6 %all-to-all-start.1 = ((bf16[16,256,256]{2,1,0:T(8,128)(2,1)}), bf16[16,256,256]{2,1,0:T(8,128)(2,1)S(1)}, u32[]{:S(2)}, u32[]{:S(2)}) async-start(bf16[16,256,256]{2,1,0:T(8,128)(2,1)} %shard_map.123), calls=%async_computation.1 | async-start | bytes 4194304 | tf_op jit(solution)/shard_map/all_to_all | solution.py:490
  52.2 1.4 %copy-start.4 = (bf16[16,256,256]{2,1,0:T(8,128)(2,1)}, bf16[16,256,256]{2,1,0:T(8,128)(2,1)S(1)}, u32[]{:S(2)}) copy-start(bf16[16,256,256]{2,1,0:T(8,128)(2,1)S(1)} %all-to-all-done.1.items_ref) | copy-start | bytes 6291460
  66.8 9.6 %copy-start.20 = (bf16[128,256]{1,0:T(8,128)(2,1)S(1)}, bf16[128,256]{1,0:T(8,128)(2,1)}, u32[]{:S(2)}) copy-start(bf16[128,256]{1,0:T(8,128)(2,1)} %get-tuple-element.29) | copy-start | bytes 196612
  66.8 9.7 %copy-start.19 = (bf16[128,256]{1,0:T(8,128)(2,1)S(1)}, bf16[128,256]{1,0:T(8,128)(2,1)}, u32[]{:S(2)}) copy-start(bf16[128,256]{1,0:T(8,128)(2,1)} %get-tuple-element.30) | copy-start | bytes 196612
  66.8 11.0 %copy-start.5 = (f32[1024,1]{1,0:T(8,128)S(1)}, f32[1024,1]{1,0:T(8,128)}, u32[]{:S(2)}) copy-start(f32[1024,1]{1,0:T(8,128)} %get-tuple-element.27.level_ref) | copy-start | bytes 12292
  66.8 11.2 %copy-start.18 = (bf16[128,256]{1,0:T(8,128)(2,1)S(1)}, bf16[128,256]{1,0:T(8,128)(2,1)}, u32[]{:S(2)}) copy-start(bf16[128,256]{1,0:T(8,128)(2,1)} %get-tuple-element.31) | copy-start | bytes 196612
  66.8 13.0 %copy-start.17 = (bf16[128,256]{1,0:T(8,128)(2,1)S(1)}, bf16[128,256]{1,0:T(8,128)(2,1)}, u32[]{:S(2)}) copy-start(bf16[128,256]{1,0:T(8,128)(2,1)} %get-tuple-element.32) | copy-start | bytes 196612
  66.8 14.5 %copy-start.16 = (bf16[128,256]{1,0:T(8,128)(2,1)S(1)}, bf16[128,256]{1,0:T(8,128)(2,1)}, u32[]{:S(2)}) copy-start(bf16[128,256]{1,0:T(8,128)(2,1)} %get-tuple-element.33) | copy-start | bytes 196612
  66.8 17.0 %copy-start.15 = (bf16[128,256]{1,0:T(8,128)(2,1)S(1)}, bf16[128,256]{1,0:T(8,128)(2,1)}, u32[]{:S(2)}) copy-start(bf16[128,256]{1,0:T(8,128)(2,1)} %get-tuple-element.34) | copy-start | bytes 196612
  66.9 17.1 %copy-start.14 = (bf16[128,256]{1,0:T(8,128)(2,1)S(1)}, bf16[128,256]{1,0:T(8,128)(2,1)}, u32[]{:S(2)}) copy-start(bf16[128,256]{1,0:T(8,128)(2,1)} %get-tuple-element.35) | copy-start | bytes 196612
  66.9 17.8 %copy-start.13 = (f32[256]{0:T(256)S(1)}, f32[256]{0:T(256)}, u32[]{:S(2)}) copy-start(f32[256]{0:T(256)} %reduce_sum.9) | copy-start | bytes 3076
  66.9 43.2 %all-to-all-start.2 = ((bf16[16,272,256]{2,1,0:T(8,128)(2,1)}), bf16[16,272,256]{2,1,0:T(8,128)(2,1)S(1)}, u32[]{:S(2)}, u32[]{:S(2)}) async-start(bf16[16,272,256]{2,1,0:T(8,128)(2,1)} %get-tuple-element.36), calls=%async_computation.2 | async-start | bytes 4456448 | tf_op jit(solution)/shard_map/all_to_all | solution.py:499
  76.4 7.4 %collective-permute-start = (bf16[128,256]{1,0:T(8,128)(2,1)S(1)}, bf16[128,256]{1,0:T(8,128)(2,1)S(1)}, u32[]{:S(2)}, u32[]{:S(2)}) collective-permute-start(bf16[128,256]{1,0:T(8,128)(2,1)S(1)} %copy-done.20), channel_id=1, source_target_pairs={{0,1},{1,2},{2,3},{3,4},{4,5},{5,6},{6,7},{7,0},{8,9},{9,10},{10,1... | collective-permute-start | bytes 196616 | tf_op jit(solution)/shard_map/ppermute | solution.py:501
  76.5 7.4 %collective-permute-start.1 = (bf16[128,256]{1,0:T(8,128)(2,1)S(1)}, bf16[128,256]{1,0:T(8,128)(2,1)S(1)}, u32[]{:S(2)}, u32[]{:S(2)}) collective-permute-start(bf16[128,256]{1,0:T(8,128)(2,1)S(1)} %copy-done.19), channel_id=1, source_target_pairs={{0,2},{1,3},{2,4},{3,5},{4,6},{5,7},{6,0},{7,1},{8,10},{9,11},{10,... | collective-permute-start | bytes 196616 | tf_op jit(solution)/shard_map/ppermute | solution.py:501
  78.0 7.9 %collective-permute-start.2 = (bf16[128,256]{1,0:T(8,128)(2,1)S(1)}, bf16[128,256]{1,0:T(8,128)(2,1)S(1)}, u32[]{:S(2)}, u32[]{:S(2)}) collective-permute-start(bf16[128,256]{1,0:T(8,128)(2,1)S(1)} %copy-done.18), channel_id=1, source_target_pairs={{0,3},{1,4},{2,5},{3,6},{4,7},{5,0},{6,1},{7,2},{8,11},{9,12},{10,... | collective-permute-start | bytes 196616 | tf_op jit(solution)/shard_map/ppermute | solution.py:501
  79.8 6.1 %collective-permute-start.3 = (bf16[128,256]{1,0:T(8,128)(2,1)S(1)}, bf16[128,256]{1,0:T(8,128)(2,1)S(1)}, u32[]{:S(2)}, u32[]{:S(2)}) collective-permute-start(bf16[128,256]{1,0:T(8,128)(2,1)S(1)} %copy-done.17), channel_id=1, source_target_pairs={{0,4},{1,5},{2,6},{3,7},{4,0},{5,1},{6,2},{7,3},{8,12},{9,13},{10,... | collective-permute-start | bytes 196616 | tf_op jit(solution)/shard_map/ppermute | solution.py:501
  81.3 5.5 %collective-permute-start.4 = (bf16[128,256]{1,0:T(8,128)(2,1)S(1)}, bf16[128,256]{1,0:T(8,128)(2,1)S(1)}, u32[]{:S(2)}, u32[]{:S(2)}) collective-permute-start(bf16[128,256]{1,0:T(8,128)(2,1)S(1)} %copy-done.16), channel_id=1, source_target_pairs={{0,5},{1,6},{2,7},{3,0},{4,1},{5,2},{6,3},{7,4},{8,13},{9,14},{10,... | collective-permute-start | bytes 196616 | tf_op jit(solution)/shard_map/ppermute | solution.py:501
  83.9 4.7 %copy-start.6 = (bf16[128,256]{1,0:T(8,128)(2,1)}, bf16[128,256]{1,0:T(8,128)(2,1)S(1)}, u32[]{:S(2)}) copy-start(bf16[128,256]{1,0:T(8,128)(2,1)S(1)} %collective-permute-done.rest_1_) | copy-start | bytes 196612
  83.9 4.2 %collective-permute-start.5 = (bf16[128,256]{1,0:T(8,128)(2,1)S(1)}, bf16[128,256]{1,0:T(8,128)(2,1)S(1)}, u32[]{:S(2)}, u32[]{:S(2)}) collective-permute-start(bf16[128,256]{1,0:T(8,128)(2,1)S(1)} %copy-done.15), channel_id=1, source_target_pairs={{0,6},{1,7},{2,0},{3,1},{4,2},{5,3},{6,4},{7,5},{8,14},{9,15},{10,... | collective-permute-start | bytes 196616 | tf_op jit(solution)/shard_map/ppermute | solution.py:501
  84.0 4.6 %copy-start.7 = (bf16[128,256]{1,0:T(8,128)(2,1)}, bf16[128,256]{1,0:T(8,128)(2,1)S(1)}, u32[]{:S(2)}) copy-start(bf16[128,256]{1,0:T(8,128)(2,1)S(1)} %collective-permute-done.1.rest_2_) | copy-start | bytes 196612
  84.0 4.6 %collective-permute-start.6 = (bf16[128,256]{1,0:T(8,128)(2,1)S(1)}, bf16[128,256]{1,0:T(8,128)(2,1)S(1)}, u32[]{:S(2)}, u32[]{:S(2)}) collective-permute-start(bf16[128,256]{1,0:T(8,128)(2,1)S(1)} %copy-done.14), channel_id=1, source_target_pairs={{0,7},{1,0},{2,1},{3,2},{4,3},{5,4},{6,5},{7,6},{8,15},{9,8},{10,9... | collective-permute-start | bytes 196616 | tf_op jit(solution)/shard_map/ppermute | solution.py:501
  85.9 2.7 %copy-start.8 = (bf16[128,256]{1,0:T(8,128)(2,1)}, bf16[128,256]{1,0:T(8,128)(2,1)S(1)}, u32[]{:S(2)}) copy-start(bf16[128,256]{1,0:T(8,128)(2,1)S(1)} %collective-permute-done.2.rest_3_) | copy-start | bytes 196612
  85.9 2.7 %copy-start.9 = (bf16[128,256]{1,0:T(8,128)(2,1)}, bf16[128,256]{1,0:T(8,128)(2,1)S(1)}, u32[]{:S(2)}) copy-start(bf16[128,256]{1,0:T(8,128)(2,1)S(1)} %collective-permute-done.3.rest_4_) | copy-start | bytes 196612
  86.8 1.8 %copy-start.10 = (bf16[128,256]{1,0:T(8,128)(2,1)}, bf16[128,256]{1,0:T(8,128)(2,1)S(1)}, u32[]{:S(2)}) copy-start(bf16[128,256]{1,0:T(8,128)(2,1)S(1)} %collective-permute-done.4.rest_5_) | copy-start | bytes 196612
  88.0 0.6 copy-start.11
  88.6 0.6 copy-start.12
  91.0 25.7 %copy-start = (bf16[512,256]{1,0:T(8,128)(2,1)S(1)}, bf16[512,256]{1,0:T(8,128)(2,1)}, u32[]{:S(2)}) copy-start(bf16[512,256]{1,0:T(8,128)(2,1)} %get-tuple-element.25.gain_ref) | copy-start | bytes 786436
  91.0 25.7 %copy-start.2 = (f32[16,1,512]{2,1,0:T(1,128)S(1)}, f32[16,1,512]{2,1,0:T(1,128)}, u32[]{:S(2)}) copy-start(f32[16,1,512]{2,1,0:T(1,128)} %copy-done.1) | copy-start | bytes 98308
  110.7 9.6 %copy-start.3 = (f32[512,1]{1,0:T(8,128)S(1)}, f32[512,1]{1,0:T(8,128)}, u32[]{:S(2)}) copy-start(f32[512,1]{1,0:T(8,128)} %get-tuple-element.39.level_ref) | copy-start | bytes 6148
  110.7 9.6 %all-to-all-start.3 = ((f32[8,1,256]{2,1,0:T(1,128)}), f32[8,1,256]{2,1,0:T(1,128)S(1)}, u32[]{:S(2)}, u32[]{:S(2)}) async-start(f32[8,1,256]{2,1,0:T(1,128)} %shard_map.127), calls=%async_computation.3 | async-start | bytes 16384 | tf_op jit(solution)/shard_map/all_to_all | solution.py:507

commit v3 on v2

--- a/solution.py
+++ b/solution.py
@@ -14,10 +14,17 @@
 popularity_prior = 0.3
 popularity_scale = 1.0
 
-VMEM_BYTES = 60 << 20
-SWEEP_BYTES = 54 << 20
+VMEM_BYTES = 16 << 20
+SWEEP_BYTES = 28 << 20
 EXTRA = 16
 LANES = 128
+IN_VMEM = pl.BlockSpec(memory_space=pltpu.VMEM)
+IN_SMEM = pl.BlockSpec(memory_space=pltpu.SMEM)
+IN_PLACE = pl.BlockSpec(memory_space=pl.ANY)
+
+
+def in_hbm(array):
+    return pltpu.with_memory_space_constraint(array, pltpu.HBM)
 
 
 def digamma_rest(x):
@@ -83,7 +90,7 @@
         cost_estimate=pl.CostEstimate(
             flops=40 * rows * factors, bytes_accessed=10 * rows * factors, transcendentals=4 * rows * factors
         ),
-    )(touched.T, item_shape, item_rate)
+    )(touched.T, in_hbm(item_shape), in_hbm(item_rate))
 
 
 def user_gain_kernel(strength, shape_ref, rate_ref, head_ref, gain_ref, level_ref, turned_ref, column_ref):
@@ -122,7 +129,7 @@
         cost_estimate=pl.CostEstimate(
             flops=40 * rows * factors, bytes_accessed=12 * rows * factors, transcendentals=4 * rows * factors
         ),
-    )(user_shape, user_rate, heads)
+    )(in_hbm(user_shape), in_hbm(user_rate), heads)
 
 
 def pick_kernel(per_owner, seat_ref, head_ref, gain_ref, picked_ref, sent):
@@ -148,17 +155,10 @@
     devices = heads.shape[0]
     return pl.pallas_call(
         functools.partial(pick_kernel, per_owner),
-        grid_spec=pltpu.PrefetchScalarGridSpec(
-            num_scalar_prefetch=1,
-            grid=(1,),
-            in_specs=[
-                pl.BlockSpec(heads.shape, lambda step, seat_ref: (0, 0, 0), memory_space=pltpu.SMEM),
-                pl.BlockSpec((items // edge, edge, factors), lambda step, seat_ref: (0, 0, 0)),
-            ],
-            out_specs=pl.BlockSpec(memory_space=pl.ANY),
-            scratch_shapes=[pltpu.SemaphoreType.DMA((devices * per_owner,))],
-        ),
-        out_shape=jax.ShapeDtypeStruct((devices, per_owner * edge, factors), jnp.bfloat16),
+        in_specs=[IN_SMEM, IN_SMEM, IN_VMEM],
+        out_specs=IN_PLACE,
+        scratch_shapes=[pltpu.SemaphoreType.DMA((devices * per_owner,))],
+        out_shape=pltpu.HBM((devices, per_owner * edge, factors), jnp.bfloat16),
         compiler_params=pltpu.CompilerParams(vmem_limit_bytes=VMEM_BYTES),
         cost_estimate=pl.CostEstimate(
             flops=0, bytes_accessed=2 * items * factors + 2 * devices * per_owner * edge * factors, transcendentals=0
@@ -213,26 +213,21 @@
     tiles, edge, _ = counts.shape
     group = 8
     depth = min(8, tiles // group)
-    dense_shape = (slot_count, user_blocks, edge, edge)
     return pl.pallas_call(
         dense_kernel,
-        grid_spec=pltpu.PrefetchScalarGridSpec(
-            num_scalar_prefetch=3,
-            grid=(1,),
-            in_specs=[pl.BlockSpec(memory_space=pl.ANY), pl.BlockSpec(after.shape, lambda step, *_: (0, 0))],
-            out_specs=pl.BlockSpec(dense_shape, lambda step, *_: (0, 0, 0, 0)),
-            scratch_shapes=[
-                pltpu.VMEM((depth, group, edge, edge), jnp.int32),
-                pltpu.SemaphoreType.DMA((depth,)),
-            ],
-        ),
-        out_shape=jax.ShapeDtypeStruct(dense_shape, jnp.bfloat16),
+        in_specs=[IN_SMEM, IN_SMEM, IN_SMEM, IN_PLACE, IN_VMEM],
+        out_specs=IN_VMEM,
+        scratch_shapes=[
+            pltpu.VMEM((depth, group, edge, edge), jnp.int32),
+            pltpu.SemaphoreType.DMA((depth,)),
+        ],
+        out_shape=jax.ShapeDtypeStruct((slot_count, user_blocks, edge, edge), jnp.bfloat16),
         compiler_params=pltpu.CompilerParams(vmem_limit_bytes=VMEM_BYTES),
         cost_estimate=pl.CostEstimate(
             flops=tiles * edge * edge, bytes_accessed=4 * counts.size + 2 * slot_count * user_blocks * edge * edge,
             transcendentals=0,
         ),
-    )(tile_user, tile_slot, live_tiles, counts, after)
+    )(tile_user, tile_slot, live_tiles, in_hbm(counts), after)
 
 
 def split_rows(value, rows):
@@ -247,110 +242,107 @@
 def sweep_kernel(
     prior_share, place_ref, dense_ref, items_ref, gain_ref, turned_ref, level_ref, total_ref, item_ref, *rest
 ):
-    user_refs, (acc_ref, early_ref, late_ref, held_ref) = rest[:-4], rest[-4:]
-    turn = pl.program_id(0)
-    per_step, touched_rows, factors = items_ref.shape
+    user_refs, (acc_ref, early_ref, late_ref, sums_ref, extra_ref, sent) = rest[:-6], rest[-6:]
+    owners, touched_rows, factors = items_ref.shape
     slots, user_blocks, edge, _ = dense_ref.shape
     users = user_blocks * edge
-    pair = per_step // 2
+    per_owner = slots // owners
+    pair = 2
     chunk = users // 2
-
-    def items_of(half):
-        return items_ref[pl.ds(half * pair, pair)].reshape(pair * touched_rows, factors)
-
-    def denominators(half):
-        turned_items = items_of(half).T
+    last = owners // pair - 1
+
+    def items_of(index):
+        return items_ref[pl.ds(index * pair, pair)].reshape(pair * touched_rows, factors)
+
+    def denominators(index):
+        turned_items = items_of(index).T
         return [
             jnp.dot(gain_ref[pl.ds(first, chunk), :], turned_items, preferred_element_type=jnp.float32)
             for first in range(0, users, chunk)
         ]
 
-    def put_ratios(half, parts, ratio_ref):
-        for index, denominator in enumerate(parts):
-            blocks = pl.ds(index * (chunk // edge), chunk // edge)
-            first = half * (slots // 2)
+    def put_ratios(index, parts, ratio_ref):
+        for place, denominator in enumerate(parts):
+            blocks = pl.ds(place * (chunk // edge), chunk // edge)
             counted = jnp.concatenate(
-                [dense_ref[slot, blocks].reshape(chunk, edge) for slot in range(first, first + slots // 2)], axis=1
+                [
+                    dense_ref[index * pair * per_owner + slot, blocks].reshape(chunk, edge)
+                    for slot in range(pair * per_owner)
+                ],
+                axis=1,
             ).astype(jnp.float32)
             inverse = pl.reciprocal(denominator, approx=True)
             inverse *= 2.0 - denominator * inverse
-            ratio_ref[pl.ds(index * chunk, chunk), :] = (counted * inverse).astype(jnp.bfloat16)
-
-    def add_products(ratio_ref, items, owner):
+            ratio_ref[pl.ds(place * chunk, chunk), :] = (counted * inverse).astype(jnp.bfloat16)
+
+    def copy_of(index):
+        return pltpu.make_async_copy(
+            sums_ref.at[pl.ds(index * pair, pair)],
+            item_ref.at[pl.ds(index * pair, pair), pl.ds(0, touched_rows)],
+            sent.at[index],
+        )
+
+    def add_products(index, ratio_ref):
+        items = items_of(index)
         for first in range(0, users, chunk):
             rows = pl.ds(first, chunk)
             acc_ref[rows, :] += jnp.dot(ratio_ref[rows, :], items, preferred_element_type=jnp.float32)
         sums = jnp.dot(turned_ref[...], ratio_ref[...], preferred_element_type=jnp.float32)
-        sums = sums.astype(jnp.bfloat16).T
-        for index in range(pair):
-            item_ref[owner + index, pl.ds(0, touched_rows), :] = sums[
-                index * touched_rows : (index + 1) * touched_rows
-            ]
-
-    @pl.when(turn == 0)
-    def _():
-        acc_ref[...] = jnp.zeros_like(acc_ref)
-        late_ref[...] = jnp.zeros_like(late_ref)
-        held_ref[...] = jnp.zeros_like(held_ref)
-
-    early = denominators(0)
-    add_products(late_ref, held_ref[...], jnp.maximum(turn * per_step - pair, pair))
-    put_ratios(0, early, early_ref)
-    late = denominators(1)
-    add_products(early_ref, items_of(0), turn * per_step)
-    put_ratios(1, late, late_ref)
-    held_ref[...] = items_of(1)
-
-    @pl.when(turn == pl.num_programs(0) - 1)
-    def _():
-        add_products(late_ref, held_ref[...], turn * per_step + pair)
-        own = users // len(user_refs)
-        part = jnp.zeros((1, factors), jnp.float32)
-        for ahead, user_ref in enumerate(user_refs):
-            target = (place_ref[0] + ahead) % len(user_refs)
-            rows = pl.ds(pl.multiple_of(target * own, own), own)
-            user_sums = acc_ref[rows, :]
-            user_ref[...] = user_sums.astype(jnp.bfloat16)
-            shape_share = prior_share + gain_ref[rows, :].astype(jnp.float32) * user_sums
-            part += jnp.sum(shape_share / (level_ref[rows, :] + total_ref[...]), axis=0, keepdims=True)
-        extra = split_rows(part, EXTRA)
-        for owner in range(item_ref.shape[0]):
-            item_ref[owner, pl.ds(touched_rows, EXTRA), :] = extra
+        sums_ref[pl.ds(index * pair, pair)] = sums.astype(jnp.bfloat16).T.reshape(pair, touched_rows, factors)
+        copy_of(index).start()
+
+    acc_ref[...] = jnp.zeros_like(acc_ref)
+    put_ratios(0, denominators(0), early_ref)
+
+    def turn(step, carry):
+        first, second, third = 2 * step, 2 * step + 1, jnp.minimum(2 * step + 2, last)
+        late = denominators(second)
+        add_products(first, early_ref)
+        put_ratios(second, late, late_ref)
+        early = denominators(third)
+        add_products(second, late_ref)
+        put_ratios(third, early, early_ref)
+        return carry
+
+    lax.fori_loop(0, (last + 1) // 2, turn, 0)
+
+    own = users // len(user_refs)
+    part = jnp.zeros((1, factors), jnp.float32)
+    for ahead, user_ref in enumerate(user_refs):
+        target = (place_ref[0] + ahead) % len(user_refs)
+        rows = pl.ds(pl.multiple_of(target * own, own), own)
+        user_sums = acc_ref[rows, :]
+        user_ref[...] = user_sums.astype(jnp.bfloat16)
+        shape_share = prior_share + gain_ref[rows, :].astype(jnp.float32) * user_sums
+        part += jnp.sum(shape_share / (level_ref[rows, :] + total_ref[...]), axis=0, keepdims=True)
+    extra_ref[...] = jnp.broadcast_to(split_rows(part, EXTRA)[None], extra_ref.shape)
+    extra_copy = pltpu.make_async_copy(
+        extra_ref, item_ref.at[:, pl.ds(touched_rows, EXTRA)], sent.at[last + 1]
+    )
+    extra_copy.start()
+    for index in range(last + 1):
+        copy_of(index).wait()
+    extra_copy.wait()
 
 
 def sweep(place, dense, items, user_gain, turned_gain, user_level, item_total, parts):
     owners, touched_rows, factors = items.shape
     users = user_gain.shape[0]
-    user_blocks, edge = dense.shape[1:3]
-    per_owner = touched_rows // edge
-    per_step = 4
     own = users // parts
-    whole = lambda turn, place_ref: (0, 0)
+    pair = 2
     out = pl.pallas_call(
         functools.partial(sweep_kernel, user_prior / parts),
-        grid_spec=pltpu.PrefetchScalarGridSpec(
-            num_scalar_prefetch=1,
-            grid=(owners // per_step,),
-            in_specs=[
-                pl.BlockSpec(
-                    (per_step * per_owner, user_blocks, edge, edge), lambda turn, place_ref: (turn, 0, 0, 0)
-                ),
-                pl.BlockSpec((per_step, touched_rows, factors), lambda turn, place_ref: (turn, 0, 0)),
-                pl.BlockSpec((users, factors), whole),
-                pl.BlockSpec((factors, users), whole),
-                pl.BlockSpec((users, 1), whole),
-                pl.BlockSpec((1, factors), whole),
-            ],
-            out_specs=[pl.BlockSpec((owners, touched_rows + EXTRA, factors), lambda turn, place_ref: (0, 0, 0))]
-            + [pl.BlockSpec((own, factors), whole)] * parts,
-            scratch_shapes=[
-                pltpu.VMEM((users, factors), jnp.float32),
-                pltpu.VMEM((users, per_step // 2 * touched_rows), jnp.bfloat16),
-                pltpu.VMEM((users, per_step // 2 * touched_rows), jnp.bfloat16),
-                pltpu.VMEM((per_step // 2 * touched_rows, factors), jnp.bfloat16),
-            ],
-        ),
-        out_shape=[jax.ShapeDtypeStruct((owners, touched_rows + EXTRA, factors), jnp.bfloat16)]
+        in_specs=[IN_SMEM] + [IN_VMEM] * 6,
+        out_specs=[IN_PLACE] + [IN_VMEM] * parts,
+        scratch_shapes=[
+            pltpu.VMEM((users, factors), jnp.float32),
+            pltpu.VMEM((users, pair * touched_rows), jnp.bfloat16),
+            pltpu.VMEM((users, pair * touched_rows), jnp.bfloat16),
+            pltpu.VMEM((owners, touched_rows, factors), jnp.bfloat16),
+            pltpu.VMEM((owners, EXTRA, factors), jnp.bfloat16),
+            pltpu.SemaphoreType.DMA((owners // pair + 1,)),
+        ],
+        out_shape=[pltpu.HBM((owners, touched_rows + EXTRA, factors), jnp.bfloat16)]
         + [jax.ShapeDtypeStruct((own, factors), jnp.bfloat16)] * parts,
         compiler_params=pltpu.CompilerParams(vmem_limit_bytes=SWEEP_BYTES),
         cost_estimate=pl.CostEstimate(
@@ -364,24 +356,20 @@
 
 def own_kernel(place_ref, gain_ref, *rest):
     sums_refs, sum_ref = rest[:-1], rest[-1]
-    sums = jnp.zeros(gain_ref.shape, jnp.float32)
+    own = sum_ref.shape[0]
+    sums = jnp.zeros(sum_ref.shape, jnp.float32)
     for sums_ref in sums_refs:
         sums += sums_ref[...].astype(jnp.float32)
-    sum_ref[...] = (gain_ref[...].astype(jnp.float32) * sums).astype(jnp.bfloat16)
+    gain = gain_ref[pl.ds(pl.multiple_of(place_ref[0] * own, own), own), :]
+    sum_ref[...] = (gain.astype(jnp.float32) * sums).astype(jnp.bfloat16)
 
 
 def own_users(place, sums, user_gain):
     own, factors = sums[0].shape
-    first = lambda step, place_ref: (0, 0)
     return pl.pallas_call(
         own_kernel,
-        grid_spec=pltpu.PrefetchScalarGridSpec(
-            num_scalar_prefetch=1,
-            grid=(1,),
-            in_specs=[pl.BlockSpec((own, factors), lambda step, place_ref: (place_ref[0], 0))]
-            + [pl.BlockSpec((own, factors), first)] * len(sums),
-            out_specs=pl.BlockSpec((own, factors), first),
-        ),
+        in_specs=[IN_SMEM] + [IN_VMEM] * (len(sums) + 1),
+        out_specs=IN_VMEM,
         out_shape=jax.ShapeDtypeStruct((own, factors), jnp.bfloat16),
         compiler_params=pltpu.CompilerParams(vmem_limit_bytes=VMEM_BYTES),
         cost_estimate=pl.CostEstimate(
@@ -390,24 +378,24 @@
     )(place, user_gain, *sums)
 
 
-def fold_kernel(sums_ref, part_ref):
+def fold_kernel(sums_ref, after_ref, part_ref):
     extra = sums_ref[0].astype(jnp.float32)
     for sender in range(1, sums_ref.shape[0]):
         extra += sums_ref[sender].astype(jnp.float32)
     part_ref[...] = jnp.broadcast_to(jnp.sum(extra, axis=0).reshape(1, 1, -1), part_ref.shape)
 
 
-def fold(sums, copies):
+def fold(sums, copies, after):
     senders, extended, factors = sums.shape
     return pl.pallas_call(
         fold_kernel,
         grid=(1,),
-        in_specs=[pl.BlockSpec((senders, EXTRA, factors), lambda step: (0, extended // EXTRA - 1, 0))],
+        in_specs=[pl.BlockSpec((senders, EXTRA, factors), lambda step: (0, extended // EXTRA - 1, 0)), IN_PLACE],
         out_specs=pl.BlockSpec((copies, 1, factors), lambda step: (0, 0, 0)),
         out_shape=jax.ShapeDtypeStruct((copies, 1, factors), jnp.float32),
-        compiler_params=pltpu.CompilerParams(vmem_limit_bytes=VMEM_BYTES // 2),
+        compiler_params=pltpu.CompilerParams(vmem_limit_bytes=VMEM_BYTES),
         cost_estimate=pl.CostEstimate(flops=0, bytes_accessed=2 * senders * EXTRA * factors, transcendentals=0),
-    )(sums)
+    )(sums, after)
 
 
 def shape_kernel(per_owner, seat_ref, head_ref, sums_ref, gain_ref, shape_ref, digamma_ref, acc_ref):
@@ -441,7 +429,7 @@
             scratch_shapes=[pltpu.VMEM((items // edge, edge, factors), jnp.float32)],
         ),
         out_shape=[jax.ShapeDtypeStruct((items, factors), jnp.float32)] * 2,
-        compiler_params=pltpu.CompilerParams(vmem_limit_bytes=VMEM_BYTES // 2),
+        compiler_params=pltpu.CompilerParams(vmem_limit_bytes=VMEM_BYTES),
         cost_estimate=pl.CostEstimate(
             flops=40 * items * factors, bytes_accessed=2 * sums.size + 10 * items * factors,
             transcendentals=3 * items * factors,
@@ -468,7 +456,7 @@
         ],
         out_specs=row_spec,
         out_shape=jax.ShapeDtypeStruct((items, factors), jnp.float32),
-        compiler_params=pltpu.CompilerParams(vmem_limit_bytes=VMEM_BYTES // 2),
+        compiler_params=pltpu.CompilerParams(vmem_limit_bytes=VMEM_BYTES),
         cost_estimate=pl.CostEstimate(
             flops=2 * items * factors, bytes_accessed=8 * items * factors, transcendentals=items * factors
         ),
@@ -504,7 +492,7 @@
     user_sum = lax.all_gather(own_users(place, user_sums, user_gain), "item", axis=0, tiled=True)
     user_shape_new = user_prior + user_sum.astype(jnp.float32)
     user_rate_new = user_level + item_total
-    user_parts = lax.all_to_all(fold(item_sums, columns), "item", 0, 0)
+    user_parts = lax.all_to_all(fold(item_sums, columns, user_shape_new), "item", 0, 0)
     item_shape_new, digammas = item_shapes(seat, heads, item_sums, item_gain, edge, per_owner)
     item_elog = item_elogs(digammas, item_level, user_parts)
     return (user_shape_new, user_rate_new, item_shape_new, item_elog)

time: 120 us -> 128 us (1.067); the launches traced: 121 us -> 126 us
  local copies, waits for them, and re-layouts: 2.67 us -> 22.2 us
  Pallas kernels: 36.6 us -> 27.5 us
  waiting for transfers between devices: 16.4 us -> 13.8 us
  other arithmetic: 3.04 us -> 1.5 us
    unnamed x42 -> x54, local copies, waits for them, and re-layouts: 2.67 us -> 22.2 us
    pallas_call x4, Pallas kernels: 25.4 us -> 17.5 us  [the longest x1 10.2 us: sweep(): pl.pallas_call(functools.partial(sweep_kernel, user_prior / parts), in_sp...]
    all_to_all x1, waiting for transfers between devices: 5.51 us -> 2.08 us  [shards(): item_sums = lax.all_to_all(item_sums, 'user', 0, 0)]
    all_to_all x1, starting transfers between devices: 9.54 us -> 7.27 us  [shards(): item_sums = lax.all_to_all(item_sums, 'user', 0, 0)]
    ppermute x7, starting transfers between devices: 7.9 us -> 9.91 us  [shards(): lax.ppermute(user_sums[k], 'item', [(j, (j + k) % columns) for j in range...]
    all_to_all x1, waiting for transfers between devices: 0.8 us -> 2.66 us  [shards(): lax.all_to_all(pick(seat, heads, item_gain, edge, per_owner), 'user', 0, 0)]
  transfers between devices with their start and end apart: 11 -> 11, of which waited for: 8 -> 5; matrix products, arithmetic and copies ran while one was open for 3% -> 1% of each run, Pallas kernels for 14% -> 8%
where the time goes in v3:
time: 128 us; the launch traced here: 126 us
  starting transfers between devices  34.4 us (27%)
  Pallas kernels  27.5 us (21%)
  blocking collectives  25.5 us (20%)
  local copies, waits for them, and re-layouts  22.2 us (17%)
  waiting for transfers between devices  13.8 us (11%)
  other arithmetic  1.5 us (1%)
  between operations  1.47 us (1%)
    unnamed x54, local copies, waits for them, and re-layouts  22.2 us
    all_gather x1, blocking collectives, shards(): lax.all_gather(own_users(place, user_sums, user_gain), 'item', axis=0, ti...  12.8 us
    all_gather x1, blocking collectives, shards(): lax.all_gather(column_total, 'item', axis=0, tiled=True)  12.7 us
    pallas_call x1, Pallas kernels, sweep(): pl.pallas_call(functools.partial(sweep_kernel, user_prior / parts), in_sp...  10.2 us
    ppermute x7, starting transfers between devices, shards(): lax.ppermute(user_sums[k], 'item', [(j, (j + k) % columns) for j in range...  9.91 us
    all_to_all x1, starting transfers between devices, shards(): heads = lax.all_to_all(heads, 'user', 0, 0)  8.43 us
    all_to_all x1, starting transfers between devices, shards(): item_sums = lax.all_to_all(item_sums, 'user', 0, 0)  7.27 us
    all_to_all x1, waiting for transfers between devices, shards(): heads = lax.all_to_all(heads, 'user', 0, 0)  6.47 us
  transfers between devices with their start and end apart: 11, of which 5 were waited for; matrix products, arithmetic and copies ran while one was open for 1% of the time, Pallas kernels for 8%

profile of v3, /device:TPU:1, one launch (start us, length us, event | category | flops | bytes accessed | tf_op | source)
XLA Modules:
  0.0 126.4 jit_solution(5941829654433131442)
XLA Ops:
  0.6 0.7 copy-done.15
  1.3 2.4 %shard_map.120 = (bf16[512,256]{1,0:T(8,128)(2,1)S(1)}, f32[512,1]{1,0:T(8,128)S(1)}, f32[16,1,512]{2,1,0:T(1,128)}) custom-call(s32[2,16]{1,0:T(2,128)S(1)} %bitcast.9, f32[512,256]{1,0:T(8,128)} %shape_ref.2, f32[512,256]{1,0:T(8,128)} %rate_ref.2), custom_call_target="tpu_custom_call" | custom-call | flops 5242880 | bytes 1310720 | tf_op jit(solution)/shard_map/pallas_call | solution.py:75
  3.7 0.7 copy-done.7
  4.4 8.4 %all-to-all-start = ((f32[16,1,512]{2,1,0:T(1,128)}), f32[16,1,512]{2,1,0:T(1,128)S(1)}, u32[]{:S(2)}, u32[]{:S(2)}) async-start(f32[16,1,512]{2,1,0:T(1,128)} %get-tuple-element.22), calls=%async_computation | async-start | bytes 65536 | tf_op jit(solution)/shard_map/all_to_all | solution.py:477
  12.8 6.5 %all-to-all-done.head_ref = f32[16,1,512]{2,1,0:T(1,128)S(1)} async-done(((f32[16,1,512]{2,1,0:T(1,128)}), f32[16,1,512]{2,1,0:T(1,128)S(1)}, u32[]{:S(2)}, u32[]{:S(2)}) %all-to-all-start) | async-done | bytes 32800 | tf_op jit(solution)/shard_map/all_to_all | solution.py:477
  19.3 2.7 %shard_map.123 = bf16[16,256,256]{2,1,0:T(8,128)(2,1)} custom-call(s32[1]{0:T(128)} %bitcast.4.seat_ref, f32[16,1,512]{2,1,0:T(1,128)S(1)} %all-to-all-done.head_ref, bf16[4,128,256]{2,1,0:T(8,128)(2,1)S(1)} %bitcast.6), custom_call_target="tpu_custom_call" | custom-call | bytes 2359296 | tf_op jit(solution)/shard_map/pallas_call | solution.py:156
  22.1 3.7 %all-to-all-start.1 = ((bf16[16,256,256]{2,1,0:T(8,128)(2,1)}), bf16[16,256,256]{2,1,0:T(8,128)(2,1)S(1)}, u32[]{:S(2)}, u32[]{:S(2)}) async-start(bf16[16,256,256]{2,1,0:T(8,128)(2,1)} %shard_map.123), calls=%async_computation.1 | async-start | bytes 4194304 | tf_op jit(solution)/shard_map/all_to_all | solution.py:478
  26.5 3.3 %shard_map.121 = (bf16[1024,256]{1,0:T(8,128)(2,1)S(1)}, f32[1024,1]{1,0:T(8,128)S(1)}, bf16[256,1024]{1,0:T(8,128)(2,1)S(1)}, f32[1,256]{1,0:T(1,128)S(1)}) custom-call(f32[1024,256]{1,0:T(8,128)} %shape_ref.3, f32[1024,256]{1,0:T(8,128)} %rate_ref.3, f32[16,1,512]{2,1,0:T(1,128)S(1)} %all-to-all-done.head_ref), custom_call_target="tpu_custom_call" | custom-call | flops 10485760 | bytes 3145728 | tf_op jit(solution)/shard_map/pallas_call | solution.py:112
  29.8 0.8 copy-done.18
  30.6 12.7 %all-gather = f32[8,1,256]{2,1,0:T(1,128)S(1)} all-gather(f32[1,1,256]{2,1,0:T(1,128)S(1)} %bitcast.10), channel_id=1, replica_groups=mesh['user'=16,'item'=8] {'item'}, dimensions={0}, use_global_device_ids=true | all-gather | bytes 9216 | tf_op jit(solution)/shard_map/all_gather | solution.py:480
  43.3 3.5 %shard_map.122.dense_ref = bf16[32,8,128,128]{3,2,1,0:T(8,128)(2,1)S(1)} custom-call(s32[256]{0:T(256)S(1)} %copy-done.16, s32[256]{0:T(256)S(1)} %copy-done.17, s32[1]{0:T(128)S(6)} %copy.13.live_ref, s32[256,128,128]{2,1,0:T(8,128)} %counts_ref.1, f32[1,256]{1,0:T(1,128)S(1)} %bitcast.7), custom_call_target="tpu_custom_call" | custom-call | flops 4194304 | bytes 25165824 | tf_op jit(solution)/shard_map/pallas_call | solution.py:216
  46.8 3.3 %copy-done = bf16[32,8,128,128]{3,2,1,0:T(8,128)(2,1)} copy-done((bf16[32,8,128,128]{3,2,1,0:T(8,128)(2,1)}, bf16[32,8,128,128]{3,2,1,0:T(8,128)(2,1)S(1)}, u32[]{:S(2)}) %copy-start) | copy-done | bytes 8388632
  50.1 2.7 %all-to-all-done.1.items_ref = bf16[16,256,256]{2,1,0:T(8,128)(2,1)S(1)} async-done(((bf16[16,256,256]{2,1,0:T(8,128)(2,1)}), bf16[16,256,256]{2,1,0:T(8,128)(2,1)S(1)}, u32[]{:S(2)}, u32[]{:S(2)}) %all-to-all-start.1) | async-done | bytes 2097184 | tf_op jit(solution)/shard_map/all_to_all | solution.py:478
  52.7 3.4 %copy-done.1 = bf16[32,8,128,128]{3,2,1,0:T(8,128)(2,1)S(1)} copy-done((bf16[32,8,128,128]{3,2,1,0:T(8,128)(2,1)S(1)}, bf16[32,8,128,128]{3,2,1,0:T(8,128)(2,1)}, u32[]{:S(2)}) %copy-start.1) | copy-done | bytes 8388632
  56.1 1.0 copy-done.19
  57.2 10.2 %shard_map.124 = (bf16[16,272,256]{2,1,0:T(8,128)(2,1)}, bf16[128,256]{1,0:T(8,128)(2,1)S(1)}, bf16[128,256]{1,0:T(8,128)(2,1)S(1)}, bf16[128,256]{1,0:T(8,128)(...) custom-call(s32[1]{0:T(128)} %bitcast.place_ref, ...), custom_call_target="tpu_custom_call" | custom-call | flops 6442450944 | bytes 13631488 | tf_op jit(solution)/shard_map/pallas_call | solution.py:333
  67.4 0.6 copy-done.9
  68.6 0.6 copy-done.22
  69.2 0.6 copy-done.23
  69.9 0.6 copy-done.24
  70.5 0.6 copy-done.25
  71.1 0.6 copy-done.26
  71.8 0.6 copy-done.20
  72.4 7.3 %all-to-all-start.2 = ((bf16[16,272,256]{2,1,0:T(8,128)(2,1)}), bf16[16,272,256]{2,1,0:T(8,128)(2,1)S(1)}, u32[]{:S(2)}, u32[]{:S(2)}) async-start(bf16[16,272,256]{2,1,0:T(8,128)(2,1)} %get-tuple-element.36), calls=%async_computation.2 | async-start | bytes 4456448 | tf_op jit(solution)/shard_map/all_to_all | solution.py:487
  79.7 2.2 %collective-permute-start = (bf16[128,256]{1,0:T(8,128)(2,1)}, bf16[128,256]{1,0:T(8,128)(2,1)S(1)}, u32[]{:S(2)}, u32[]{:S(2)}) collective-permute-start(bf16[128,256]{1,0:T(8,128)(2,1)} %copy-done.26), channel_id=1, source_target_pairs={{0,1},{1,2},{2,3},{3,4},{4,5},{5,6},{6,7},{7,0},{8,9},{9,10},{10,1... | collective-permute-start | bytes 196616 | tf_op jit(solution)/shard_map/ppermute | solution.py:489
  81.9 1.3 %collective-permute-start.1 = (bf16[128,256]{1,0:T(8,128)(2,1)}, bf16[128,256]{1,0:T(8,128)(2,1)S(1)}, u32[]{:S(2)}, u32[]{:S(2)}) collective-permute-start(bf16[128,256]{1,0:T(8,128)(2,1)} %copy-done.25), channel_id=1, source_target_pairs={{0,2},{1,3},{2,4},{3,5},{4,6},{5,7},{6,0},{7,1},{8,10},{9,11},{10,... | collective-permute-start | bytes 196616 | tf_op jit(solution)/shard_map/ppermute | solution.py:489
  83.2 1.7 %collective-permute-start.2 = (bf16[128,256]{1,0:T(8,128)(2,1)}, bf16[128,256]{1,0:T(8,128)(2,1)}, u32[]{:S(2)}, u32[]{:S(2)}) collective-permute-start(bf16[128,256]{1,0:T(8,128)(2,1)} %copy-done.24), channel_id=1, source_target_pairs={{0,3},{1,4},{2,5},{3,6},{4,7},{5,0},{6,1},{7,2},{8,11},{9,12},{10,... | collective-permute-start | bytes 196616 | tf_op jit(solution)/shard_map/ppermute | solution.py:489
  85.2 2.0 %collective-permute-start.4 = (bf16[128,256]{1,0:T(8,128)(2,1)}, bf16[128,256]{1,0:T(8,128)(2,1)}, u32[]{:S(2)}, u32[]{:S(2)}) collective-permute-start(bf16[128,256]{1,0:T(8,128)(2,1)} %copy-done.22), channel_id=1, source_target_pairs={{0,5},{1,6},{2,7},{3,0},{4,1},{5,2},{6,3},{7,4},{8,13},{9,14},{10,... | collective-permute-start | bytes 196616 | tf_op jit(solution)/shard_map/ppermute | solution.py:489
  87.2 0.6 copy-done.11
  87.8 0.8 collective-permute-start.5
  88.6 0.6 copy-done.13
  89.2 1.6 %collective-permute-start.6 = (bf16[128,256]{1,0:T(8,128)(2,1)}, bf16[128,256]{1,0:T(8,128)(2,1)}, u32[]{:S(2)}, u32[]{:S(2)}) collective-permute-start(bf16[128,256]{1,0:T(8,128)(2,1)} %copy-done.20), channel_id=1, source_target_pairs={{0,7},{1,0},{2,1},{3,2},{4,3},{5,4},{6,5},{7,6},{8,15},{9,8},{10,9... | collective-permute-start | bytes 196616 | tf_op jit(solution)/shard_map/ppermute | solution.py:489
  91.6 2.1 %collective-permute-done.6.rest_7_ = bf16[128,256]{1,0:T(8,128)(2,1)} collective-permute-done((bf16[128,256]{1,0:T(8,128)(2,1)}, bf16[128,256]{1,0:T(8,128)(2,1)}, u32[]{:S(2)}, u32[]{:S(2)}) %collective-permute-start.6) | collective-permute-done | bytes 65568 | tf_op jit(solution)/shard_map/ppermute | solution.py:489
  93.6 0.8 copy-done.10
  94.5 0.8 copy-done.12
  95.3 0.8 copy-done.14
  96.2 1.0 shard_map.125
  97.2 12.8 %all_gather.7 = bf16[1024,256]{1,0:T(8,128)(2,1)S(1)} all-gather(bf16[128,256]{1,0:T(8,128)(2,1)S(1)} %shard_map.125), channel_id=1, replica_groups=mesh['user'=16,'item'=8] {'item'}, dimensions={0}, use_global_device_ids=true | all-gather | bytes 589824 | tf_op jit(solution)/shard_map/all_gather | solution.py:492
  110.2 2.1 %all-to-all-done.2.sums_ref = bf16[16,272,256]{2,1,0:T(8,128)(2,1)S(1)} async-done(((bf16[16,272,256]{2,1,0:T(8,128)(2,1)}), bf16[16,272,256]{2,1,0:T(8,128)(2,1)S(1)}, u32[]{:S(2)}, u32[]{:S(2)}) %all-to-all-start.2) | async-done | bytes 2228256 | tf_op jit(solution)/shard_map/all_to_all | solution.py:487
  112.2 0.6 shard_map.127
  112.9 5.1 %all-to-all-start.3 = ((f32[8,1,256]{2,1,0:T(1,128)}), f32[8,1,256]{2,1,0:T(1,128)S(1)}, u32[]{:S(2)}, u32[]{:S(2)}) async-start(f32[8,1,256]{2,1,0:T(1,128)} %shard_map.127), calls=%async_computation.3 | async-start | bytes 16384 | tf_op jit(solution)/shard_map/all_to_all | solution.py:495
  117.9 1.2 broadcast_add_fusion
  119.1 0.8 copy-done.4
  119.9 2.8 %shard_map.126 = (f32[512,256]{1,0:T(8,128)}, f32[512,256]{1,0:T(8,128)S(1)}) custom-call(s32[1]{0:T(128)} %bitcast.4.seat_ref, f32[16,1,512]{2,1,0:T(1,128)S(1)} %copy-done.4, bf16[16,272,256]{2,1,0:T(8,128)(2,1)S(1)} %all-to-all-done.2.sums_ref, bf16[512,256]{1,0:T(8,128)(2,1)S(1)} %get-tuple-element.25.gain_ref), custom_call_target="tpu_custom_call" | custom-call | flops 5242880 | bytes 3538944 | tf_op jit(solution)/shard_map/pallas_call | solution.py:418
  122.6 0.8 copy-done.5
  123.4 1.0 copy-done.6
  124.5 0.9 copy-done.8
  125.4 0.9 shard_map.128
  (43 shorter events, 1.9 us)
Async XLA Ops:
  0.6 0.7 copy-start.15
  3.7 0.7 copy-start.7
  4.4 14.9 %all-to-all-start = ((f32[16,1,512]{2,1,0:T(1,128)}), f32[16,1,512]{2,1,0:T(1,128)S(1)}, u32[]{:S(2)}, u32[]{:S(2)}) async-start(f32[16,1,512]{2,1,0:T(1,128)} %get-tuple-element.22), calls=%async_computation | async-start | bytes 65536 | tf_op jit(solution)/shard_map/all_to_all | solution.py:477
  19.3 7.2 %copy-start.3 = (f32[16,1,512]{2,1,0:T(1,128)}, f32[16,1,512]{2,1,0:T(1,128)S(1)}, u32[]{:S(2)}) copy-start(f32[16,1,512]{2,1,0:T(1,128)S(1)} %all-to-all-done.head_ref) | copy-start | bytes 98308
  22.1 21.2 %copy-start.16 = (s32[256]{0:T(256)S(1)}, s32[256]{0:T(256)}, u32[]{:S(2)}) copy-start(s32[256]{0:T(256)} %user_of.1) | copy-start | bytes 3076
  22.1 21.2 %copy-start.17 = (s32[256]{0:T(256)S(1)}, s32[256]{0:T(256)}, u32[]{:S(2)}) copy-start(s32[256]{0:T(256)} %slot_of.1) | copy-start | bytes 3076
  22.1 30.6 %all-to-all-start.1 = ((bf16[16,256,256]{2,1,0:T(8,128)(2,1)}), bf16[16,256,256]{2,1,0:T(8,128)(2,1)S(1)}, u32[]{:S(2)}, u32[]{:S(2)}) async-start(bf16[16,256,256]{2,1,0:T(8,128)(2,1)} %shard_map.123), calls=%async_computation.1 | async-start | bytes 4194304 | tf_op jit(solution)/shard_map/all_to_all | solution.py:478
  29.8 0.8 copy-start.18
  46.8 3.3 %copy-start = (bf16[32,8,128,128]{3,2,1,0:T(8,128)(2,1)}, bf16[32,8,128,128]{3,2,1,0:T(8,128)(2,1)S(1)}, u32[]{:S(2)}) copy-start(bf16[32,8,128,128]{3,2,1,0:T(8,128)(2,1)S(1)} %shard_map.122.dense_ref) | copy-start | bytes 25165828
  52.7 3.4 %copy-start.1 = (bf16[32,8,128,128]{3,2,1,0:T(8,128)(2,1)S(1)}, bf16[32,8,128,128]{3,2,1,0:T(8,128)(2,1)}, u32[]{:S(2)}) copy-start(bf16[32,8,128,128]{3,2,1,0:T(8,128)(2,1)} %copy-done) | copy-start | bytes 25165828
  56.1 1.0 copy-start.19
  67.4 0.6 copy-start.9
  68.0 0.6 copy-start.21
  68.6 0.6 copy-start.22
  69.2 0.6 copy-start.23
  69.9 0.6 copy-start.24
  70.5 0.6 copy-start.25
  71.1 0.6 copy-start.26
  71.8 0.6 copy-start.20
  72.4 39.9 %all-to-all-start.2 = ((bf16[16,272,256]{2,1,0:T(8,128)(2,1)}), bf16[16,272,256]{2,1,0:T(8,128)(2,1)S(1)}, u32[]{:S(2)}, u32[]{:S(2)}) async-start(bf16[16,272,256]{2,1,0:T(8,128)(2,1)} %get-tuple-element.36), calls=%async_computation.2 | async-start | bytes 4456448 | tf_op jit(solution)/shard_map/all_to_all | solution.py:487
  79.7 7.5 %collective-permute-start = (bf16[128,256]{1,0:T(8,128)(2,1)}, bf16[128,256]{1,0:T(8,128)(2,1)S(1)}, u32[]{:S(2)}, u32[]{:S(2)}) collective-permute-start(bf16[128,256]{1,0:T(8,128)(2,1)} %copy-done.26), channel_id=1, source_target_pairs={{0,1},{1,2},{2,3},{3,4},{4,5},{5,6},{6,7},{7,0},{8,9},{9,10},{10,1... | collective-permute-start | bytes 196616 | tf_op jit(solution)/shard_map/ppermute | solution.py:489
  81.9 6.8 %collective-permute-start.1 = (bf16[128,256]{1,0:T(8,128)(2,1)}, bf16[128,256]{1,0:T(8,128)(2,1)S(1)}, u32[]{:S(2)}, u32[]{:S(2)}) collective-permute-start(bf16[128,256]{1,0:T(8,128)(2,1)} %copy-done.25), channel_id=1, source_target_pairs={{0,2},{1,3},{2,4},{3,5},{4,6},{5,7},{6,0},{7,1},{8,10},{9,11},{10,... | collective-permute-start | bytes 196616 | tf_op jit(solution)/shard_map/ppermute | solution.py:489
  83.2 7.9 %collective-permute-start.2 = (bf16[128,256]{1,0:T(8,128)(2,1)}, bf16[128,256]{1,0:T(8,128)(2,1)}, u32[]{:S(2)}, u32[]{:S(2)}) collective-permute-start(bf16[128,256]{1,0:T(8,128)(2,1)} %copy-done.24), channel_id=1, source_target_pairs={{0,3},{1,4},{2,5},{3,6},{4,7},{5,0},{6,1},{7,2},{8,11},{9,12},{10,... | collective-permute-start | bytes 196616 | tf_op jit(solution)/shard_map/ppermute | solution.py:489
  84.8 6.2 %collective-permute-start.3 = (bf16[128,256]{1,0:T(8,128)(2,1)}, bf16[128,256]{1,0:T(8,128)(2,1)}, u32[]{:S(2)}, u32[]{:S(2)}) collective-permute-start(bf16[128,256]{1,0:T(8,128)(2,1)} %copy-done.23), channel_id=1, source_target_pairs={{0,4},{1,5},{2,6},{3,7},{4,0},{5,1},{6,2},{7,3},{8,12},{9,13},{10,... | collective-permute-start | bytes 196616 | tf_op jit(solution)/shard_map/ppermute | solution.py:489
  85.2 6.4 %collective-permute-start.4 = (bf16[128,256]{1,0:T(8,128)(2,1)}, bf16[128,256]{1,0:T(8,128)(2,1)}, u32[]{:S(2)}, u32[]{:S(2)}) collective-permute-start(bf16[128,256]{1,0:T(8,128)(2,1)} %copy-done.22), channel_id=1, source_target_pairs={{0,5},{1,6},{2,7},{3,0},{4,1},{5,2},{6,3},{7,4},{8,13},{9,14},{10,... | collective-permute-start | bytes 196616 | tf_op jit(solution)/shard_map/ppermute | solution.py:489
  87.2 0.6 copy-start.11
  87.8 3.8 %collective-permute-start.5 = (bf16[128,256]{1,0:T(8,128)(2,1)}, bf16[128,256]{1,0:T(8,128)(2,1)}, u32[]{:S(2)}, u32[]{:S(2)}) collective-permute-start(bf16[128,256]{1,0:T(8,128)(2,1)} %copy-done.21), channel_id=1, source_target_pairs={{0,6},{1,7},{2,0},{3,1},{4,2},{5,3},{6,4},{7,5},{8,14},{9,15},{10,... | collective-permute-start | bytes 196616 | tf_op jit(solution)/shard_map/ppermute | solution.py:489
  88.6 0.6 copy-start.13
  89.2 4.4 %collective-permute-start.6 = (bf16[128,256]{1,0:T(8,128)(2,1)}, bf16[128,256]{1,0:T(8,128)(2,1)}, u32[]{:S(2)}, u32[]{:S(2)}) collective-permute-start(bf16[128,256]{1,0:T(8,128)(2,1)} %copy-done.20), channel_id=1, source_target_pairs={{0,7},{1,0},{2,1},{3,2},{4,3},{5,4},{6,5},{7,6},{8,15},{9,8},{10,9... | collective-permute-start | bytes 196616 | tf_op jit(solution)/shard_map/ppermute | solution.py:489
  93.6 0.8 copy-start.10
  94.5 0.8 copy-start.12
  95.3 0.8 copy-start.14
  110.1 12.5 %copy-start.2 = (f32[1024,256]{1,0:T(8,128)}, f32[1024,256]{1,0:T(8,128)S(1)}, u32[]{:S(2)}) copy-start(f32[1024,256]{1,0:T(8,128)S(1)} %convert_add_fusion.after_ref) | copy-start | bytes 3145732
  112.9 10.6 %all-to-all-start.3 = ((f32[8,1,256]{2,1,0:T(1,128)}), f32[8,1,256]{2,1,0:T(1,128)S(1)}, u32[]{:S(2)}, u32[]{:S(2)}) async-start(f32[8,1,256]{2,1,0:T(1,128)} %shard_map.127), calls=%async_computation.3 | async-start | bytes 16384 | tf_op jit(solution)/shard_map/all_to_all | solution.py:495
  119.1 0.8 copy-start.4
  122.6 0.8 copy-start.5
  123.4 1.0 copy-start.6
  124.5 0.9 copy-start.8

commit v4 on v3

--- a/solution.py
+++ b/solution.py
@@ -14,8 +14,8 @@
 popularity_prior = 0.3
 popularity_scale = 1.0
 
-VMEM_BYTES = 16 << 20
-SWEEP_BYTES = 28 << 20
+VMEM_BYTES = 24 << 20
+SWEEP_BYTES = 36 << 20
 EXTRA = 16
 LANES = 128
 IN_VMEM = pl.BlockSpec(memory_space=pltpu.VMEM)
@@ -47,50 +47,83 @@
     return gain.astype(jnp.bfloat16), strength / (prior + jnp.sum(mean, axis=1, keepdims=True)), mean
 
 
-def item_gain_kernel(strength, touched_ref, shape_ref, rate_ref, gain_ref, level_ref, head_ref):
-    turn = pl.program_id(0)
-    gain_ref[...], level_ref[...], mean = gains_of(
+def head_kernel(touched_ref, shape_from, rate_from, head_ref, shape_ref, rate_ref, arrived):
+    per_owner, devices = touched_ref.shape
+    rows, factors = shape_ref.shape
+    parts = arrived.shape[1]
+    step = rows // parts
+
+    def fetch(part):
+        piece = pl.ds(part * step, step)
+        return [
+            pltpu.make_async_copy(shape_from.at[piece], shape_ref.at[piece], arrived.at[0, part]),
+            pltpu.make_async_copy(rate_from.at[piece], rate_ref.at[piece], arrived.at[1, part]),
+        ]
+
+    for part in range(parts):
+        for copy in fetch(part):
+            copy.start()
+    head_ref[...] = jnp.zeros_like(head_ref)
+    for place in range(per_owner):
+        blocks = touched_ref[pl.ds(place, 1), :].astype(jnp.float32).reshape(1, 1, devices)
+        head_ref[:, :, pl.ds(place * LANES, devices)] = jnp.broadcast_to(blocks, (devices, 1, devices))
+    total = jnp.zeros((1, factors), jnp.float32)
+    for part in range(parts):
+        for copy in fetch(part):
+            copy.wait()
+        piece = pl.ds(part * step, step)
+        total += jnp.sum(shape_ref[piece, :] / rate_ref[piece, :], axis=0, keepdims=True)
+    head_ref[:, :, pl.ds(per_owner * LANES, factors)] = jnp.broadcast_to(
+        total.reshape(1, 1, factors), (devices, 1, factors)
+    )
+
+
+def head_of(touched, item_shape, item_rate):
+    rows, factors = item_shape.shape
+    devices, per_owner = touched.shape
+    head_shape = (devices, 1, per_owner * LANES + factors)
+    return pl.pallas_call(
+        head_kernel,
+        grid=(1,),
+        in_specs=[pl.BlockSpec((per_owner, devices), lambda r: (0, 0)), IN_PLACE, IN_PLACE],
+        out_specs=pl.BlockSpec(head_shape, lambda r: (0, 0, 0)),
+        out_shape=pltpu.HBM(head_shape, jnp.float32),
+        scratch_shapes=[
+            pltpu.VMEM((rows, factors), jnp.float32),
+            pltpu.VMEM((rows, factors), jnp.float32),
+            pltpu.SemaphoreType.DMA((2, 4)),
+        ],
+        compiler_params=pltpu.CompilerParams(vmem_limit_bytes=VMEM_BYTES),
+        cost_estimate=pl.CostEstimate(
+            flops=4 * rows * factors, bytes_accessed=8 * rows * factors, transcendentals=rows * factors
+        ),
+    )(in_hbm(touched.T), in_hbm(item_shape), in_hbm(item_rate))
+
+
+def item_gain_kernel(strength, shape_ref, rate_ref, gain_ref, level_ref):
+    gain_ref[...], level_ref[...], _ = gains_of(
         shape_ref[...], rate_ref[...], popularity_prior / popularity_scale, strength
     )
-    per_owner, devices = touched_ref.shape
-    factors = mean.shape[1]
-    total = jnp.broadcast_to(jnp.sum(mean, axis=0).reshape(1, 1, factors), (devices, 1, factors))
-
-    @pl.when(turn == 0)
-    def _():
-        head_ref[...] = jnp.zeros_like(head_ref)
-        for place in range(per_owner):
-            blocks = touched_ref[pl.ds(place, 1), :].astype(jnp.float32).reshape(1, 1, devices)
-            head_ref[:, :, pl.ds(place * LANES, devices)] = jnp.broadcast_to(blocks, (devices, 1, devices))
-
-    head_ref[:, :, pl.ds(per_owner * LANES, factors)] += total
-
-
-def item_gains(touched, item_shape, item_rate):
+
+
+def item_gains(item_shape, item_rate):
     rows, factors = item_shape.shape
-    devices, per_owner = touched.shape
     step = rows // 2
     row_spec = pl.BlockSpec((step, factors), lambda r: (r, 0))
-    head_shape = (devices, 1, per_owner * LANES + factors)
     return pl.pallas_call(
         functools.partial(item_gain_kernel, popularity_prior + factors * item_prior),
         grid=(rows // step,),
-        in_specs=[pl.BlockSpec((per_owner, devices), lambda r: (0, 0)), row_spec, row_spec],
-        out_specs=[
-            row_spec,
-            pl.BlockSpec((step, 1), lambda r: (r, 0)),
-            pl.BlockSpec(head_shape, lambda r: (0, 0, 0)),
-        ],
+        in_specs=[row_spec, row_spec],
+        out_specs=[row_spec, pl.BlockSpec((step, 1), lambda r: (r, 0))],
         out_shape=[
-            jax.ShapeDtypeStruct((rows, factors), jnp.bfloat16),
-            jax.ShapeDtypeStruct((rows, 1), jnp.float32),
-            jax.ShapeDtypeStruct(head_shape, jnp.float32),
+            pltpu.HBM((rows, factors), jnp.bfloat16),
+            pltpu.HBM((rows, 1), jnp.float32),
         ],
         compiler_params=pltpu.CompilerParams(vmem_limit_bytes=VMEM_BYTES),
         cost_estimate=pl.CostEstimate(
             flops=40 * rows * factors, bytes_accessed=10 * rows * factors, transcendentals=4 * rows * factors
         ),
-    )(touched.T, in_hbm(item_shape), in_hbm(item_rate))
+    )(in_hbm(item_shape), in_hbm(item_rate))
 
 
 def user_gain_kernel(strength, shape_ref, rate_ref, head_ref, gain_ref, level_ref, turned_ref, column_ref):
@@ -120,10 +153,10 @@
             pl.BlockSpec((1, factors), lambda r: (0, 0)),
         ],
         out_shape=[
-            jax.ShapeDtypeStruct((rows, factors), jnp.bfloat16),
-            jax.ShapeDtypeStruct((rows, 1), jnp.float32),
-            jax.ShapeDtypeStruct((factors, rows), jnp.bfloat16),
-            jax.ShapeDtypeStruct((1, factors), jnp.float32),
+            pltpu.HBM((rows, factors), jnp.bfloat16),
+            pltpu.HBM((rows, 1), jnp.float32),
+            pltpu.HBM((factors, rows), jnp.bfloat16),
+            pltpu.HBM((1, factors), jnp.float32),
         ],
         compiler_params=pltpu.CompilerParams(vmem_limit_bytes=VMEM_BYTES),
         cost_estimate=pl.CostEstimate(
@@ -132,8 +165,15 @@
     )(in_hbm(user_shape), in_hbm(user_rate), heads)
 
 
-def pick_kernel(per_owner, seat_ref, head_ref, gain_ref, picked_ref, sent):
-    edge = gain_ref.shape[1]
+def pick_kernel(per_owner, seat_ref, head_ref, gain_from, picked_ref, gain_ref, arrived, sent):
+    blocks, edge, _ = gain_ref.shape
+    fetches = [
+        pltpu.make_async_copy(gain_from.at[block], gain_ref.at[block], arrived.at[block]) for block in range(blocks)
+    ]
+    for copy in fetches:
+        copy.start()
+    for copy in fetches:
+        copy.wait()
     copies = []
     for device in range(head_ref.shape[0]):
         for place in range(per_owner):
@@ -155,18 +195,22 @@
     devices = heads.shape[0]
     return pl.pallas_call(
         functools.partial(pick_kernel, per_owner),
-        in_specs=[IN_SMEM, IN_SMEM, IN_VMEM],
+        in_specs=[IN_SMEM, IN_SMEM, IN_PLACE],
         out_specs=IN_PLACE,
-        scratch_shapes=[pltpu.SemaphoreType.DMA((devices * per_owner,))],
+        scratch_shapes=[
+            pltpu.VMEM((items // edge, edge, factors), jnp.bfloat16),
+            pltpu.SemaphoreType.DMA((items // edge,)),
+            pltpu.SemaphoreType.DMA((devices * per_owner,)),
+        ],
         out_shape=pltpu.HBM((devices, per_owner * edge, factors), jnp.bfloat16),
         compiler_params=pltpu.CompilerParams(vmem_limit_bytes=VMEM_BYTES),
         cost_estimate=pl.CostEstimate(
             flops=0, bytes_accessed=2 * items * factors + 2 * devices * per_owner * edge * factors, transcendentals=0
         ),
-    )(seat, heads, item_gain.reshape(items // edge, edge, factors))
-
-
-def dense_kernel(user_of, slot_of, live_ref, counts_ref, after_ref, dense_ref, held_ref, arrived):
+    )(seat, heads, in_hbm(item_gain.reshape(items // edge, edge, factors)))
+
+
+def dense_kernel(user_of, slot_of, live_ref, counts_ref, after_ref, out_ref, dense_ref, held_ref, arrived, sent):
     depth, group = held_ref.shape[:2]
     live = live_ref[0]
     groups = (live + group - 1) // group
@@ -207,6 +251,17 @@
         return carry
 
     lax.fori_loop(0, groups, add_group, 0)
+    slots = dense_ref.shape[0] // sent.shape[0]
+    copies = [
+        pltpu.make_async_copy(
+            dense_ref.at[pl.ds(part * slots, slots)], out_ref.at[pl.ds(part * slots, slots)], sent.at[part]
+        )
+        for part in range(sent.shape[0])
+    ]
+    for copy in copies:
+        copy.start()
+    for copy in copies:
+        copy.wait()
 
 
 def dense_counts(counts, tile_user, tile_slot, live_tiles, slot_count, user_blocks, after):
@@ -216,12 +271,14 @@
     return pl.pallas_call(
         dense_kernel,
         in_specs=[IN_SMEM, IN_SMEM, IN_SMEM, IN_PLACE, IN_VMEM],
-        out_specs=IN_VMEM,
+        out_specs=IN_PLACE,
         scratch_shapes=[
+            pltpu.VMEM((slot_count, user_blocks, edge, edge), jnp.bfloat16),
             pltpu.VMEM((depth, group, edge, edge), jnp.int32),
             pltpu.SemaphoreType.DMA((depth,)),
-        ],
-        out_shape=jax.ShapeDtypeStruct((slot_count, user_blocks, edge, edge), jnp.bfloat16),
+            pltpu.SemaphoreType.DMA((16,)),
+        ],
+        out_shape=pltpu.HBM((slot_count, user_blocks, edge, edge), jnp.bfloat16),
         compiler_params=pltpu.CompilerParams(vmem_limit_bytes=VMEM_BYTES),
         cost_estimate=pl.CostEstimate(
             flops=tiles * edge * edge, bytes_accessed=4 * counts.size + 2 * slot_count * user_blocks * edge * edge,
@@ -240,9 +297,11 @@
 
 
 def sweep_kernel(
-    prior_share, place_ref, dense_ref, items_ref, gain_ref, turned_ref, level_ref, total_ref, item_ref, *rest
+    prior_share, place_ref, dense_from, items_ref, gain_from, turned_from, level_from, total_ref, item_ref, *rest
 ):
-    user_refs, (acc_ref, early_ref, late_ref, sums_ref, extra_ref, sent) = rest[:-6], rest[-6:]
+    user_outs, rest = rest[:-12], rest[-12:]
+    dense_ref, gain_ref, turned_ref, level_ref, acc_ref, early_ref, late_ref, sums_ref, extra_ref, users_ref = rest[:10]
+    arrived, sent = rest[10:]
     owners, touched_rows, factors = items_ref.shape
     slots, user_blocks, edge, _ = dense_ref.shape
     users = user_blocks * edge
@@ -291,11 +350,41 @@
         sums_ref[pl.ds(index * pair, pair)] = sums.astype(jnp.bfloat16).T.reshape(pair, touched_rows, factors)
         copy_of(index).start()
 
+    def fetch(index):
+        slots_of = pl.ds(index * pair * per_owner, pair * per_owner)
+        return pltpu.make_async_copy(dense_from.at[slots_of], dense_ref.at[slots_of], arrived.at[index])
+
+    gain_rows = [pl.ds(first, chunk) for first in range(0, users, chunk)]
+    first_copies = [
+        pltpu.make_async_copy(gain_from.at[rows], gain_ref.at[rows], arrived.at[last + 1 + place])
+        for place, rows in enumerate(gain_rows)
+    ]
+    later_copies = [
+        pltpu.make_async_copy(source, target, arrived.at[last + 3 + place])
+        for place, (source, target) in enumerate(((turned_from, turned_ref), (level_from, level_ref)))
+    ]
+    first_copies[0].start()
+    fetch(0).start()
+    first_copies[1].start()
     acc_ref[...] = jnp.zeros_like(acc_ref)
+    for copy in first_copies:
+        copy.wait()
+    later_copies[0].start()
+    for index in range(1, last + 1):
+        fetch(index).start()
+    later_copies[1].start()
+    fetch(0).wait()
     put_ratios(0, denominators(0), early_ref)
+    later_copies[0].wait()
 
     def turn(step, carry):
         first, second, third = 2 * step, 2 * step + 1, jnp.minimum(2 * step + 2, last)
+        fetch(second).wait()
+
+        @pl.when(third > second)
+        def _():
+            fetch(third).wait()
+
         late = denominators(second)
         add_products(first, early_ref)
         put_ratios(second, late, late_ref)
@@ -306,23 +395,29 @@
 
     lax.fori_loop(0, (last + 1) // 2, turn, 0)
 
-    own = users // len(user_refs)
+    own = users // len(user_outs)
+    copies = []
+    for ahead, user_out in enumerate(user_outs):
+        target = (place_ref[0] + ahead) % len(user_outs)
+        rows = pl.ds(pl.multiple_of(target * own, own), own)
+        users_ref[ahead] = acc_ref[rows, :].astype(jnp.bfloat16)
+        copies.append(pltpu.make_async_copy(users_ref.at[ahead], user_out, sent.at[last + 2 + ahead]))
+        copies[-1].start()
+    later_copies[1].wait()
     part = jnp.zeros((1, factors), jnp.float32)
-    for ahead, user_ref in enumerate(user_refs):
-        target = (place_ref[0] + ahead) % len(user_refs)
-        rows = pl.ds(pl.multiple_of(target * own, own), own)
-        user_sums = acc_ref[rows, :]
-        user_ref[...] = user_sums.astype(jnp.bfloat16)
-        shape_share = prior_share + gain_ref[rows, :].astype(jnp.float32) * user_sums
+    for first in range(0, users, own):
+        rows = pl.ds(first, own)
+        shape_share = prior_share + gain_ref[rows, :].astype(jnp.float32) * acc_ref[rows, :]
         part += jnp.sum(shape_share / (level_ref[rows, :] + total_ref[...]), axis=0, keepdims=True)
     extra_ref[...] = jnp.broadcast_to(split_rows(part, EXTRA)[None], extra_ref.shape)
-    extra_copy = pltpu.make_async_copy(
-        extra_ref, item_ref.at[:, pl.ds(touched_rows, EXTRA)], sent.at[last + 1]
+    copies.append(
+        pltpu.make_async_copy(extra_ref, item_ref.at[:, pl.ds(touched_rows, EXTRA)], sent.at[last + 1])
     )
-    extra_copy.start()
+    copies[-1].start()
     for index in range(last + 1):
         copy_of(index).wait()
-    extra_copy.wait()
+    for copy in copies:
+        copy.wait()
 
 
 def sweep(place, dense, items, user_gain, turned_gain, user_level, item_total, parts):
@@ -332,130 +427,149 @@
     pair = 2
     out = pl.pallas_call(
         functools.partial(sweep_kernel, user_prior / parts),
-        in_specs=[IN_SMEM] + [IN_VMEM] * 6,
-        out_specs=[IN_PLACE] + [IN_VMEM] * parts,
+        in_specs=[IN_SMEM, IN_PLACE, IN_VMEM, IN_PLACE, IN_PLACE, IN_PLACE, IN_VMEM],
+        out_specs=[IN_PLACE] * (parts + 1),
         scratch_shapes=[
+            pltpu.VMEM(dense.shape, jnp.bfloat16),
+            pltpu.VMEM((users, factors), jnp.bfloat16),
+            pltpu.VMEM((factors, users), jnp.bfloat16),
+            pltpu.VMEM((users, 1), jnp.float32),
             pltpu.VMEM((users, factors), jnp.float32),
             pltpu.VMEM((users, pair * touched_rows), jnp.bfloat16),
             pltpu.VMEM((users, pair * touched_rows), jnp.bfloat16),
             pltpu.VMEM((owners, touched_rows, factors), jnp.bfloat16),
             pltpu.VMEM((owners, EXTRA, factors), jnp.bfloat16),
-            pltpu.SemaphoreType.DMA((owners // pair + 1,)),
+            pltpu.VMEM((parts, own, factors), jnp.bfloat16),
+            pltpu.SemaphoreType.DMA((owners // pair + 4,)),
+            pltpu.SemaphoreType.DMA((owners // pair + 1 + parts,)),
         ],
         out_shape=[pltpu.HBM((owners, touched_rows + EXTRA, factors), jnp.bfloat16)]
-        + [jax.ShapeDtypeStruct((own, factors), jnp.bfloat16)] * parts,
+        + [pltpu.HBM((own, factors), jnp.bfloat16)] * parts,
         compiler_params=pltpu.CompilerParams(vmem_limit_bytes=SWEEP_BYTES),
         cost_estimate=pl.CostEstimate(
             flops=6 * owners * touched_rows * users * factors,
             bytes_accessed=2 * dense.size + 4 * items.size + 4 * users * factors,
             transcendentals=owners * touched_rows * users,
         ),
-    )(place, dense, items, user_gain, turned_gain, user_level, item_total)
+    )(place, in_hbm(dense), items, in_hbm(user_gain), in_hbm(turned_gain), in_hbm(user_level), item_total)
     return out[0], out[1:]
 
 
 def own_kernel(place_ref, gain_ref, *rest):
     sums_refs, sum_ref = rest[:-1], rest[-1]
-    own = sum_ref.shape[0]
     sums = jnp.zeros(sum_ref.shape, jnp.float32)
     for sums_ref in sums_refs:
         sums += sums_ref[...].astype(jnp.float32)
-    gain = gain_ref[pl.ds(pl.multiple_of(place_ref[0] * own, own), own), :]
-    sum_ref[...] = (gain.astype(jnp.float32) * sums).astype(jnp.bfloat16)
+    sum_ref[...] = (gain_ref[...].astype(jnp.float32) * sums).astype(jnp.bfloat16)
 
 
 def own_users(place, sums, user_gain):
     own, factors = sums[0].shape
+    first = lambda step, place_ref: (0, 0)
     return pl.pallas_call(
         own_kernel,
-        in_specs=[IN_SMEM] + [IN_VMEM] * (len(sums) + 1),
-        out_specs=IN_VMEM,
-        out_shape=jax.ShapeDtypeStruct((own, factors), jnp.bfloat16),
+        grid_spec=pltpu.PrefetchScalarGridSpec(
+            num_scalar_prefetch=1,
+            grid=(1,),
+            in_specs=[pl.BlockSpec((own, factors), lambda step, place_ref: (place_ref[0], 0))]
+            + [pl.BlockSpec((own, factors), first)] * len(sums),
+            out_specs=pl.BlockSpec((own, factors), first),
+        ),
+        out_shape=pltpu.HBM((own, factors), jnp.bfloat16),
         compiler_params=pltpu.CompilerParams(vmem_limit_bytes=VMEM_BYTES),
         cost_estimate=pl.CostEstimate(
             flops=2 * len(sums) * own * factors, bytes_accessed=2 * len(sums) * own * factors, transcendentals=0
         ),
-    )(place, user_gain, *sums)
-
-
-def fold_kernel(sums_ref, after_ref, part_ref):
+    )(place, in_hbm(user_gain), *sums)
+
+
+def fold_kernel(sums_ref, shape_after_ref, rate_after_ref, part_ref):
     extra = sums_ref[0].astype(jnp.float32)
     for sender in range(1, sums_ref.shape[0]):
         extra += sums_ref[sender].astype(jnp.float32)
     part_ref[...] = jnp.broadcast_to(jnp.sum(extra, axis=0).reshape(1, 1, -1), part_ref.shape)
 
 
-def fold(sums, copies, after):
+def fold(sums, copies, *after):
     senders, extended, factors = sums.shape
     return pl.pallas_call(
         fold_kernel,
         grid=(1,),
-        in_specs=[pl.BlockSpec((senders, EXTRA, factors), lambda step: (0, extended // EXTRA - 1, 0)), IN_PLACE],
+        in_specs=[pl.BlockSpec((senders, EXTRA, factors), lambda step: (0, extended // EXTRA - 1, 0)), IN_PLACE, IN_PLACE],
         out_specs=pl.BlockSpec((copies, 1, factors), lambda step: (0, 0, 0)),
-        out_shape=jax.ShapeDtypeStruct((copies, 1, factors), jnp.float32),
+        out_shape=pltpu.HBM((copies, 1, factors), jnp.float32),
         compiler_params=pltpu.CompilerParams(vmem_limit_bytes=VMEM_BYTES),
         cost_estimate=pl.CostEstimate(flops=0, bytes_accessed=2 * senders * EXTRA * factors, transcendentals=0),
-    )(sums, after)
-
-
-def shape_kernel(per_owner, seat_ref, head_ref, sums_ref, gain_ref, shape_ref, digamma_ref, acc_ref):
-    edge = acc_ref.shape[1]
+    )(sums, *(in_hbm(array) for array in after))
+
+
+def shape_kernel(
+    per_owner, seat_ref, head_ref, sums_ref, gain_from, shape_out, digamma_ref, acc_ref, gain_ref, shape_ref, arrived, sent
+):
+    blocks, edge, _ = acc_ref.shape
+    fetch = pltpu.make_async_copy(gain_from, gain_ref, arrived)
+    fetch.start()
     acc_ref[...] = jnp.zeros_like(acc_ref)
     for sender in range(sums_ref.shape[0]):
         for place in range(per_owner):
             block = head_ref[sender, 0, place * LANES + seat_ref[0]].astype(jnp.int32)
             acc_ref[block] += sums_ref[sender, pl.ds(place * edge, edge), :].astype(jnp.float32)
-    for block in range(acc_ref.shape[0]):
+    fetch.wait()
+    copies = []
+    for block in range(blocks):
         rows = pl.ds(block * edge, edge)
         shape_new = item_prior + gain_ref[rows, :].astype(jnp.float32) * acc_ref[block]
         shape_ref[rows, :] = shape_new
+        copies.append(pltpu.make_async_copy(shape_ref.at[rows], shape_out.at[rows], sent.at[block]))
+        copies[-1].start()
         digamma_ref[rows, :] = digamma(shape_new)
+    for copy in copies:
+        copy.wait()
 
 
 def item_shapes(seat, heads, sums, item_gain, edge, per_owner):
     items, factors = item_gain.shape
-    whole = lambda step, seat_ref: (0, 0)
     return pl.pallas_call(
         functools.partial(shape_kernel, per_owner),
-        grid_spec=pltpu.PrefetchScalarGridSpec(
-            num_scalar_prefetch=1,
-            grid=(1,),
-            in_specs=[
-                pl.BlockSpec(heads.shape, lambda step, seat_ref: (0, 0, 0), memory_space=pltpu.SMEM),
-                pl.BlockSpec(sums.shape, lambda step, seat_ref: (0, 0, 0)),
-                pl.BlockSpec((items, factors), whole),
-            ],
-            out_specs=[pl.BlockSpec((items, factors), whole)] * 2,
-            scratch_shapes=[pltpu.VMEM((items // edge, edge, factors), jnp.float32)],
-        ),
-        out_shape=[jax.ShapeDtypeStruct((items, factors), jnp.float32)] * 2,
+        in_specs=[IN_SMEM, IN_SMEM, IN_VMEM, IN_PLACE],
+        out_specs=[IN_PLACE, IN_VMEM],
+        scratch_shapes=[
+            pltpu.VMEM((items // edge, edge, factors), jnp.float32),
+            pltpu.VMEM((items, factors), jnp.bfloat16),
+            pltpu.VMEM((items, factors), jnp.float32),
+            pltpu.SemaphoreType.DMA,
+            pltpu.SemaphoreType.DMA((items // edge,)),
+        ],
+        out_shape=[pltpu.HBM((items, factors), jnp.float32), jax.ShapeDtypeStruct((items, factors), jnp.float32)],
         compiler_params=pltpu.CompilerParams(vmem_limit_bytes=VMEM_BYTES),
         cost_estimate=pl.CostEstimate(
             flops=40 * items * factors, bytes_accessed=2 * sums.size + 10 * items * factors,
             transcendentals=3 * items * factors,
         ),
-    )(seat, heads, sums, item_gain)
-
-
-def elog_kernel(digamma_ref, level_ref, parts_ref, elog_ref):
+    )(seat, heads, sums, in_hbm(item_gain))
+
+
+def elog_kernel(digamma_ref, level_ref, parts_ref, elog_out, elog_ref, sent):
     user_total = jnp.sum(parts_ref[...], axis=0)
-    elog_ref[...] = digamma_ref[...] - jnp.log(level_ref[...] + user_total)
+    step = elog_ref.shape[0] // sent.shape[0]
+    copies = []
+    for piece in range(sent.shape[0]):
+        rows = pl.ds(piece * step, step)
+        elog_ref[rows, :] = digamma_ref[rows, :] - jnp.log(level_ref[rows, :] + user_total)
+        copies.append(pltpu.make_async_copy(elog_ref.at[rows], elog_out.at[rows], sent.at[piece]))
+        copies[-1].start()
+    for copy in copies:
+        copy.wait()
 
 
 def item_elogs(digammas, item_level, user_parts):
     items, factors = digammas.shape
-    step = items // 2
-    row_spec = pl.BlockSpec((step, factors), lambda r: (r, 0))
     return pl.pallas_call(
         elog_kernel,
-        grid=(items // step,),
-        in_specs=[
-            row_spec,
-            pl.BlockSpec((step, 1), lambda r: (r, 0)),
-            pl.BlockSpec(user_parts.shape, lambda r: (0, 0, 0)),
-        ],
-        out_specs=row_spec,
-        out_shape=jax.ShapeDtypeStruct((items, factors), jnp.float32),
+        in_specs=[IN_VMEM, IN_VMEM, IN_VMEM],
+        out_specs=IN_PLACE,
+        scratch_shapes=[pltpu.VMEM((items, factors), jnp.float32), pltpu.SemaphoreType.DMA((4,))],
+        out_shape=pltpu.HBM((items, factors), jnp.float32),
         compiler_params=pltpu.CompilerParams(vmem_limit_bytes=VMEM_BYTES),
         cost_estimate=pl.CostEstimate(
             flops=2 * items * factors, bytes_accessed=8 * items * factors, transcendentals=items * factors
@@ -473,8 +587,8 @@
     columns = lax.axis_size("item")
     place = lax.axis_index("item").astype(jnp.int32).reshape(1)
     seat = lax.axis_index("user").astype(jnp.int32).reshape(1)
-    item_gain, item_level, heads = item_gains(touched, item_shape, item_rate)
-    heads = lax.all_to_all(heads, "user", 0, 0)
+    heads = lax.all_to_all(head_of(touched, item_shape, item_rate), "user", 0, 0)
+    item_gain, item_level = item_gains(item_shape, item_rate)
     item_rows = lax.all_to_all(pick(seat, heads, item_gain, edge, per_owner), "user", 0, 0)
     user_gain, user_level, turned_gain, column_total = user_gains(user_shape, user_rate, heads)
     item_total = jnp.sum(lax.all_gather(column_total, "item", axis=0, tiled=True), axis=0, keepdims=True)
@@ -492,7 +606,7 @@
     user_sum = lax.all_gather(own_users(place, user_sums, user_gain), "item", axis=0, tiled=True)
     user_shape_new = user_prior + user_sum.astype(jnp.float32)
     user_rate_new = user_level + item_total
-    user_parts = lax.all_to_all(fold(item_sums, columns, user_shape_new), "item", 0, 0)
+    user_parts = lax.all_to_all(fold(item_sums, columns, user_shape_new, user_rate_new), "item", 0, 0)
     item_shape_new, digammas = item_shapes(seat, heads, item_sums, item_gain, edge, per_owner)
     item_elog = item_elogs(digammas, item_level, user_parts)
     return (user_shape_new, user_rate_new, item_shape_new, item_elog)

time: 128 us -> 118 us (0.922); the launches traced: 126 us -> 119 us
  local copies, waits for them, and re-layouts: 22.2 us -> 0.06 us
  Pallas kernels: 27.5 us -> 37.6 us
  waiting for transfers between devices: 13.8 us -> 17.7 us
    unnamed x54 -> x24, local copies, waits for them, and re-layouts: 22.2 us -> 0.06 us
    all_to_all x1, waiting for transfers between devices: 2.08 us -> 7.16 us  [shards(): item_sums = lax.all_to_all(item_sums, 'user', 0, 0)]
    pallas_call x3 -> x4, Pallas kernels: 4.75 us -> 8.01 us  [the longest x1 2.86 us: item_shapes(): pl.pallas_call(functools.partial(shape_kernel, per_owner), in_specs=[IN_S...]
    pallas_call x1, Pallas kernels: 3.5 us -> 6.29 us  [dense_counts(): pl.pallas_call(dense_kernel, in_specs=[IN_SMEM, IN_SMEM, IN_SMEM, IN_PLAC...]
    pallas_call x1, Pallas kernels: 10.2 us -> 12.2 us  [sweep(): pl.pallas_call(functools.partial(sweep_kernel, user_prior / parts), in_sp...]
  transfers between devices with their start and end apart: 11 -> 11, of which waited for: 5 -> 7; matrix products, arithmetic and copies ran while one was open for 1% -> 2% of each run, Pallas kernels for 8% -> 15%
where the time goes in v4:
time: 118 us; the launch traced here: 119 us
  Pallas kernels  37.6 us (32%)
  starting transfers between devices  33.9 us (29%)
  blocking collectives  26 us (22%)
  waiting for transfers between devices  17.7 us (15%)
  other arithmetic  2.47 us (2%)
  between operations  1.48 us (1%)
    all_gather x1, blocking collectives, shards(): lax.all_gather(own_users(place, user_sums, user_gain), 'item', axis=0, ti...  13 us
    all_gather x1, blocking collectives, shards(): lax.all_gather(column_total, 'item', axis=0, tiled=True)  12.9 us
    pallas_call x1, Pallas kernels, sweep(): pl.pallas_call(functools.partial(sweep_kernel, user_prior / parts), in_sp...  12.2 us
    ppermute x7, starting transfers between devices, shards(): lax.ppermute(user_sums[k], 'item', [(j, (j + k) % columns) for j in range...  9.07 us
    all_to_all x1, starting transfers between devices, shards(): lax.all_to_all(head_of(touched, item_shape, item_rate), 'user', 0, 0)  8.44 us
    all_to_all x1, starting transfers between devices, shards(): item_sums = lax.all_to_all(item_sums, 'user', 0, 0)  8.33 us
    all_to_all x1, waiting for transfers between devices, shards(): item_sums = lax.all_to_all(item_sums, 'user', 0, 0)  7.16 us
    pallas_call x1, Pallas kernels, dense_counts(): pl.pallas_call(dense_kernel, in_specs=[IN_SMEM, IN_SMEM, IN_SMEM, IN_PLAC...  6.29 us
  transfers between devices with their start and end apart: 11, of which 7 were waited for; matrix products, arithmetic and copies ran while one was open for 2% of the time, Pallas kernels for 15%

profile of v4, /device:TPU:1, one launch (start us, length us, event | category | flops | bytes accessed | tf_op | source)
XLA Modules:
  0.0 119.2 jit_solution(6548343826385370717)
XLA Ops:
  0.6 2.7 %shard_map.120 = f32[16,1,512]{2,1,0:T(1,128)} custom-call(s32[2,16]{1,0:T(2,128)} %bitcast.9, f32[512,256]{1,0:T(8,128)} %shape_ref.3, f32[512,256]{1,0:T(8,128)} %rate_ref.3), custom_call_target="tpu_custom_call" | custom-call | flops 524288 | bytes 1048576 | tf_op jit(solution)/shard_map/pallas_call | solution.py:85
  3.3 8.4 %all-to-all-start = ((f32[16,1,512]{2,1,0:T(1,128)}), f32[16,1,512]{2,1,0:T(1,128)S(1)}, u32[]{:S(2)}, u32[]{:S(2)}) async-start(f32[16,1,512]{2,1,0:T(1,128)} %shard_map.120), calls=%async_computation | async-start | bytes 65536 | tf_op jit(solution)/shard_map/all_to_all | solution.py:590
  11.8 2.4 %shard_map.123 = (bf16[512,256]{1,0:T(8,128)(2,1)}, f32[512,1]{1,0:T(8,128)}) custom-call(f32[512,256]{1,0:T(8,128)} %shape_ref.3, f32[512,256]{1,0:T(8,128)} %rate_ref.3), custom_call_target="tpu_custom_call" | custom-call | flops 5242880 | bytes 1310720 | tf_op jit(solution)/shard_map/pallas_call | solution.py:113
  14.2 4.1 %all-to-all-done.head_ref = f32[16,1,512]{2,1,0:T(1,128)S(1)} async-done(((f32[16,1,512]{2,1,0:T(1,128)}), f32[16,1,512]{2,1,0:T(1,128)S(1)}, u32[]{:S(2)}, u32[]{:S(2)}) %all-to-all-start) | async-done | bytes 32800 | tf_op jit(solution)/shard_map/all_to_all | solution.py:590
  18.2 3.7 %shard_map.124 = bf16[16,256,256]{2,1,0:T(8,128)(2,1)} custom-call(s32[1]{0:T(128)} %bitcast.4.seat_ref, f32[16,1,512]{2,1,0:T(1,128)S(1)} %all-to-all-done.head_ref, bf16[4,128,256]{2,1,0:T(8,128)(2,1)} %bitcast.8), custom_call_target="tpu_custom_call" | custom-call | bytes 2359296 | tf_op jit(solution)/shard_map/pallas_call | solution.py:196
  22.0 0.0 copy-start.2
  22.0 0.0 copy-start.3
  22.0 3.7 %all-to-all-start.1 = ((bf16[16,256,256]{2,1,0:T(8,128)(2,1)}), bf16[16,256,256]{2,1,0:T(8,128)(2,1)S(1)}, u32[]{:S(2)}, u32[]{:S(2)}) async-start(bf16[16,256,256]{2,1,0:T(8,128)(2,1)} %shard_map.124), calls=%async_computation.1 | async-start | bytes 4194304 | tf_op jit(solution)/shard_map/all_to_all | solution.py:592
  26.4 4.3 %shard_map.121 = (bf16[1024,256]{1,0:T(8,128)(2,1)}, f32[1024,1]{1,0:T(8,128)}, bf16[256,1024]{1,0:T(8,128)(2,1)}, f32[1,256]{1,0:T(1,128)}) custom-call(f32[1024,256]{1,0:T(8,128)} %shape_ref.2, f32[1024,256]{1,0:T(8,128)} %rate_ref.2, f32[16,1,512]{2,1,0:T(1,128)S(1)} %all-to-all-done.head_ref), custom_call_target="tpu_custom_call" | custom-call | flops 10485760 | bytes 3145728 | tf_op jit(solution)/shard_map/pallas_call | solution.py:145
  30.7 12.9 %all-gather = f32[8,1,256]{2,1,0:T(1,128)S(1)} all-gather(f32[1,1,256]{2,1,0:T(1,128)} %bitcast.10), channel_id=1, replica_groups=mesh['user'=16,'item'=8] {'item'}, dimensions={0}, use_global_device_ids=true | all-gather | bytes 9216 | tf_op jit(solution)/shard_map/all_gather | solution.py:594
  43.7 0.0 copy-done.2
  43.7 6.3 %shard_map.122.dense_from = bf16[32,8,128,128]{3,2,1,0:T(8,128)(2,1)} custom-call(s32[256]{0:T(256)S(1)} %copy-done.2, s32[256]{0:T(256)S(1)} %copy-done.3, s32[1]{0:T(128)S(6)} %copy.13.live_ref, s32[256,128,128]{2,1,0:T(8,128)} %counts_ref.1, f32[1,256]{1,0:T(1,128)S(1)} %bitcast.6), custom_call_target="tpu_custom_call" | custom-call | flops 4194304 | bytes 25165824 | tf_op jit(solution)/shard_map/pallas_call | solution.py:271
  50.0 2.7 %all-to-all-done.1.items_ref = bf16[16,256,256]{2,1,0:T(8,128)(2,1)S(1)} async-done(((bf16[16,256,256]{2,1,0:T(8,128)(2,1)}), bf16[16,256,256]{2,1,0:T(8,128)(2,1)S(1)}, u32[]{:S(2)}, u32[]{:S(2)}) %all-to-all-start.1) | async-done | bytes 2097184 | tf_op jit(solution)/shard_map/all_to_all | solution.py:592
  52.6 12.2 %shard_map.125 = (bf16[16,272,256]{2,1,0:T(8,128)(2,1)}, bf16[128,256]{1,0:T(8,128)(2,1)}, bf16[128,256]{1,0:T(8,128)(2,1)}, bf16[128,256]{1,0:T(8,128)(2,1)}, b...) custom-call(s32[1]{0:T(128)} %bitcast.place_ref, ...), custom_call_target="tpu_custom_call" | custom-call | flops 6442450944 | bytes 13631488 | tf_op jit(solution)/shard_map/pallas_call | solution.py:428
  64.9 0.0 copy-start.4
  64.9 0.0 copy-start.9
  64.9 0.0 copy-start.8
  64.9 0.0 copy-start.7
  64.9 0.0 copy-start.6
  64.9 0.0 copy-start.5
  64.9 0.0 copy-start.1
  64.9 8.3 %all-to-all-start.2 = ((bf16[16,272,256]{2,1,0:T(8,128)(2,1)}), bf16[16,272,256]{2,1,0:T(8,128)(2,1)S(1)}, u32[]{:S(2)}, u32[]{:S(2)}) async-start(bf16[16,272,256]{2,1,0:T(8,128)(2,1)} %get-tuple-element.34), calls=%async_computation.2 | async-start | bytes 4456448 | tf_op jit(solution)/shard_map/all_to_all | solution.py:601
  73.3 1.3 %collective-permute-start = (bf16[128,256]{1,0:T(8,128)(2,1)S(1)}, bf16[128,256]{1,0:T(8,128)(2,1)S(1)}, u32[]{:S(2)}, u32[]{:S(2)}) collective-permute-start(bf16[128,256]{1,0:T(8,128)(2,1)S(1)} %copy-done.11), channel_id=1, source_target_pairs={{0,1},{1,2},{2,3},{3,4},{4,5},{5,6},{6,7},{7,0},{8,9},{9,10},{10,1... | collective-permute-start | bytes 196616 | tf_op jit(solution)/shard_map/ppermute | solution.py:603
  74.6 1.3 %collective-permute-start.1 = (bf16[128,256]{1,0:T(8,128)(2,1)S(1)}, bf16[128,256]{1,0:T(8,128)(2,1)S(1)}, u32[]{:S(2)}, u32[]{:S(2)}) collective-permute-start(bf16[128,256]{1,0:T(8,128)(2,1)S(1)} %copy-done.10), channel_id=1, source_target_pairs={{0,2},{1,3},{2,4},{3,5},{4,6},{5,7},{6,0},{7,1},{8,10},{9,11},{10,... | collective-permute-start | bytes 196616 | tf_op jit(solution)/shard_map/ppermute | solution.py:603
  75.9 0.0 copy-done.4
  75.9 0.2 reduce.1
  76.1 1.8 %collective-permute-start.2 = (bf16[128,256]{1,0:T(8,128)(2,1)S(1)}, bf16[128,256]{1,0:T(8,128)(2,1)S(1)}, u32[]{:S(2)}, u32[]{:S(2)}) collective-permute-start(bf16[128,256]{1,0:T(8,128)(2,1)S(1)} %copy-done.9), channel_id=1, source_target_pairs={{0,3},{1,4},{2,5},{3,6},{4,7},{5,0},{6,1},{7,2},{8,11},{9,12},{10,... | collective-permute-start | bytes 196616 | tf_op jit(solution)/shard_map/ppermute | solution.py:603
  77.9 0.4 collective-permute-start.3
  78.2 1.9 %collective-permute-start.4 = (bf16[128,256]{1,0:T(8,128)(2,1)S(1)}, bf16[128,256]{1,0:T(8,128)(2,1)S(1)}, u32[]{:S(2)}, u32[]{:S(2)}) collective-permute-start(bf16[128,256]{1,0:T(8,128)(2,1)S(1)} %copy-done.7), channel_id=1, source_target_pairs={{0,5},{1,6},{2,7},{3,0},{4,1},{5,2},{6,3},{7,4},{8,13},{9,14},{10,... | collective-permute-start | bytes 196616 | tf_op jit(solution)/shard_map/ppermute | solution.py:603
  80.2 0.0 collective-permute-done.rest_1_
  80.2 0.8 collective-permute-start.5
  81.0 0.0 collective-permute-done.1.rest_2_
  81.0 1.6 %collective-permute-start.6 = (bf16[128,256]{1,0:T(8,128)(2,1)S(1)}, bf16[128,256]{1,0:T(8,128)(2,1)S(1)}, u32[]{:S(2)}, u32[]{:S(2)}) collective-permute-start(bf16[128,256]{1,0:T(8,128)(2,1)S(1)} %copy-done.5), channel_id=1, source_target_pairs={{0,7},{1,0},{2,1},{3,2},{4,3},{5,4},{6,5},{7,6},{8,15},{9,8},{10,9... | collective-permute-start | bytes 196616 | tf_op jit(solution)/shard_map/ppermute | solution.py:603
  82.6 1.2 broadcast_add_fusion.rate_after_ref
  83.8 0.0 collective-permute-done.2.rest_3_
  83.8 0.0 collective-permute-done.3.rest_4_
  83.8 0.4 collective-permute-done.4.rest_5_
  84.2 0.1 collective-permute-done.5.rest_6_
  84.3 1.5 %collective-permute-done.6.rest_7_ = bf16[128,256]{1,0:T(8,128)(2,1)S(1)} collective-permute-done((bf16[128,256]{1,0:T(8,128)(2,1)S(1)}, bf16[128,256]{1,0:T(8,128)(2,1)S(1)}, u32[]{:S(2)}, u32[]{:S(2)}) %collective-permute-start.6) | collective-permute-done | bytes 65568 | tf_op jit(solution)/shard_map/ppermute | solution.py:603
  85.8 1.5 %shard_map.126 = bf16[128,256]{1,0:T(8,128)(2,1)} custom-call(s32[1]{0:T(128)} %bitcast.place_ref, bf16[1024,256]{1,0:T(8,128)(2,1)} %get-tuple-element.21.gain_from.gain_ref, bf16[128,256]{1,0:T(8,128)(2,1)S(1)} %copy-done.1, bf16[128,256]{1,0:T(8,128)(2,1)S(1)} %collective-permute-done.rest_1_, bf16[128,256]{1,0:T(8,128)(2,1)S(1)} %collective-permute-done.1.rest_2_, ...), custom_call_target="tpu_custom_call" | custom-call | flops 524288 | bytes 524288 | tf_op jit(solution)/shard_map/pallas_call | solution.py:469
  87.4 13.0 %all_gather.7 = bf16[1024,256]{1,0:T(8,128)(2,1)S(1)} all-gather(bf16[128,256]{1,0:T(8,128)(2,1)} %shard_map.126), channel_id=1, replica_groups=mesh['user'=16,'item'=8] {'item'}, dimensions={0}, use_global_device_ids=true | all-gather | bytes 589824 | tf_op jit(solution)/shard_map/all_gather | solution.py:606
  100.4 1.1 convert_add_fusion.shape_after_ref
  101.5 7.2 %all-to-all-done.2.sums_ref = bf16[16,272,256]{2,1,0:T(8,128)(2,1)S(1)} async-done(((bf16[16,272,256]{2,1,0:T(8,128)(2,1)}), bf16[16,272,256]{2,1,0:T(8,128)(2,1)S(1)}, u32[]{:S(2)}, u32[]{:S(2)}) %all-to-all-start.2) | async-done | bytes 2228256 | tf_op jit(solution)/shard_map/all_to_all | solution.py:601
  108.6 0.6 shard_map.128
  109.3 4.3 %all-to-all-start.3 = ((f32[8,1,256]{2,1,0:T(1,128)}), f32[8,1,256]{2,1,0:T(1,128)S(1)}, u32[]{:S(2)}, u32[]{:S(2)}) async-start(f32[8,1,256]{2,1,0:T(1,128)} %shard_map.128), calls=%async_computation.3 | async-start | bytes 16384 | tf_op jit(solution)/shard_map/all_to_all | solution.py:609
  113.6 2.9 %shard_map.127 = (f32[512,256]{1,0:T(8,128)}, f32[512,256]{1,0:T(8,128)S(1)}) custom-call(s32[1]{0:T(128)} %bitcast.4.seat_ref, f32[16,1,512]{2,1,0:T(1,128)S(1)} %all-to-all-done.head_ref, bf16[16,272,256]{2,1,0:T(8,128)(2,1)S(1)} %all-to-all-done.2.sums_ref, bf16[512,256]{1,0:T(8,128)(2,1)} %get-tuple-element.23.gain_from), custom_call_target="tpu_custom_call" | custom-call | flops 5242880 | bytes 3538944 | tf_op jit(solution)/shard_map/pallas_call | solution.py:532
  116.5 1.8 %all-to-all-done.3.parts_ref = f32[8,1,256]{2,1,0:T(1,128)S(1)} async-done(((f32[8,1,256]{2,1,0:T(1,128)}), f32[8,1,256]{2,1,0:T(1,128)S(1)}, u32[]{:S(2)}, u32[]{:S(2)}) %all-to-all-start.3) | async-done | bytes 8224 | tf_op jit(solution)/shard_map/all_to_all | solution.py:609
  118.2 0.9 shard_map.129
  (14 shorter events, 0.1 us)
Async XLA Ops:
  3.3 14.9 %all-to-all-start = ((f32[16,1,512]{2,1,0:T(1,128)}), f32[16,1,512]{2,1,0:T(1,128)S(1)}, u32[]{:S(2)}, u32[]{:S(2)}) async-start(f32[16,1,512]{2,1,0:T(1,128)} %shard_map.120), calls=%async_computation | async-start | bytes 65536 | tf_op jit(solution)/shard_map/all_to_all | solution.py:590
  22.0 21.7 %copy-start.2 = (s32[256]{0:T(256)S(1)}, s32[256]{0:T(256)}, u32[]{:S(2)}) copy-start(s32[256]{0:T(256)} %user_of.1) | copy-start | bytes 3076
  22.0 21.7 %copy-start.3 = (s32[256]{0:T(256)S(1)}, s32[256]{0:T(256)}, u32[]{:S(2)}) copy-start(s32[256]{0:T(256)} %slot_of.1) | copy-start | bytes 3076
  22.0 30.6 %all-to-all-start.1 = ((bf16[16,256,256]{2,1,0:T(8,128)(2,1)}), bf16[16,256,256]{2,1,0:T(8,128)(2,1)S(1)}, u32[]{:S(2)}, u32[]{:S(2)}) async-start(bf16[16,256,256]{2,1,0:T(8,128)(2,1)} %shard_map.124), calls=%async_computation.1 | async-start | bytes 4194304 | tf_op jit(solution)/shard_map/all_to_all | solution.py:592
  64.8 8.4 %copy-start.11 = (bf16[128,256]{1,0:T(8,128)(2,1)S(1)}, bf16[128,256]{1,0:T(8,128)(2,1)}, u32[]{:S(2)}) copy-start(bf16[128,256]{1,0:T(8,128)(2,1)} %get-tuple-element.27) | copy-start | bytes 196612
  64.8 9.7 %copy-start.10 = (bf16[128,256]{1,0:T(8,128)(2,1)S(1)}, bf16[128,256]{1,0:T(8,128)(2,1)}, u32[]{:S(2)}) copy-start(bf16[128,256]{1,0:T(8,128)(2,1)} %get-tuple-element.28) | copy-start | bytes 196612
  64.9 11.0 %copy-start.4 = (f32[1024,1]{1,0:T(8,128)S(1)}, f32[1024,1]{1,0:T(8,128)}, u32[]{:S(2)}) copy-start(f32[1024,1]{1,0:T(8,128)} %get-tuple-element.25.level_from) | copy-start | bytes 12292
  64.9 11.2 %copy-start.9 = (bf16[128,256]{1,0:T(8,128)(2,1)S(1)}, bf16[128,256]{1,0:T(8,128)(2,1)}, u32[]{:S(2)}) copy-start(bf16[128,256]{1,0:T(8,128)(2,1)} %get-tuple-element.29) | copy-start | bytes 196612
  64.9 13.0 %copy-start.8 = (bf16[128,256]{1,0:T(8,128)(2,1)S(1)}, bf16[128,256]{1,0:T(8,128)(2,1)}, u32[]{:S(2)}) copy-start(bf16[128,256]{1,0:T(8,128)(2,1)} %get-tuple-element.30) | copy-start | bytes 196612
  64.9 13.3 %copy-start.7 = (bf16[128,256]{1,0:T(8,128)(2,1)S(1)}, bf16[128,256]{1,0:T(8,128)(2,1)}, u32[]{:S(2)}) copy-start(bf16[128,256]{1,0:T(8,128)(2,1)} %get-tuple-element.31) | copy-start | bytes 196612
  64.9 15.3 %copy-start.6 = (bf16[128,256]{1,0:T(8,128)(2,1)S(1)}, bf16[128,256]{1,0:T(8,128)(2,1)}, u32[]{:S(2)}) copy-start(bf16[128,256]{1,0:T(8,128)(2,1)} %get-tuple-element.32) | copy-start | bytes 196612
  64.9 16.1 %copy-start.5 = (bf16[128,256]{1,0:T(8,128)(2,1)S(1)}, bf16[128,256]{1,0:T(8,128)(2,1)}, u32[]{:S(2)}) copy-start(bf16[128,256]{1,0:T(8,128)(2,1)} %get-tuple-element.33) | copy-start | bytes 196612
  64.9 20.9 %copy-start.1 = (bf16[128,256]{1,0:T(8,128)(2,1)S(1)}, bf16[128,256]{1,0:T(8,128)(2,1)}, u32[]{:S(2)}) copy-start(bf16[128,256]{1,0:T(8,128)(2,1)} %get-tuple-element.26.rest_0_) | copy-start | bytes 196612
  64.9 43.7 %all-to-all-start.2 = ((bf16[16,272,256]{2,1,0:T(8,128)(2,1)}), bf16[16,272,256]{2,1,0:T(8,128)(2,1)S(1)}, u32[]{:S(2)}, u32[]{:S(2)}) async-start(bf16[16,272,256]{2,1,0:T(8,128)(2,1)} %get-tuple-element.34), calls=%async_computation.2 | async-start | bytes 4456448 | tf_op jit(solution)/shard_map/all_to_all | solution.py:601
  73.3 6.9 %collective-permute-start = (bf16[128,256]{1,0:T(8,128)(2,1)S(1)}, bf16[128,256]{1,0:T(8,128)(2,1)S(1)}, u32[]{:S(2)}, u32[]{:S(2)}) collective-permute-start(bf16[128,256]{1,0:T(8,128)(2,1)S(1)} %copy-done.11), channel_id=1, source_target_pairs={{0,1},{1,2},{2,3},{3,4},{4,5},{5,6},{6,7},{7,0},{8,9},{9,10},{10,1... | collective-permute-start | bytes 196616 | tf_op jit(solution)/shard_map/ppermute | solution.py:603
  74.6 6.4 %collective-permute-start.1 = (bf16[128,256]{1,0:T(8,128)(2,1)S(1)}, bf16[128,256]{1,0:T(8,128)(2,1)S(1)}, u32[]{:S(2)}, u32[]{:S(2)}) collective-permute-start(bf16[128,256]{1,0:T(8,128)(2,1)S(1)} %copy-done.10), channel_id=1, source_target_pairs={{0,2},{1,3},{2,4},{3,5},{4,6},{5,7},{6,0},{7,1},{8,10},{9,11},{10,... | collective-permute-start | bytes 196616 | tf_op jit(solution)/shard_map/ppermute | solution.py:603
  76.1 7.7 %collective-permute-start.2 = (bf16[128,256]{1,0:T(8,128)(2,1)S(1)}, bf16[128,256]{1,0:T(8,128)(2,1)S(1)}, u32[]{:S(2)}, u32[]{:S(2)}) collective-permute-start(bf16[128,256]{1,0:T(8,128)(2,1)S(1)} %copy-done.9), channel_id=1, source_target_pairs={{0,3},{1,4},{2,5},{3,6},{4,7},{5,0},{6,1},{7,2},{8,11},{9,12},{10,... | collective-permute-start | bytes 196616 | tf_op jit(solution)/shard_map/ppermute | solution.py:603
  77.9 5.9 %collective-permute-start.3 = (bf16[128,256]{1,0:T(8,128)(2,1)S(1)}, bf16[128,256]{1,0:T(8,128)(2,1)S(1)}, u32[]{:S(2)}, u32[]{:S(2)}) collective-permute-start(bf16[128,256]{1,0:T(8,128)(2,1)S(1)} %copy-done.8), channel_id=1, source_target_pairs={{0,4},{1,5},{2,6},{3,7},{4,0},{5,1},{6,2},{7,3},{8,12},{9,13},{10,... | collective-permute-start | bytes 196616 | tf_op jit(solution)/shard_map/ppermute | solution.py:603
  78.2 6.0 %collective-permute-start.4 = (bf16[128,256]{1,0:T(8,128)(2,1)S(1)}, bf16[128,256]{1,0:T(8,128)(2,1)S(1)}, u32[]{:S(2)}, u32[]{:S(2)}) collective-permute-start(bf16[128,256]{1,0:T(8,128)(2,1)S(1)} %copy-done.7), channel_id=1, source_target_pairs={{0,5},{1,6},{2,7},{3,0},{4,1},{5,2},{6,3},{7,4},{8,13},{9,14},{10,... | collective-permute-start | bytes 196616 | tf_op jit(solution)/shard_map/ppermute | solution.py:603
  80.2 4.2 %collective-permute-start.5 = (bf16[128,256]{1,0:T(8,128)(2,1)S(1)}, bf16[128,256]{1,0:T(8,128)(2,1)S(1)}, u32[]{:S(2)}, u32[]{:S(2)}) collective-permute-start(bf16[128,256]{1,0:T(8,128)(2,1)S(1)} %copy-done.6), channel_id=1, source_target_pairs={{0,6},{1,7},{2,0},{3,1},{4,2},{5,3},{6,4},{7,5},{8,14},{9,15},{10,... | collective-permute-start | bytes 196616 | tf_op jit(solution)/shard_map/ppermute | solution.py:603
  81.0 4.8 %collective-permute-start.6 = (bf16[128,256]{1,0:T(8,128)(2,1)S(1)}, bf16[128,256]{1,0:T(8,128)(2,1)S(1)}, u32[]{:S(2)}, u32[]{:S(2)}) collective-permute-start(bf16[128,256]{1,0:T(8,128)(2,1)S(1)} %copy-done.5), channel_id=1, source_target_pairs={{0,7},{1,0},{2,1},{3,2},{4,3},{5,4},{6,5},{7,6},{8,15},{9,8},{10,9... | collective-permute-start | bytes 196616 | tf_op jit(solution)/shard_map/ppermute | solution.py:603
  109.3 9.0 %copy-start = (f32[512,1]{1,0:T(8,128)S(1)}, f32[512,1]{1,0:T(8,128)}, u32[]{:S(2)}) copy-start(f32[512,1]{1,0:T(8,128)} %get-tuple-element.37.level_ref) | copy-start | bytes 6148
  109.3 9.0 %all-to-all-start.3 = ((f32[8,1,256]{2,1,0:T(1,128)}), f32[8,1,256]{2,1,0:T(1,128)S(1)}, u32[]{:S(2)}, u32[]{:S(2)}) async-start(f32[8,1,256]{2,1,0:T(1,128)} %shard_map.128), calls=%async_computation.3 | async-start | bytes 16384 | tf_op jit(solution)/shard_map/all_to_all | solution.py:609

commit v5 on v4

--- a/solution.py
+++ b/solution.py
@@ -47,51 +47,55 @@
     return gain.astype(jnp.bfloat16), strength / (prior + jnp.sum(mean, axis=1, keepdims=True)), mean
 
 
-def head_kernel(touched_ref, shape_from, rate_from, head_ref, shape_ref, rate_ref, arrived):
+def head_kernel(touched_from, shape_from, rate_from, head_ref, touched_ref, shape_ref, rate_ref, arrived):
     per_owner, devices = touched_ref.shape
     rows, factors = shape_ref.shape
-    parts = arrived.shape[1]
+    parts = (arrived.shape[0] - 1) // 2
     step = rows // parts
 
     def fetch(part):
         piece = pl.ds(part * step, step)
         return [
-            pltpu.make_async_copy(shape_from.at[piece], shape_ref.at[piece], arrived.at[0, part]),
-            pltpu.make_async_copy(rate_from.at[piece], rate_ref.at[piece], arrived.at[1, part]),
+            pltpu.make_async_copy(shape_from.at[piece], shape_ref.at[piece], arrived.at[2 * part]),
+            pltpu.make_async_copy(rate_from.at[piece], rate_ref.at[piece], arrived.at[2 * part + 1]),
         ]
 
+    table = pltpu.make_async_copy(touched_from, touched_ref, arrived.at[2 * parts])
     for part in range(parts):
         for copy in fetch(part):
             copy.start()
-    head_ref[...] = jnp.zeros_like(head_ref)
-    for place in range(per_owner):
-        blocks = touched_ref[pl.ds(place, 1), :].astype(jnp.float32).reshape(1, 1, devices)
-        head_ref[:, :, pl.ds(place * LANES, devices)] = jnp.broadcast_to(blocks, (devices, 1, devices))
+    table.start()
     total = jnp.zeros((1, factors), jnp.float32)
     for part in range(parts):
         for copy in fetch(part):
             copy.wait()
         piece = pl.ds(part * step, step)
         total += jnp.sum(shape_ref[piece, :] / rate_ref[piece, :], axis=0, keepdims=True)
-    head_ref[:, :, pl.ds(per_owner * LANES, factors)] = jnp.broadcast_to(
-        total.reshape(1, 1, factors), (devices, 1, factors)
+    table.wait()
+    blocks = touched_ref[...].astype(jnp.float32)
+    row = jnp.concatenate(
+        [blocks[place : place + 1] for place in range(per_owner)]
+        + [jnp.zeros((1, LANES - per_owner * devices), jnp.float32), total],
+        axis=1,
     )
+    head_ref[...] = jnp.broadcast_to(row.reshape(1, 1, LANES + factors), head_ref.shape)
 
 
 def head_of(touched, item_shape, item_rate):
     rows, factors = item_shape.shape
     devices, per_owner = touched.shape
-    head_shape = (devices, 1, per_owner * LANES + factors)
+    head_shape = (devices, 1, LANES + factors)
     return pl.pallas_call(
         head_kernel,
         grid=(1,),
-        in_specs=[pl.BlockSpec((per_owner, devices), lambda r: (0, 0)), IN_PLACE, IN_PLACE],
+        in_specs=[IN_PLACE, IN_PLACE, IN_PLACE],
         out_specs=pl.BlockSpec(head_shape, lambda r: (0, 0, 0)),
         out_shape=pltpu.HBM(head_shape, jnp.float32),
         scratch_shapes=[
+            pltpu.VMEM((per_owner, devices), jnp.int32),
             pltpu.VMEM((rows, factors), jnp.float32),
             pltpu.VMEM((rows, factors), jnp.float32),
-            pltpu.SemaphoreType.DMA((2, 4)),
+            pltpu.SemaphoreType.DMA((9,)),
         ],
         compiler_params=pltpu.CompilerParams(vmem_limit_bytes=VMEM_BYTES),
         cost_estimate=pl.CostEstimate(
@@ -165,27 +169,30 @@
     )(in_hbm(user_shape), in_hbm(user_rate), heads)
 
 
-def pick_kernel(per_owner, seat_ref, head_ref, gain_from, picked_ref, gain_ref, arrived, sent):
+def block_at(table_ref, device, place, seat):
+    return table_ref[device, 0, place * table_ref.shape[0] + seat].astype(jnp.int32)
+
+
+def pick_kernel(per_owner, seat_ref, head_from, gain_from, picked_out, table_ref, gain_ref, picked_ref, arrived, sent):
     blocks, edge, _ = gain_ref.shape
-    fetches = [
+    devices = table_ref.shape[0]
+    fetches = [pltpu.make_async_copy(head_from.at[:, :, pl.ds(0, LANES)], table_ref, arrived.at[blocks])] + [
         pltpu.make_async_copy(gain_from.at[block], gain_ref.at[block], arrived.at[block]) for block in range(blocks)
     ]
     for copy in fetches:
         copy.start()
     for copy in fetches:
         copy.wait()
+    per_copy = devices // sent.shape[0]
     copies = []
-    for device in range(head_ref.shape[0]):
-        for place in range(per_owner):
-            block = head_ref[device, 0, place * LANES + seat_ref[0]].astype(jnp.int32)
-            copies.append(
-                pltpu.make_async_copy(
-                    gain_ref.at[block],
-                    picked_ref.at[device, pl.ds(place * edge, edge)],
-                    sent.at[device * per_owner + place],
-                )
-            )
-            copies[-1].start()
+    for part in range(sent.shape[0]):
+        for device in range(part * per_copy, (part + 1) * per_copy):
+            for place in range(per_owner):
+                block = block_at(table_ref, device, place, seat_ref[0])
+                picked_ref[device, pl.ds(place * edge, edge), :] = gain_ref[block]
+        piece = pl.ds(part * per_copy, per_copy)
+        copies.append(pltpu.make_async_copy(picked_ref.at[piece], picked_out.at[piece], sent.at[part]))
+        copies[-1].start()
     for copy in copies:
         copy.wait()
 
@@ -195,12 +202,14 @@
     devices = heads.shape[0]
     return pl.pallas_call(
         functools.partial(pick_kernel, per_owner),
-        in_specs=[IN_SMEM, IN_SMEM, IN_PLACE],
+        in_specs=[IN_SMEM, IN_PLACE, IN_PLACE],
         out_specs=IN_PLACE,
         scratch_shapes=[
+            pltpu.SMEM((devices, 1, LANES), jnp.float32),
             pltpu.VMEM((items // edge, edge, factors), jnp.bfloat16),
-            pltpu.SemaphoreType.DMA((items // edge,)),
-            pltpu.SemaphoreType.DMA((devices * per_owner,)),
+            pltpu.VMEM((devices, per_owner * edge, factors), jnp.bfloat16),
+            pltpu.SemaphoreType.DMA((items // edge + 1,)),
+            pltpu.SemaphoreType.DMA((min(8, devices),)),
         ],
         out_shape=pltpu.HBM((devices, per_owner * edge, factors), jnp.bfloat16),
         compiler_params=pltpu.CompilerParams(vmem_limit_bytes=VMEM_BYTES),
@@ -330,9 +339,9 @@
                 ],
                 axis=1,
             ).astype(jnp.float32)
-            inverse = pl.reciprocal(denominator, approx=True)
-            inverse *= 2.0 - denominator * inverse
-            ratio_ref[pl.ds(place * chunk, chunk), :] = (counted * inverse).astype(jnp.bfloat16)
+            ratio_ref[pl.ds(place * chunk, chunk), :] = (counted * pl.reciprocal(denominator, approx=True)).astype(
+                jnp.bfloat16
+            )
 
     def copy_of(index):
         return pltpu.make_async_copy(
@@ -408,7 +417,8 @@
     for first in range(0, users, own):
         rows = pl.ds(first, own)
         shape_share = prior_share + gain_ref[rows, :].astype(jnp.float32) * acc_ref[rows, :]
-        part += jnp.sum(shape_share / (level_ref[rows, :] + total_ref[...]), axis=0, keepdims=True)
+        inverse_rate = pl.reciprocal(level_ref[rows, :] + total_ref[...], approx=True)
+        part += jnp.sum(shape_share * inverse_rate, axis=0, keepdims=True)
     extra_ref[...] = jnp.broadcast_to(split_rows(part, EXTRA)[None], extra_ref.shape)
     copies.append(
         pltpu.make_async_copy(extra_ref, item_ref.at[:, pl.ds(touched_rows, EXTRA)], sent.at[last + 1])
@@ -504,17 +514,21 @@
 
 
 def shape_kernel(
-    per_owner, seat_ref, head_ref, sums_ref, gain_from, shape_out, digamma_ref, acc_ref, gain_ref, shape_ref, arrived, sent
+    per_owner, seat_ref, head_from, sums_ref, gain_from, shape_out, digamma_ref, table_ref, acc_ref, gain_ref, shape_ref,
+    arrived, sent,
 ):
     blocks, edge, _ = acc_ref.shape
-    fetch = pltpu.make_async_copy(gain_from, gain_ref, arrived)
-    fetch.start()
+    table = pltpu.make_async_copy(head_from.at[:, :, pl.ds(0, LANES)], table_ref, arrived.at[0])
+    gains = pltpu.make_async_copy(gain_from, gain_ref, arrived.at[1])
+    table.start()
+    gains.start()
     acc_ref[...] = jnp.zeros_like(acc_ref)
+    table.wait()
     for sender in range(sums_ref.shape[0]):
         for place in range(per_owner):
-            block = head_ref[sender, 0, place * LANES + seat_ref[0]].astype(jnp.int32)
+            block = block_at(table_ref, sender, place, seat_ref[0])
             acc_ref[block] += sums_ref[sender, pl.ds(place * edge, edge), :].astype(jnp.float32)
-    fetch.wait()
+    gains.wait()
     copies = []
     for block in range(blocks):
         rows = pl.ds(block * edge, edge)
@@ -531,13 +545,14 @@
     items, factors = item_gain.shape
     return pl.pallas_call(
         functools.partial(shape_kernel, per_owner),
-        in_specs=[IN_SMEM, IN_SMEM, IN_VMEM, IN_PLACE],
+        in_specs=[IN_SMEM, IN_PLACE, IN_VMEM, IN_PLACE],
         out_specs=[IN_PLACE, IN_VMEM],
         scratch_shapes=[
+            pltpu.SMEM((heads.shape[0], 1, LANES), jnp.float32),
             pltpu.VMEM((items // edge, edge, factors), jnp.float32),
             pltpu.VMEM((items, factors), jnp.bfloat16),
             pltpu.VMEM((items, factors), jnp.float32),
-            pltpu.SemaphoreType.DMA,
+            pltpu.SemaphoreType.DMA((2,)),
             pltpu.SemaphoreType.DMA((items // edge,)),
         ],
         out_shape=[pltpu.HBM((items, factors), jnp.float32), jax.ShapeDtypeStruct((items, factors), jnp.float32)],

time: 118 us -> 116 us (0.983)
  Pallas kernels: 37.6 us -> 36.1 us
  waiting for transfers between devices: 17.7 us -> 16.3 us
    all_to_all x1, waiting for transfers between devices: 2.65 us -> 1.05 us  [shards(): lax.all_to_all(pick(seat, heads, item_gain, edge, per_owner), 'user', 0, 0)]
    pallas_call x1, Pallas kernels: 6.29 us -> 7.75 us  [dense_counts(): pl.pallas_call(dense_kernel, in_specs=[IN_SMEM, IN_SMEM, IN_SMEM, IN_PLAC...]
    pallas_call x1, Pallas kernels: 3.73 us -> 2.47 us  [pick(): pl.pallas_call(functools.partial(pick_kernel, per_owner), in_specs=[IN_SM...]
where the time goes in v5:
time: 116 us; the launch traced here: 117 us
  Pallas kernels  36.1 us (31%)
  starting transfers between devices  34.4 us (30%)
  blocking collectives  26 us (22%)
  waiting for transfers between devices  16.3 us (14%)
  other arithmetic  2.47 us (2%)
  between operations  1.48 us (1%)
    all_gather x1, blocking collectives, shards(): lax.all_gather(own_users(place, user_sums, user_gain), 'item', axis=0, ti...  13 us
    all_gather x1, blocking collectives, shards(): lax.all_gather(column_total, 'item', axis=0, tiled=True)  13 us
    pallas_call x1, Pallas kernels, sweep(): pl.pallas_call(functools.partial(sweep_kernel, user_prior / parts), in_sp...  12.1 us
    ppermute x7, starting transfers between devices, shards(): lax.ppermute(user_sums[k], 'item', [(j, (j + k) % columns) for j in range...  9.04 us
    all_to_all x1, starting transfers between devices, shards(): item_sums = lax.all_to_all(item_sums, 'user', 0, 0)  8.47 us
    all_to_all x1, starting transfers between devices, shards(): lax.all_to_all(head_of(touched, item_shape, item_rate), 'user', 0, 0)  8.44 us
    pallas_call x1, Pallas kernels, dense_counts(): pl.pallas_call(dense_kernel, in_specs=[IN_SMEM, IN_SMEM, IN_SMEM, IN_PLAC...  7.75 us
    all_to_all x1, waiting for transfers between devices, shards(): item_sums = lax.all_to_all(item_sums, 'user', 0, 0)  6.47 us
  transfers between devices with their start and end apart: 11, of which 7 were waited for; matrix products, arithmetic and copies ran while one was open for 2% of the time, Pallas kernels for 15%

profile of v5, /device:TPU:1, one launch (start us, length us, event | category | flops | bytes accessed | tf_op | source)
XLA Modules:
  0.0 116.8 jit_solution(3991833188884309778)
XLA Ops:
  0.6 2.1 %shard_map.120 = f32[16,1,384]{2,1,0:T(1,128)} custom-call(s32[2,16]{1,0:T(2,128)} %bitcast.9, f32[512,256]{1,0:T(8,128)} %shape_ref.3, f32[512,256]{1,0:T(8,128)} %rate_ref.3), custom_call_target="tpu_custom_call" | custom-call | flops 524288 | bytes 1048576 | tf_op jit(solution)/shard_map/pallas_call | solution.py:88
  2.7 8.4 %all-to-all-start = ((f32[16,1,384]{2,1,0:T(1,128)}), f32[16,1,384]{2,1,0:T(1,128)S(1)}, u32[]{:S(2)}, u32[]{:S(2)}) async-start(f32[16,1,384]{2,1,0:T(1,128)} %shard_map.120), calls=%async_computation | async-start | bytes 49152 | tf_op jit(solution)/shard_map/all_to_all | solution.py:605
  11.2 2.4 %shard_map.123 = (bf16[512,256]{1,0:T(8,128)(2,1)}, f32[512,1]{1,0:T(8,128)}) custom-call(f32[512,256]{1,0:T(8,128)} %shape_ref.3, f32[512,256]{1,0:T(8,128)} %rate_ref.3), custom_call_target="tpu_custom_call" | custom-call | flops 5242880 | bytes 1310720 | tf_op jit(solution)/shard_map/pallas_call | solution.py:117
  13.6 4.1 %all-to-all-done.head_ref.head_from = f32[16,1,384]{2,1,0:T(1,128)S(1)} async-done(((f32[16,1,384]{2,1,0:T(1,128)}), f32[16,1,384]{2,1,0:T(1,128)S(1)}, u32[]{:S(2)}, u32[]{:S(2)}) %all-to-all-start) | async-done | bytes 24608 | tf_op jit(solution)/shard_map/all_to_all | solution.py:605
  17.6 2.5 %shard_map.124 = bf16[16,256,256]{2,1,0:T(8,128)(2,1)} custom-call(s32[1]{0:T(128)} %bitcast.4.seat_ref, f32[16,1,384]{2,1,0:T(1,128)S(1)} %all-to-all-done.head_ref.head_from, bf16[4,128,256]{2,1,0:T(8,128)(2,1)} %bitcast.8), custom_call_target="tpu_custom_call" | custom-call | bytes 2359296 | tf_op jit(solution)/shard_map/pallas_call | solution.py:203
  20.1 0.0 copy-start.2
  20.1 0.0 copy-start.3
  20.1 3.7 %all-to-all-start.1 = ((bf16[16,256,256]{2,1,0:T(8,128)(2,1)}), bf16[16,256,256]{2,1,0:T(8,128)(2,1)S(1)}, u32[]{:S(2)}, u32[]{:S(2)}) async-start(bf16[16,256,256]{2,1,0:T(8,128)(2,1)} %shard_map.124), calls=%async_computation.1 | async-start | bytes 4194304 | tf_op jit(solution)/shard_map/all_to_all | solution.py:607
  24.5 4.3 %shard_map.121 = (bf16[1024,256]{1,0:T(8,128)(2,1)}, f32[1024,1]{1,0:T(8,128)}, bf16[256,1024]{1,0:T(8,128)(2,1)}, f32[1,256]{1,0:T(1,128)}) custom-call(f32[1024,256]{1,0:T(8,128)} %shape_ref.2, f32[1024,256]{1,0:T(8,128)} %rate_ref.2, f32[16,1,384]{2,1,0:T(1,128)S(1)} %all-to-all-done.head_ref.head_from), custom_call_target="tpu_custom_call" | custom-call | flops 10485760 | bytes 3145728 | tf_op jit(solution)/shard_map/pallas_call | solution.py:149
  28.8 13.0 %all-gather = f32[8,1,256]{2,1,0:T(1,128)S(1)} all-gather(f32[1,1,256]{2,1,0:T(1,128)} %bitcast.10), channel_id=1, replica_groups=mesh['user'=16,'item'=8] {'item'}, dimensions={0}, use_global_device_ids=true | all-gather | bytes 9216 | tf_op jit(solution)/shard_map/all_gather | solution.py:609
  41.8 0.0 copy-done.2
  41.8 7.8 %shard_map.122.dense_from = bf16[32,8,128,128]{3,2,1,0:T(8,128)(2,1)} custom-call(s32[256]{0:T(256)S(1)} %copy-done.2, s32[256]{0:T(256)S(1)} %copy-done.3, s32[1]{0:T(128)S(6)} %copy.13.live_ref, s32[256,128,128]{2,1,0:T(8,128)} %counts_ref.1, f32[1,256]{1,0:T(1,128)S(1)} %bitcast.6), custom_call_target="tpu_custom_call" | custom-call | flops 4194304 | bytes 25165824 | tf_op jit(solution)/shard_map/pallas_call | solution.py:280
  49.6 1.1 all-to-all-done.1.items_ref
  50.6 12.1 %shard_map.125 = (bf16[16,272,256]{2,1,0:T(8,128)(2,1)}, bf16[128,256]{1,0:T(8,128)(2,1)}, bf16[128,256]{1,0:T(8,128)(2,1)}, bf16[128,256]{1,0:T(8,128)(2,1)}, b...) custom-call(s32[1]{0:T(128)} %bitcast.place_ref, ...), custom_call_target="tpu_custom_call" | custom-call | flops 6442450944 | bytes 13631488 | tf_op jit(solution)/shard_map/pallas_call | solution.py:438
  62.7 0.0 copy-start.11
  62.7 0.0 copy-start.10
  62.7 0.0 copy-start.4
  62.8 0.0 copy-start.1
  62.8 8.5 %all-to-all-start.2 = ((bf16[16,272,256]{2,1,0:T(8,128)(2,1)}), bf16[16,272,256]{2,1,0:T(8,128)(2,1)S(1)}, u32[]{:S(2)}, u32[]{:S(2)}) async-start(bf16[16,272,256]{2,1,0:T(8,128)(2,1)} %get-tuple-element.34), calls=%async_computation.2 | async-start | bytes 4456448 | tf_op jit(solution)/shard_map/all_to_all | solution.py:616
  71.3 0.0 copy-done.11
  71.3 1.3 %collective-permute-start = (bf16[128,256]{1,0:T(8,128)(2,1)S(1)}, bf16[128,256]{1,0:T(8,128)(2,1)S(1)}, u32[]{:S(2)}, u32[]{:S(2)}) collective-permute-start(bf16[128,256]{1,0:T(8,128)(2,1)S(1)} %copy-done.11), channel_id=1, source_target_pairs={{0,1},{1,2},{2,3},{3,4},{4,5},{5,6},{6,7},{7,0},{8,9},{9,10},{10,1... | collective-permute-start | bytes 196616 | tf_op jit(solution)/shard_map/ppermute | solution.py:618
  72.6 1.3 %collective-permute-start.1 = (bf16[128,256]{1,0:T(8,128)(2,1)S(1)}, bf16[128,256]{1,0:T(8,128)(2,1)S(1)}, u32[]{:S(2)}, u32[]{:S(2)}) collective-permute-start(bf16[128,256]{1,0:T(8,128)(2,1)S(1)} %copy-done.10), channel_id=1, source_target_pairs={{0,2},{1,3},{2,4},{3,5},{4,6},{5,7},{6,0},{7,1},{8,10},{9,11},{10,... | collective-permute-start | bytes 196616 | tf_op jit(solution)/shard_map/ppermute | solution.py:618
  73.9 0.2 reduce.1
  74.1 1.8 %collective-permute-start.2 = (bf16[128,256]{1,0:T(8,128)(2,1)S(1)}, bf16[128,256]{1,0:T(8,128)(2,1)S(1)}, u32[]{:S(2)}, u32[]{:S(2)}) collective-permute-start(bf16[128,256]{1,0:T(8,128)(2,1)S(1)} %copy-done.9), channel_id=1, source_target_pairs={{0,3},{1,4},{2,5},{3,6},{4,7},{5,0},{6,1},{7,2},{8,11},{9,12},{10,... | collective-permute-start | bytes 196616 | tf_op jit(solution)/shard_map/ppermute | solution.py:618
  75.8 0.0 copy-done.8
  75.8 0.3 collective-permute-start.3
  76.2 2.2 %collective-permute-start.4 = (bf16[128,256]{1,0:T(8,128)(2,1)S(1)}, bf16[128,256]{1,0:T(8,128)(2,1)S(1)}, u32[]{:S(2)}, u32[]{:S(2)}) collective-permute-start(bf16[128,256]{1,0:T(8,128)(2,1)S(1)} %copy-done.7), channel_id=1, source_target_pairs={{0,5},{1,6},{2,7},{3,0},{4,1},{5,2},{6,3},{7,4},{8,13},{9,14},{10,... | collective-permute-start | bytes 196616 | tf_op jit(solution)/shard_map/ppermute | solution.py:618
  78.4 0.0 collective-permute-done.rest_1_
  78.4 0.5 collective-permute-start.5
  79.0 0.0 collective-permute-done.1.rest_2_
  79.0 0.0 copy-done.5
  79.0 1.6 %collective-permute-start.6 = (bf16[128,256]{1,0:T(8,128)(2,1)S(1)}, bf16[128,256]{1,0:T(8,128)(2,1)S(1)}, u32[]{:S(2)}, u32[]{:S(2)}) collective-permute-start(bf16[128,256]{1,0:T(8,128)(2,1)S(1)} %copy-done.5), channel_id=1, source_target_pairs={{0,7},{1,0},{2,1},{3,2},{4,3},{5,4},{6,5},{7,6},{8,15},{9,8},{10,9... | collective-permute-start | bytes 196616 | tf_op jit(solution)/shard_map/ppermute | solution.py:618
  80.6 1.2 %broadcast_add_fusion.rate_after_ref = f32[1024,256]{1,0:T(8,128)} fusion(f32[256]{0:T(256)S(1)} %reduce_sum.9, f32[1024]{0:T(1024)S(1)} %reduce.1), kind=kLoop, calls=%fused_computation.1 | loop fusion | flops 262144 | bytes 1053696 | tf_op jit(solution)/shard_map/add | solution.py:623
  81.7 0.0 collective-permute-done.2.rest_3_
  81.7 0.0 collective-permute-done.3.rest_4_
  81.8 0.4 collective-permute-done.4.rest_5_
  82.2 0.1 collective-permute-done.5.rest_6_
  82.3 1.5 %collective-permute-done.6.rest_7_ = bf16[128,256]{1,0:T(8,128)(2,1)S(1)} collective-permute-done((bf16[128,256]{1,0:T(8,128)(2,1)S(1)}, bf16[128,256]{1,0:T(8,128)(2,1)S(1)}, u32[]{:S(2)}, u32[]{:S(2)}) %collective-permute-start.6) | collective-permute-done | bytes 65568 | tf_op jit(solution)/shard_map/ppermute | solution.py:618
  83.8 0.0 copy-done.1
  83.8 1.6 %shard_map.126 = bf16[128,256]{1,0:T(8,128)(2,1)} custom-call(s32[1]{0:T(128)} %bitcast.place_ref, bf16[1024,256]{1,0:T(8,128)(2,1)} %get-tuple-element.21.gain_from.gain_ref, bf16[128,256]{1,0:T(8,128)(2,1)S(1)} %copy-done.1, bf16[128,256]{1,0:T(8,128)(2,1)S(1)} %collective-permute-done.rest_1_, bf16[128,256]{1,0:T(8,128)(2,1)S(1)} %collective-permute-done.1.rest_2_, ...), custom_call_target="tpu_custom_call" | custom-call | flops 524288 | bytes 524288 | tf_op jit(solution)/shard_map/pallas_call | solution.py:479
  85.4 13.0 %all_gather.7 = bf16[1024,256]{1,0:T(8,128)(2,1)S(1)} all-gather(bf16[128,256]{1,0:T(8,128)(2,1)} %shard_map.126), channel_id=1, replica_groups=mesh['user'=16,'item'=8] {'item'}, dimensions={0}, use_global_device_ids=true | all-gather | bytes 589824 | tf_op jit(solution)/shard_map/all_gather | solution.py:621
  98.4 1.1 convert_add_fusion.shape_after_ref
  99.4 6.5 %all-to-all-done.2.sums_ref = bf16[16,272,256]{2,1,0:T(8,128)(2,1)S(1)} async-done(((bf16[16,272,256]{2,1,0:T(8,128)(2,1)}), bf16[16,272,256]{2,1,0:T(8,128)(2,1)S(1)}, u32[]{:S(2)}, u32[]{:S(2)}) %all-to-all-start.2) | async-done | bytes 2228256 | tf_op jit(solution)/shard_map/all_to_all | solution.py:616
  105.9 0.6 shard_map.128
  106.6 4.7 %all-to-all-start.3 = ((f32[8,1,256]{2,1,0:T(1,128)}), f32[8,1,256]{2,1,0:T(1,128)S(1)}, u32[]{:S(2)}, u32[]{:S(2)}) async-start(f32[8,1,256]{2,1,0:T(1,128)} %shard_map.128), calls=%async_computation.3 | async-start | bytes 16384 | tf_op jit(solution)/shard_map/all_to_all | solution.py:624
  111.2 1.9 %shard_map.127 = (f32[512,256]{1,0:T(8,128)}, f32[512,256]{1,0:T(8,128)S(1)}) custom-call(s32[1]{0:T(128)} %bitcast.4.seat_ref, f32[16,1,384]{2,1,0:T(1,128)S(1)} %all-to-all-done.head_ref.head_from, bf16[16,272,256]{2,1,0:T(8,128)(2,1)S(1)} %all-to-all-done.2.sums_ref, bf16[512,256]{1,0:T(8,128)(2,1)} %get-tuple-element.23.gain_from), custom_call_target="tpu_custom_call" | custom-call | flops 5242880 | bytes 3538944 | tf_op jit(solution)/shard_map/pallas_call | solution.py:546
  113.2 2.7 %all-to-all-done.3.parts_ref = f32[8,1,256]{2,1,0:T(1,128)S(1)} async-done(((f32[8,1,256]{2,1,0:T(1,128)}), f32[8,1,256]{2,1,0:T(1,128)S(1)}, u32[]{:S(2)}, u32[]{:S(2)}) %all-to-all-start.3) | async-done | bytes 8224 | tf_op jit(solution)/shard_map/all_to_all | solution.py:624
  115.9 0.9 shard_map.129
  (14 shorter events, 0.1 us)
Async XLA Ops:
  2.7 14.9 %all-to-all-start = ((f32[16,1,384]{2,1,0:T(1,128)}), f32[16,1,384]{2,1,0:T(1,128)S(1)}, u32[]{:S(2)}, u32[]{:S(2)}) async-start(f32[16,1,384]{2,1,0:T(1,128)} %shard_map.120), calls=%async_computation | async-start | bytes 49152 | tf_op jit(solution)/shard_map/all_to_all | solution.py:605
  20.1 21.7 %copy-start.2 = (s32[256]{0:T(256)S(1)}, s32[256]{0:T(256)}, u32[]{:S(2)}) copy-start(s32[256]{0:T(256)} %user_of.1) | copy-start | bytes 3076
  20.1 21.7 %copy-start.3 = (s32[256]{0:T(256)S(1)}, s32[256]{0:T(256)}, u32[]{:S(2)}) copy-start(s32[256]{0:T(256)} %slot_of.1) | copy-start | bytes 3076
  20.1 30.5 %all-to-all-start.1 = ((bf16[16,256,256]{2,1,0:T(8,128)(2,1)}), bf16[16,256,256]{2,1,0:T(8,128)(2,1)S(1)}, u32[]{:S(2)}, u32[]{:S(2)}) async-start(bf16[16,256,256]{2,1,0:T(8,128)(2,1)} %shard_map.124), calls=%async_computation.1 | async-start | bytes 4194304 | tf_op jit(solution)/shard_map/all_to_all | solution.py:607
  62.7 8.6 %copy-start.11 = (bf16[128,256]{1,0:T(8,128)(2,1)S(1)}, bf16[128,256]{1,0:T(8,128)(2,1)}, u32[]{:S(2)}) copy-start(bf16[128,256]{1,0:T(8,128)(2,1)} %get-tuple-element.27) | copy-start | bytes 196612
  62.7 9.8 %copy-start.10 = (bf16[128,256]{1,0:T(8,128)(2,1)S(1)}, bf16[128,256]{1,0:T(8,128)(2,1)}, u32[]{:S(2)}) copy-start(bf16[128,256]{1,0:T(8,128)(2,1)} %get-tuple-element.28) | copy-start | bytes 196612
  62.7 11.1 %copy-start.4 = (f32[1024,1]{1,0:T(8,128)S(1)}, f32[1024,1]{1,0:T(8,128)}, u32[]{:S(2)}) copy-start(f32[1024,1]{1,0:T(8,128)} %get-tuple-element.25.level_from) | copy-start | bytes 12292
  62.7 11.3 %copy-start.9 = (bf16[128,256]{1,0:T(8,128)(2,1)S(1)}, bf16[128,256]{1,0:T(8,128)(2,1)}, u32[]{:S(2)}) copy-start(bf16[128,256]{1,0:T(8,128)(2,1)} %get-tuple-element.29) | copy-start | bytes 196612
  62.7 13.1 %copy-start.8 = (bf16[128,256]{1,0:T(8,128)(2,1)S(1)}, bf16[128,256]{1,0:T(8,128)(2,1)}, u32[]{:S(2)}) copy-start(bf16[128,256]{1,0:T(8,128)(2,1)} %get-tuple-element.30) | copy-start | bytes 196612
  62.8 13.4 %copy-start.7 = (bf16[128,256]{1,0:T(8,128)(2,1)S(1)}, bf16[128,256]{1,0:T(8,128)(2,1)}, u32[]{:S(2)}) copy-start(bf16[128,256]{1,0:T(8,128)(2,1)} %get-tuple-element.31) | copy-start | bytes 196612
  62.8 15.7 %copy-start.6 = (bf16[128,256]{1,0:T(8,128)(2,1)S(1)}, bf16[128,256]{1,0:T(8,128)(2,1)}, u32[]{:S(2)}) copy-start(bf16[128,256]{1,0:T(8,128)(2,1)} %get-tuple-element.32) | copy-start | bytes 196612
  62.8 16.2 %copy-start.5 = (bf16[128,256]{1,0:T(8,128)(2,1)S(1)}, bf16[128,256]{1,0:T(8,128)(2,1)}, u32[]{:S(2)}) copy-start(bf16[128,256]{1,0:T(8,128)(2,1)} %get-tuple-element.33) | copy-start | bytes 196612
  62.8 21.0 %copy-start.1 = (bf16[128,256]{1,0:T(8,128)(2,1)S(1)}, bf16[128,256]{1,0:T(8,128)(2,1)}, u32[]{:S(2)}) copy-start(bf16[128,256]{1,0:T(8,128)(2,1)} %get-tuple-element.26.rest_0_) | copy-start | bytes 196612
  62.8 43.1 %all-to-all-start.2 = ((bf16[16,272,256]{2,1,0:T(8,128)(2,1)}), bf16[16,272,256]{2,1,0:T(8,128)(2,1)S(1)}, u32[]{:S(2)}, u32[]{:S(2)}) async-start(bf16[16,272,256]{2,1,0:T(8,128)(2,1)} %get-tuple-element.34), calls=%async_computation.2 | async-start | bytes 4456448 | tf_op jit(solution)/shard_map/all_to_all | solution.py:616
  71.3 7.2 %collective-permute-start = (bf16[128,256]{1,0:T(8,128)(2,1)S(1)}, bf16[128,256]{1,0:T(8,128)(2,1)S(1)}, u32[]{:S(2)}, u32[]{:S(2)}) collective-permute-start(bf16[128,256]{1,0:T(8,128)(2,1)S(1)} %copy-done.11), channel_id=1, source_target_pairs={{0,1},{1,2},{2,3},{3,4},{4,5},{5,6},{6,7},{7,0},{8,9},{9,10},{10,1... | collective-permute-start | bytes 196616 | tf_op jit(solution)/shard_map/ppermute | solution.py:618
  72.6 6.4 %collective-permute-start.1 = (bf16[128,256]{1,0:T(8,128)(2,1)S(1)}, bf16[128,256]{1,0:T(8,128)(2,1)S(1)}, u32[]{:S(2)}, u32[]{:S(2)}) collective-permute-start(bf16[128,256]{1,0:T(8,128)(2,1)S(1)} %copy-done.10), channel_id=1, source_target_pairs={{0,2},{1,3},{2,4},{3,5},{4,6},{5,7},{6,0},{7,1},{8,10},{9,11},{10,... | collective-permute-start | bytes 196616 | tf_op jit(solution)/shard_map/ppermute | solution.py:618
  74.1 7.7 %collective-permute-start.2 = (bf16[128,256]{1,0:T(8,128)(2,1)S(1)}, bf16[128,256]{1,0:T(8,128)(2,1)S(1)}, u32[]{:S(2)}, u32[]{:S(2)}) collective-permute-start(bf16[128,256]{1,0:T(8,128)(2,1)S(1)} %copy-done.9), channel_id=1, source_target_pairs={{0,3},{1,4},{2,5},{3,6},{4,7},{5,0},{6,1},{7,2},{8,11},{9,12},{10,... | collective-permute-start | bytes 196616 | tf_op jit(solution)/shard_map/ppermute | solution.py:618
  75.8 5.9 %collective-permute-start.3 = (bf16[128,256]{1,0:T(8,128)(2,1)S(1)}, bf16[128,256]{1,0:T(8,128)(2,1)S(1)}, u32[]{:S(2)}, u32[]{:S(2)}) collective-permute-start(bf16[128,256]{1,0:T(8,128)(2,1)S(1)} %copy-done.8), channel_id=1, source_target_pairs={{0,4},{1,5},{2,6},{3,7},{4,0},{5,1},{6,2},{7,3},{8,12},{9,13},{10,... | collective-permute-start | bytes 196616 | tf_op jit(solution)/shard_map/ppermute | solution.py:618
  76.2 6.0 %collective-permute-start.4 = (bf16[128,256]{1,0:T(8,128)(2,1)S(1)}, bf16[128,256]{1,0:T(8,128)(2,1)S(1)}, u32[]{:S(2)}, u32[]{:S(2)}) collective-permute-start(bf16[128,256]{1,0:T(8,128)(2,1)S(1)} %copy-done.7), channel_id=1, source_target_pairs={{0,5},{1,6},{2,7},{3,0},{4,1},{5,2},{6,3},{7,4},{8,13},{9,14},{10,... | collective-permute-start | bytes 196616 | tf_op jit(solution)/shard_map/ppermute | solution.py:618
  78.4 3.9 %collective-permute-start.5 = (bf16[128,256]{1,0:T(8,128)(2,1)S(1)}, bf16[128,256]{1,0:T(8,128)(2,1)S(1)}, u32[]{:S(2)}, u32[]{:S(2)}) collective-permute-start(bf16[128,256]{1,0:T(8,128)(2,1)S(1)} %copy-done.6), channel_id=1, source_target_pairs={{0,6},{1,7},{2,0},{3,1},{4,2},{5,3},{6,4},{7,5},{8,14},{9,15},{10,... | collective-permute-start | bytes 196616 | tf_op jit(solution)/shard_map/ppermute | solution.py:618
  79.0 4.8 %collective-permute-start.6 = (bf16[128,256]{1,0:T(8,128)(2,1)S(1)}, bf16[128,256]{1,0:T(8,128)(2,1)S(1)}, u32[]{:S(2)}, u32[]{:S(2)}) collective-permute-start(bf16[128,256]{1,0:T(8,128)(2,1)S(1)} %copy-done.5), channel_id=1, source_target_pairs={{0,7},{1,0},{2,1},{3,2},{4,3},{5,4},{6,5},{7,6},{8,15},{9,8},{10,9... | collective-permute-start | bytes 196616 | tf_op jit(solution)/shard_map/ppermute | solution.py:618
  106.6 9.3 %copy-start = (f32[512,1]{1,0:T(8,128)S(1)}, f32[512,1]{1,0:T(8,128)}, u32[]{:S(2)}) copy-start(f32[512,1]{1,0:T(8,128)} %get-tuple-element.37.level_ref) | copy-start | bytes 6148
  106.6 9.3 %all-to-all-start.3 = ((f32[8,1,256]{2,1,0:T(1,128)}), f32[8,1,256]{2,1,0:T(1,128)S(1)}, u32[]{:S(2)}, u32[]{:S(2)}) async-start(f32[8,1,256]{2,1,0:T(1,128)} %shard_map.128), calls=%async_computation.3 | async-start | bytes 16384 | tf_op jit(solution)/shard_map/all_to_all | solution.py:624

commit v6 on v5

--- a/solution.py
+++ b/solution.py
@@ -16,7 +16,6 @@
 
 VMEM_BYTES = 24 << 20
 SWEEP_BYTES = 36 << 20
-EXTRA = 16
 LANES = 128
 IN_VMEM = pl.BlockSpec(memory_space=pltpu.VMEM)
 IN_SMEM = pl.BlockSpec(memory_space=pltpu.SMEM)
@@ -296,21 +295,12 @@
     )(tile_user, tile_slot, live_tiles, in_hbm(counts), after)
 
 
-def split_rows(value, rows):
-    high = value.astype(jnp.bfloat16).astype(jnp.float32)
-    middle = (value - high).astype(jnp.bfloat16).astype(jnp.float32)
-    low = value - high - middle
-    row = lax.broadcasted_iota(jnp.int32, (rows, value.shape[1]), 0)
-    block = jnp.where(row == 0, high, jnp.where(row == 1, middle, jnp.where(row == 2, low, 0.0)))
-    return block.astype(jnp.bfloat16)
-
-
 def sweep_kernel(
-    prior_share, place_ref, dense_from, items_ref, gain_from, turned_from, level_from, total_ref, item_ref, *rest
+    prior_share, place_ref, dense_from, items_ref, gain_from, turned_from, level_from, total_ref,
+    item_ref, kept_out, given_out, part_out,
+    dense_ref, gain_ref, turned_ref, level_ref, acc_ref, early_ref, late_ref, sums_ref, given_ref, part_ref,
+    arrived, sent,
 ):
-    user_outs, rest = rest[:-12], rest[-12:]
-    dense_ref, gain_ref, turned_ref, level_ref, acc_ref, early_ref, late_ref, sums_ref, extra_ref, users_ref = rest[:10]
-    arrived, sent = rest[10:]
     owners, touched_rows, factors = items_ref.shape
     slots, user_blocks, edge, _ = dense_ref.shape
     users = user_blocks * edge
@@ -404,25 +394,28 @@
 
     lax.fori_loop(0, (last + 1) // 2, turn, 0)
 
-    own = users // len(user_outs)
+    half = users // 2
+    step = half // 2
+    core = lax.rem(place_ref[0], 2)
     copies = []
-    for ahead, user_out in enumerate(user_outs):
-        target = (place_ref[0] + ahead) % len(user_outs)
-        rows = pl.ds(pl.multiple_of(target * own, own), own)
-        users_ref[ahead] = acc_ref[rows, :].astype(jnp.bfloat16)
-        copies.append(pltpu.make_async_copy(users_ref.at[ahead], user_out, sent.at[last + 2 + ahead]))
-        copies[-1].start()
+    for index in range(2):
+        kept = pl.ds(pl.multiple_of(core * half + index * step, step), step)
+        given = pl.ds(pl.multiple_of((1 - core) * half + index * step, step), step)
+        rows = pl.ds(index * step, step)
+        given_ref[rows, :] = acc_ref[given, :].astype(jnp.bfloat16)
+        copies.append(pltpu.make_async_copy(acc_ref.at[kept], kept_out.at[rows], sent.at[last + 1 + 2 * index]))
+        copies.append(pltpu.make_async_copy(given_ref.at[rows], given_out.at[rows], sent.at[last + 2 + 2 * index]))
+    for copy in copies:
+        copy.start()
     later_copies[1].wait()
     part = jnp.zeros((1, factors), jnp.float32)
-    for first in range(0, users, own):
-        rows = pl.ds(first, own)
+    for first in range(0, users, step):
+        rows = pl.ds(first, step)
         shape_share = prior_share + gain_ref[rows, :].astype(jnp.float32) * acc_ref[rows, :]
         inverse_rate = pl.reciprocal(level_ref[rows, :] + total_ref[...], approx=True)
         part += jnp.sum(shape_share * inverse_rate, axis=0, keepdims=True)
-    extra_ref[...] = jnp.broadcast_to(split_rows(part, EXTRA)[None], extra_ref.shape)
-    copies.append(
-        pltpu.make_async_copy(extra_ref, item_ref.at[:, pl.ds(touched_rows, EXTRA)], sent.at[last + 1])
-    )
+    part_ref[...] = part
+    copies.append(pltpu.make_async_copy(part_ref, part_out, sent.at[last + 5]))
     copies[-1].start()
     for index in range(last + 1):
         copy_of(index).wait()
@@ -430,15 +423,14 @@
         copy.wait()
 
 
-def sweep(place, dense, items, user_gain, turned_gain, user_level, item_total, parts):
+def sweep(place, dense, items, user_gain, turned_gain, user_level, item_total, columns):
     owners, touched_rows, factors = items.shape
     users = user_gain.shape[0]
-    own = users // parts
     pair = 2
-    out = pl.pallas_call(
-        functools.partial(sweep_kernel, user_prior / parts),
+    return pl.pallas_call(
+        functools.partial(sweep_kernel, user_prior / columns),
         in_specs=[IN_SMEM, IN_PLACE, IN_VMEM, IN_PLACE, IN_PLACE, IN_PLACE, IN_VMEM],
-        out_specs=[IN_PLACE] * (parts + 1),
+        out_specs=[IN_PLACE] * 4,
         scratch_shapes=[
             pltpu.VMEM(dense.shape, jnp.bfloat16),
             pltpu.VMEM((users, factors), jnp.bfloat16),
@@ -448,13 +440,17 @@
             pltpu.VMEM((users, pair * touched_rows), jnp.bfloat16),
             pltpu.VMEM((users, pair * touched_rows), jnp.bfloat16),
             pltpu.VMEM((owners, touched_rows, factors), jnp.bfloat16),
-            pltpu.VMEM((owners, EXTRA, factors), jnp.bfloat16),
-            pltpu.VMEM((parts, own, factors), jnp.bfloat16),
+            pltpu.VMEM((users // 2, factors), jnp.bfloat16),
+            pltpu.VMEM((1, factors), jnp.float32),
             pltpu.SemaphoreType.DMA((owners // pair + 4,)),
-            pltpu.SemaphoreType.DMA((owners // pair + 1 + parts,)),
-        ],
-        out_shape=[pltpu.HBM((owners, touched_rows + EXTRA, factors), jnp.bfloat16)]
-        + [pltpu.HBM((own, factors), jnp.bfloat16)] * parts,
+            pltpu.SemaphoreType.DMA((owners // pair + 5,)),
+        ],
+        out_shape=[
+            pltpu.HBM((owners, touched_rows, factors), jnp.bfloat16),
+            pltpu.HBM((users // 2, factors), jnp.float32),
+            pltpu.HBM((users // 2, factors), jnp.bfloat16),
+            pltpu.HBM((1, factors), jnp.float32),
+        ],
         compiler_params=pltpu.CompilerParams(vmem_limit_bytes=SWEEP_BYTES),
         cost_estimate=pl.CostEstimate(
             flops=6 * owners * touched_rows * users * factors,
@@ -462,134 +458,122 @@
             transcendentals=owners * touched_rows * users,
         ),
     )(place, in_hbm(dense), items, in_hbm(user_gain), in_hbm(turned_gain), in_hbm(user_level), item_total)
-    return out[0], out[1:]
-
-
-def own_kernel(place_ref, gain_ref, *rest):
-    sums_refs, sum_ref = rest[:-1], rest[-1]
-    sums = jnp.zeros(sum_ref.shape, jnp.float32)
-    for sums_ref in sums_refs:
-        sums += sums_ref[...].astype(jnp.float32)
-    sum_ref[...] = (gain_ref[...].astype(jnp.float32) * sums).astype(jnp.bfloat16)
-
-
-def own_users(place, sums, user_gain):
-    own, factors = sums[0].shape
-    first = lambda step, place_ref: (0, 0)
-    return pl.pallas_call(
-        own_kernel,
+
+
+def chip_kernel(kept_ref, got_ref, sum_ref):
+    sum_ref[...] = (kept_ref[...] + got_ref[...].astype(jnp.float32)).astype(jnp.bfloat16)
+
+
+def chip_sums(kept, got):
+    rows, factors = kept.shape
+    spec = pl.BlockSpec((rows // 2, factors), lambda r: (r, 0))
+    return pl.pallas_call(
+        chip_kernel,
+        grid=(2,),
+        in_specs=[spec, spec],
+        out_specs=spec,
+        out_shape=pltpu.HBM((rows, factors), jnp.bfloat16),
+        compiler_params=pltpu.CompilerParams(vmem_limit_bytes=VMEM_BYTES),
+        cost_estimate=pl.CostEstimate(flops=rows * factors, bytes_accessed=8 * rows * factors, transcendentals=0),
+    )(kept, got)
+
+
+def slab_kernel(place_ref, gain_ref, *rest):
+    sums_refs, shape_ref = rest[:-1], rest[-1]
+    parts = [ref[...].astype(jnp.float32) for ref in sums_refs]
+    while len(parts) > 1:
+        apart = len(parts) // 2
+        parts = [parts[k] + parts[k + apart] for k in range(apart)]
+    shape_ref[...] = user_prior + gain_ref[...].astype(jnp.float32) * parts[0]
+
+
+def slab_shapes(place, sums, user_gain):
+    rows, factors = sums[0].shape
+    spec = pl.BlockSpec((rows // 2, factors), lambda r, place_ref: (r, 0))
+    return pl.pallas_call(
+        slab_kernel,
         grid_spec=pltpu.PrefetchScalarGridSpec(
             num_scalar_prefetch=1,
-            grid=(1,),
-            in_specs=[pl.BlockSpec((own, factors), lambda step, place_ref: (place_ref[0], 0))]
-            + [pl.BlockSpec((own, factors), first)] * len(sums),
-            out_specs=pl.BlockSpec((own, factors), first),
-        ),
-        out_shape=pltpu.HBM((own, factors), jnp.bfloat16),
-        compiler_params=pltpu.CompilerParams(vmem_limit_bytes=VMEM_BYTES),
-        cost_estimate=pl.CostEstimate(
-            flops=2 * len(sums) * own * factors, bytes_accessed=2 * len(sums) * own * factors, transcendentals=0
+            grid=(2,),
+            in_specs=[pl.BlockSpec((rows // 2, factors), lambda r, place_ref: (lax.rem(place_ref[0], 2) * 2 + r, 0))]
+            + [spec] * len(sums),
+            out_specs=spec,
+        ),
+        out_shape=pltpu.HBM((rows, factors), jnp.float32),
+        compiler_params=pltpu.CompilerParams(vmem_limit_bytes=VMEM_BYTES),
+        cost_estimate=pl.CostEstimate(
+            flops=len(sums) * rows * factors, bytes_accessed=2 * (len(sums) + 3) * rows * factors, transcendentals=0
         ),
     )(place, in_hbm(user_gain), *sums)
 
 
-def fold_kernel(sums_ref, shape_after_ref, rate_after_ref, part_ref):
-    extra = sums_ref[0].astype(jnp.float32)
-    for sender in range(1, sums_ref.shape[0]):
-        extra += sums_ref[sender].astype(jnp.float32)
-    part_ref[...] = jnp.broadcast_to(jnp.sum(extra, axis=0).reshape(1, 1, -1), part_ref.shape)
-
-
-def fold(sums, copies, *after):
-    senders, extended, factors = sums.shape
-    return pl.pallas_call(
-        fold_kernel,
-        grid=(1,),
-        in_specs=[pl.BlockSpec((senders, EXTRA, factors), lambda step: (0, extended // EXTRA - 1, 0)), IN_PLACE, IN_PLACE],
-        out_specs=pl.BlockSpec((copies, 1, factors), lambda step: (0, 0, 0)),
-        out_shape=pltpu.HBM((copies, 1, factors), jnp.float32),
-        compiler_params=pltpu.CompilerParams(vmem_limit_bytes=VMEM_BYTES),
-        cost_estimate=pl.CostEstimate(flops=0, bytes_accessed=2 * senders * EXTRA * factors, transcendentals=0),
-    )(sums, *(in_hbm(array) for array in after))
-
-
-def shape_kernel(
-    per_owner, seat_ref, head_from, sums_ref, gain_from, shape_out, digamma_ref, table_ref, acc_ref, gain_ref, shape_ref,
-    arrived, sent,
+def item_kernel(
+    per_owner, seat_ref, head_from, sums_ref, gain_from, level_from, total_ref, shape_out, elog_out,
+    table_ref, acc_ref, gain_ref, level_ref, shape_ref, elog_ref, arrived, sent,
 ):
     blocks, edge, _ = acc_ref.shape
-    table = pltpu.make_async_copy(head_from.at[:, :, pl.ds(0, LANES)], table_ref, arrived.at[0])
-    gains = pltpu.make_async_copy(gain_from, gain_ref, arrived.at[1])
-    table.start()
-    gains.start()
+    fetches = [
+        pltpu.make_async_copy(source, target, arrived.at[place])
+        for place, (source, target) in enumerate(
+            ((head_from.at[:, :, pl.ds(0, LANES)], table_ref), (gain_from, gain_ref), (level_from, level_ref))
+        )
+    ]
+    for copy in fetches:
+        copy.start()
     acc_ref[...] = jnp.zeros_like(acc_ref)
-    table.wait()
+    fetches[0].wait()
     for sender in range(sums_ref.shape[0]):
         for place in range(per_owner):
             block = block_at(table_ref, sender, place, seat_ref[0])
             acc_ref[block] += sums_ref[sender, pl.ds(place * edge, edge), :].astype(jnp.float32)
-    gains.wait()
+    for copy in fetches[1:]:
+        copy.wait()
     copies = []
     for block in range(blocks):
         rows = pl.ds(block * edge, edge)
         shape_new = item_prior + gain_ref[rows, :].astype(jnp.float32) * acc_ref[block]
         shape_ref[rows, :] = shape_new
-        copies.append(pltpu.make_async_copy(shape_ref.at[rows], shape_out.at[rows], sent.at[block]))
-        copies[-1].start()
-        digamma_ref[rows, :] = digamma(shape_new)
+        elog_ref[rows, :] = digamma(shape_new) - jnp.log(level_ref[rows, :] + total_ref[...])
+        copies.append(pltpu.make_async_copy(shape_ref.at[rows], shape_out.at[rows], sent.at[2 * block]))
+        copies.append(pltpu.make_async_copy(elog_ref.at[rows], elog_out.at[rows], sent.at[2 * block + 1]))
+        for copy in copies[-2:]:
+            copy.start()
     for copy in copies:
         copy.wait()
 
 
-def item_shapes(seat, heads, sums, item_gain, edge, per_owner):
+def item_update(seat, heads, sums, item_gain, item_level, user_total, edge, per_owner):
     items, factors = item_gain.shape
     return pl.pallas_call(
-        functools.partial(shape_kernel, per_owner),
-        in_specs=[IN_SMEM, IN_PLACE, IN_VMEM, IN_PLACE],
-        out_specs=[IN_PLACE, IN_VMEM],
+        functools.partial(item_kernel, per_owner),
+        in_specs=[IN_SMEM, IN_PLACE, IN_VMEM, IN_PLACE, IN_PLACE, IN_VMEM],
+        out_specs=[IN_PLACE, IN_PLACE],
         scratch_shapes=[
             pltpu.SMEM((heads.shape[0], 1, LANES), jnp.float32),
             pltpu.VMEM((items // edge, edge, factors), jnp.float32),
             pltpu.VMEM((items, factors), jnp.bfloat16),
+            pltpu.VMEM((items, 1), jnp.float32),
             pltpu.VMEM((items, factors), jnp.float32),
-            pltpu.SemaphoreType.DMA((2,)),
-            pltpu.SemaphoreType.DMA((items // edge,)),
-        ],
-        out_shape=[pltpu.HBM((items, factors), jnp.float32), jax.ShapeDtypeStruct((items, factors), jnp.float32)],
+            pltpu.VMEM((items, factors), jnp.float32),
+            pltpu.SemaphoreType.DMA((3,)),
+            pltpu.SemaphoreType.DMA((2 * (items // edge),)),
+        ],
+        out_shape=[pltpu.HBM((items, factors), jnp.float32)] * 2,
         compiler_params=pltpu.CompilerParams(vmem_limit_bytes=VMEM_BYTES),
         cost_estimate=pl.CostEstimate(
             flops=40 * items * factors, bytes_accessed=2 * sums.size + 10 * items * factors,
-            transcendentals=3 * items * factors,
-        ),
-    )(seat, heads, sums, in_hbm(item_gain))
-
-
-def elog_kernel(digamma_ref, level_ref, parts_ref, elog_out, elog_ref, sent):
-    user_total = jnp.sum(parts_ref[...], axis=0)
-    step = elog_ref.shape[0] // sent.shape[0]
-    copies = []
-    for piece in range(sent.shape[0]):
-        rows = pl.ds(piece * step, step)
-        elog_ref[rows, :] = digamma_ref[rows, :] - jnp.log(level_ref[rows, :] + user_total)
-        copies.append(pltpu.make_async_copy(elog_ref.at[rows], elog_out.at[rows], sent.at[piece]))
-        copies[-1].start()
-    for copy in copies:
-        copy.wait()
-
-
-def item_elogs(digammas, item_level, user_parts):
-    items, factors = digammas.shape
-    return pl.pallas_call(
-        elog_kernel,
-        in_specs=[IN_VMEM, IN_VMEM, IN_VMEM],
-        out_specs=IN_PLACE,
-        scratch_shapes=[pltpu.VMEM((items, factors), jnp.float32), pltpu.SemaphoreType.DMA((4,))],
-        out_shape=pltpu.HBM((items, factors), jnp.float32),
-        compiler_params=pltpu.CompilerParams(vmem_limit_bytes=VMEM_BYTES),
-        cost_estimate=pl.CostEstimate(
-            flops=2 * items * factors, bytes_accessed=8 * items * factors, transcendentals=items * factors
-        ),
-    )(digammas, item_level, user_parts)
+            transcendentals=4 * items * factors,
+        ),
+    )(seat, heads, sums, in_hbm(item_gain), in_hbm(item_level), user_total)
+
+
+def ahead(array, axis, count):
+    size = lax.axis_size(axis)
+    return lax.ppermute(array, axis, [(j, (j + count) % size) for j in range(size)])
+
+
+def across(array, axis, bit):
+    return lax.ppermute(array, axis, [(j, j ^ bit) for j in range(lax.axis_size(axis))])
 
 
 def shards(
@@ -610,20 +594,27 @@
     dense = dense_counts(
         counts, tile_user, tile_slot, live_tiles, owners * per_owner, user_blocks, item_total
     )
-    item_sums, user_sums = sweep(
+    item_sums, kept, given, user_total = sweep(
         place, dense, item_rows, user_gain, turned_gain, user_level, item_total, columns
     )
     item_sums = lax.all_to_all(item_sums, "user", 0, 0)
-    user_sums = [user_sums[0]] + [
-        lax.ppermute(user_sums[k], "item", [(j, (j + k) % columns) for j in range(columns)])
-        for k in range(1, columns)
-    ]
-    user_sum = lax.all_gather(own_users(place, user_sums, user_gain), "item", axis=0, tiled=True)
-    user_shape_new = user_prior + user_sum.astype(jnp.float32)
+    user_total = jnp.sum(lax.all_gather(user_total, "item", axis=0, tiled=True), axis=0, keepdims=True)
+    bit = 1
+    while bit < owners:
+        user_total = user_total + across(user_total, "user", bit)
+        bit *= 2
+    chip = chip_sums(kept, across(given, "item", 1))
+    own_shapes = slab_shapes(place, [chip] + [ahead(chip, "item", count) for count in range(2, columns, 2)], user_gain)
+    other_shapes = across(own_shapes, "item", 1)
+    user_shape_new = jnp.where(
+        place[0] % 2 == 0,
+        jnp.concatenate([own_shapes, other_shapes], axis=0),
+        jnp.concatenate([other_shapes, own_shapes], axis=0),
+    )
     user_rate_new = user_level + item_total
-    user_parts = lax.all_to_all(fold(item_sums, columns, user_shape_new, user_rate_new), "item", 0, 0)
-    item_shape_new, digammas = item_shapes(seat, heads, item_sums, item_gain, edge, per_owner)
-    item_elog = item_elogs(digammas, item_level, user_parts)
+    item_shape_new, item_elog = item_update(
+        seat, heads, item_sums, item_gain, item_level, user_total, edge, per_owner
+    )
     return (user_shape_new, user_rate_new, item_shape_new, item_elog)
 
 

time: 116 us -> 125 us (1.078)
  the two profiles are of different devices: /device:TPU:1 before, /device:TPU:2 now
where the time goes in v6:
time: 125 us
  Pallas kernels  38.8 us (31%)
  starting transfers between devices  32.5 us (26%)
  waiting for transfers between devices  25.6 us (20%)
  blocking collectives  21.5 us (17%)
  other arithmetic  3.74 us (3%)
  between operations  1.43 us (1%)
    pallas_call x1, Pallas kernels, sweep(): pl.pallas_call(functools.partial(sweep_kernel, user_prior / columns), in_...  12 us
    all_gather x1, blocking collectives, shards(): lax.all_gather(column_total, 'item', axis=0, tiled=True)  11 us
    ppermute x3, waiting for transfers between devices, ahead(): lax.ppermute(array, axis, [(j, (j + count) % size) for j in range(size)])  11 us
    ppermute x6, waiting for transfers between devices, across(): lax.ppermute(array, axis, [(j, j ^ bit) for j in range(lax.axis_size(axis...  10.8 us
    pallas_call x1, Pallas kernels, dense_counts(): pl.pallas_call(dense_kernel, in_specs=[IN_SMEM, IN_SMEM, IN_SMEM, IN_PLAC...  10.5 us
    all_gather x1, blocking collectives, shards(): lax.all_gather(user_total, 'item', axis=0, tiled=True)  10.4 us
    all_to_all x1, starting transfers between devices, shards(): lax.all_to_all(head_of(touched, item_shape, item_rate), 'user', 0, 0)  8.33 us
    all_to_all x1, starting transfers between devices, shards(): item_sums = lax.all_to_all(item_sums, 'user', 0, 0)  7.43 us
  transfers between devices with their start and end apart: 12, of which 9 were waited for; matrix products, arithmetic and copies ran while one was open for 3% of the time, Pallas kernels for 16%

profile of v6, /device:TPU:2, one launch (start us, length us, event | category | flops | bytes accessed | tf_op | source)
XLA Modules:
  0.0 124.6 jit_solution(9951152523838431146)
XLA Ops:
  0.6 2.1 %shard_map.120 = f32[16,1,384]{2,1,0:T(1,128)} custom-call(s32[2,16]{1,0:T(2,128)} %bitcast.13, f32[512,256]{1,0:T(8,128)} %shape_ref.3, f32[512,256]{1,0:T(8,128)} %rate_ref.3), custom_call_target="tpu_custom_call" | custom-call | flops 524288 | bytes 1048576 | tf_op jit(solution)/shard_map/pallas_call | solution.py:87
  2.7 8.3 %all-to-all-start = ((f32[16,1,384]{2,1,0:T(1,128)}), f32[16,1,384]{2,1,0:T(1,128)S(1)}, u32[]{:S(2)}, u32[]{:S(2)}) async-start(f32[16,1,384]{2,1,0:T(1,128)} %shard_map.120), calls=%async_computation | async-start | bytes 49152 | tf_op jit(solution)/shard_map/all_to_all | solution.py:589
  11.1 2.4 %shard_map.123 = (bf16[512,256]{1,0:T(8,128)(2,1)}, f32[512,1]{1,0:T(8,128)}) custom-call(f32[512,256]{1,0:T(8,128)} %shape_ref.3, f32[512,256]{1,0:T(8,128)} %rate_ref.3), custom_call_target="tpu_custom_call" | custom-call | flops 5242880 | bytes 1310720 | tf_op jit(solution)/shard_map/pallas_call | solution.py:116
  13.4 3.8 %all-to-all-done.head_ref.head_from = f32[16,1,384]{2,1,0:T(1,128)S(1)} async-done(((f32[16,1,384]{2,1,0:T(1,128)}), f32[16,1,384]{2,1,0:T(1,128)S(1)}, u32[]{:S(2)}, u32[]{:S(2)}) %all-to-all-start) | async-done | bytes 24608 | tf_op jit(solution)/shard_map/all_to_all | solution.py:589
  17.3 2.4 %shard_map.124 = bf16[16,256,256]{2,1,0:T(8,128)(2,1)} custom-call(s32[1]{0:T(128)} %bitcast.4.seat_ref, f32[16,1,384]{2,1,0:T(1,128)S(1)} %all-to-all-done.head_ref.head_from, bf16[4,128,256]{2,1,0:T(8,128)(2,1)} %bitcast.10), custom_call_target="tpu_custom_call" | custom-call | bytes 2359296 | tf_op jit(solution)/shard_map/pallas_call | solution.py:202
  19.7 5.0 %all-to-all-start.1 = ((bf16[16,256,256]{2,1,0:T(8,128)(2,1)}), bf16[16,256,256]{2,1,0:T(8,128)(2,1)S(1)}, u32[]{:S(2)}, u32[]{:S(2)}) async-start(bf16[16,256,256]{2,1,0:T(8,128)(2,1)} %shard_map.124), calls=%async_computation.1 | async-start | bytes 4194304 | tf_op jit(solution)/shard_map/all_to_all | solution.py:591
  24.7 0.0 copy-start.3
  25.4 4.3 %shard_map.121 = (bf16[1024,256]{1,0:T(8,128)(2,1)}, f32[1024,1]{1,0:T(8,128)}, bf16[256,1024]{1,0:T(8,128)(2,1)}, f32[1,256]{1,0:T(1,128)}) custom-call(f32[1024,256]{1,0:T(8,128)} %shape_ref.2, f32[1024,256]{1,0:T(8,128)} %rate_ref.2, f32[16,1,384]{2,1,0:T(1,128)S(1)} %all-to-all-done.head_ref.head_from), custom_call_target="tpu_custom_call" | custom-call | flops 10485760 | bytes 3145728 | tf_op jit(solution)/shard_map/pallas_call | solution.py:148
  29.7 11.0 %all-gather = f32[8,1,256]{2,1,0:T(1,128)S(1)} all-gather(f32[1,1,256]{2,1,0:T(1,128)} %bitcast.15), channel_id=1, replica_groups=mesh['user'=16,'item'=8] {'item'}, dimensions={0}, use_global_device_ids=true | all-gather | bytes 9216 | tf_op jit(solution)/shard_map/all_gather | solution.py:593
  40.8 0.0 copy-done.2
  40.8 0.0 copy-done.3
  40.8 10.5 %shard_map.122.dense_from = bf16[32,8,128,128]{3,2,1,0:T(8,128)(2,1)} custom-call(s32[256]{0:T(256)S(1)} %copy-done.2, s32[256]{0:T(256)S(1)} %copy-done.3, s32[1]{0:T(128)S(6)} %copy.13.live_ref, s32[256,128,128]{2,1,0:T(8,128)} %counts_ref.1, f32[1,256]{1,0:T(1,128)S(1)} %bitcast.8), custom_call_target="tpu_custom_call" | custom-call | flops 4194304 | bytes 25165824 | tf_op jit(solution)/shard_map/pallas_call | solution.py:279
  51.3 0.0 all-to-all-done.1.items_ref
  51.3 12.0 %shard_map.125 = (bf16[16,256,256]{2,1,0:T(8,128)(2,1)}, f32[512,256]{1,0:T(8,128)}, bf16[512,256]{1,0:T(8,128)(2,1)}, f32[1,256]{1,0:T(1,128)}) custom-call(s32[1]{0:T(128)} %bitcast.place_ref, bf16[32,8,128,128]{3,2,1,0:T(8,128)(2,1)} %shard_map.122.dense_from, bf16[16,256,256]{2,1,0:T(8,128)(2,1)S(1)} %all-to-all-done.1.items_ref, ...), custom_call_target="tpu_custom_call" | custom-call | flops 6442450944 | bytes 13631488 | tf_op jit(solution)/shard_map/pallas_call | solution.py:430
  63.4 0.0 copy-start.6
  63.4 0.0 copy-start.1
  63.4 7.4 %all-to-all-start.2 = ((bf16[16,256,256]{2,1,0:T(8,128)(2,1)}), bf16[16,256,256]{2,1,0:T(8,128)(2,1)S(1)}, u32[]{:S(2)}, u32[]{:S(2)}) async-start(bf16[16,256,256]{2,1,0:T(8,128)(2,1)} %get-tuple-element.23), calls=%async_computation.2 | async-start | bytes 4194304 | tf_op jit(solution)/shard_map/all_to_all | solution.py:600
  70.8 0.0 copy-start.4
  70.8 0.0 copy-done.6
  70.8 0.1 collective-permute-start
  70.9 1.5 %collective-permute-done.got_ref = bf16[512,256]{1,0:T(8,128)(2,1)S(1)} collective-permute-done((bf16[512,256]{1,0:T(8,128)(2,1)S(1)}, bf16[512,256]{1,0:T(8,128)(2,1)S(1)}, u32[]{:S(2)}, u32[]{:S(2)}) %collective-permute-start) | collective-permute-done | bytes 262176 | tf_op jit(solution)/shard_map/ppermute | solution.py:576
  72.4 0.0 copy-done.1
  72.5 0.7 shard_map.126.rest_0_
  73.2 0.8 collective-permute-start.1
  74.0 2.9 %collective-permute-start.2 = (bf16[512,256]{1,0:T(8,128)(2,1)}, bf16[512,256]{1,0:T(8,128)(2,1)S(1)}, u32[]{:S(2)}, u32[]{:S(2)}) collective-permute-start(bf16[512,256]{1,0:T(8,128)(2,1)} %shard_map.126.rest_0_), channel_id=1, source_target_pairs={{0,4},{1,5},{2,6},{3,7},{4,0},{5,1},{6,2},{7,3},{8,12},{9,13},{10,... | collective-permute-start | bytes 786440 | tf_op jit(solution)/shard_map/ppermute | solution.py:572
  76.9 1.3 %collective-permute-start.3 = (bf16[512,256]{1,0:T(8,128)(2,1)}, bf16[512,256]{1,0:T(8,128)(2,1)S(1)}, u32[]{:S(2)}, u32[]{:S(2)}) collective-permute-start(bf16[512,256]{1,0:T(8,128)(2,1)} %shard_map.126.rest_0_), channel_id=1, source_target_pairs={{0,6},{1,7},{2,0},{3,1},{4,2},{5,3},{6,4},{7,5},{8,14},{9,15},{10,... | collective-permute-start | bytes 786440 | tf_op jit(solution)/shard_map/ppermute | solution.py:572
  78.2 5.1 %collective-permute-done.1.rest_1_ = bf16[512,256]{1,0:T(8,128)(2,1)S(1)} collective-permute-done((bf16[512,256]{1,0:T(8,128)(2,1)}, bf16[512,256]{1,0:T(8,128)(2,1)S(1)}, u32[]{:S(2)}, u32[]{:S(2)}) %collective-permute-start.1) | collective-permute-done | bytes 262176 | tf_op jit(solution)/shard_map/ppermute | solution.py:572
  83.3 5.7 %collective-permute-done.2.rest_2_ = bf16[512,256]{1,0:T(8,128)(2,1)S(1)} collective-permute-done((bf16[512,256]{1,0:T(8,128)(2,1)}, bf16[512,256]{1,0:T(8,128)(2,1)S(1)}, u32[]{:S(2)}, u32[]{:S(2)}) %collective-permute-start.2) | collective-permute-done | bytes 262176 | tf_op jit(solution)/shard_map/ppermute | solution.py:572
  89.0 0.2 collective-permute-done.3.rest_3_
  89.2 0.9 copy-done
  90.1 1.8 %shard_map.127 = f32[512,256]{1,0:T(8,128)} custom-call(s32[1]{0:T(128)} %bitcast.place_ref, bf16[1024,256]{1,0:T(8,128)(2,1)} %get-tuple-element.16.gain_from.gain_ref, bf16[512,256]{1,0:T(8,128)(2,1)S(1)} %copy-done, bf16[512,256]{1,0:T(8,128)(2,1)S(1)} %collective-permute-done.1.rest_1_, bf16[512,256]{1,0:T(8,128)(2,1)S(1)} %collective-permute-done.2.rest_2_, ...), custom_call_target="tpu_custom_call" | custom-call | flops 524288 | bytes 1835008 | tf_op jit(solution)/shard_map/pallas_call | solution.py:493
  92.0 0.0 collective-permute-start.4
  92.0 0.0 copy-done.5
  92.0 10.4 %all-gather.1 = f32[8,1,256]{2,1,0:T(1,128)S(1)} all-gather(f32[1,1,256]{2,1,0:T(1,128)S(1)} %bitcast.14), channel_id=1, replica_groups=mesh['user'=16,'item'=8] {'item'}, dimensions={0}, use_global_device_ids=true | all-gather | bytes 9216 | tf_op jit(solution)/shard_map/all_gather | solution.py:601
  102.4 0.2 collective-permute-start.5
  102.6 3.5 %collective-permute-done.5 = f32[1,256]{1,0:T(1,128)S(1)} collective-permute-done((f32[1,256]{1,0:T(1,128)S(1)}, f32[1,256]{1,0:T(1,128)S(1)}, u32[]{:S(2)}, u32[]{:S(2)}) %collective-permute-start.5) | collective-permute-done | bytes 1056 | tf_op jit(solution)/shard_map/ppermute | solution.py:576
  106.1 2.1 %collective-permute-start.6 = (f32[1,256]{1,0:T(1,128)S(1)}, f32[1,256]{1,0:T(1,128)S(1)}, u32[]{:S(2)}, u32[]{:S(2)}) collective-permute-start(f32[1,256]{1,0:T(1,128)S(1)} %add.36), channel_id=1, source_target_pairs={{0,16},{8,24},{16,0},{24,8},{32,48},{40,56},{48,32},{56,40},{64,80... | collective-permute-start | bytes 3080 | tf_op jit(solution)/shard_map/ppermute | solution.py:576
  108.1 3.0 %collective-permute-done.6 = f32[1,256]{1,0:T(1,128)S(1)} collective-permute-done((f32[1,256]{1,0:T(1,128)S(1)}, f32[1,256]{1,0:T(1,128)S(1)}, u32[]{:S(2)}, u32[]{:S(2)}) %collective-permute-start.6) | collective-permute-done | bytes 1056 | tf_op jit(solution)/shard_map/ppermute | solution.py:576
  111.1 1.5 %collective-permute-start.7 = (f32[1,256]{1,0:T(1,128)S(1)}, f32[1,256]{1,0:T(1,128)S(1)}, u32[]{:S(2)}, u32[]{:S(2)}) collective-permute-start(f32[1,256]{1,0:T(1,128)S(1)} %add.37), channel_id=1, source_target_pairs={{0,32},{8,40},{16,48},{24,56},{32,0},{40,8},{48,16},{56,24},{64,96... | collective-permute-start | bytes 3080 | tf_op jit(solution)/shard_map/ppermute | solution.py:576
  112.6 0.2 reduce.2
  112.8 1.9 %collective-permute-done.7 = f32[1,256]{1,0:T(1,128)S(1)} collective-permute-done((f32[1,256]{1,0:T(1,128)S(1)}, f32[1,256]{1,0:T(1,128)S(1)}, u32[]{:S(2)}, u32[]{:S(2)}) %collective-permute-start.7) | collective-permute-done | bytes 1056 | tf_op jit(solution)/shard_map/ppermute | solution.py:576
  114.7 3.0 %collective-permute-start.8 = (f32[1,256]{1,0:T(1,128)S(1)}, f32[1,256]{1,0:T(1,128)S(1)}, u32[]{:S(2)}, u32[]{:S(2)}) collective-permute-start(f32[1,256]{1,0:T(1,128)S(1)} %add.38), channel_id=1, source_target_pairs={{0,64},{8,72},{16,80},{24,88},{32,96},{40,104},{48,112},{56,120},{... | collective-permute-start | bytes 3080 | tf_op jit(solution)/shard_map/ppermute | solution.py:576
  117.7 1.2 broadcast_add_fusion
  118.9 0.9 collective-permute-done.8
  119.8 0.0 collective-permute-done.4
  119.8 2.3 %maximum_select_fusion = f32[1024,256]{1,0:T(8,128)} fusion(f32[512,256]{1,0:T(8,128)S(1)} %collective-permute-done.4, f32[512,256]{1,0:T(8,128)} %shard_map.127, pred[]{:T(512)S(6)} %eq.5), kind=kLoop, calls=%fused_computation | loop fusion | flops 786432 | bytes 2097153 | tf_op jit(solution)/shard_map/jit(_where)/select_n | solution.py:609
  122.1 0.0 all-to-all-done.2.sums_ref
  122.1 2.5 %shard_map.128 = (f32[512,256]{1,0:T(8,128)}, f32[512,256]{1,0:T(8,128)}) custom-call(s32[1]{0:T(128)} %bitcast.4.seat_ref, f32[16,1,384]{2,1,0:T(1,128)S(1)} %all-to-all-done.head_ref.head_from, bf16[16,256,256]{2,1,0:T(8,128)(2,1)S(1)} %all-to-all-done.2.sums_ref, bf16[512,256]{1,0:T(8,128)(2,1)} %get-tuple-element.18.gain_from, ...), custom_call_target="tpu_custom_call" | custom-call | flops 5242880 | bytes 3407872 | tf_op jit(solution)/shard_map/pallas_call | solution.py:547
  (10 shorter events, 0.1 us)
Async XLA Ops:
  2.7 14.6 %all-to-all-start = ((f32[16,1,384]{2,1,0:T(1,128)}), f32[16,1,384]{2,1,0:T(1,128)S(1)}, u32[]{:S(2)}, u32[]{:S(2)}) async-start(f32[16,1,384]{2,1,0:T(1,128)} %shard_map.120), calls=%async_computation | async-start | bytes 49152 | tf_op jit(solution)/shard_map/all_to_all | solution.py:589
  19.7 31.6 %all-to-all-start.1 = ((bf16[16,256,256]{2,1,0:T(8,128)(2,1)}), bf16[16,256,256]{2,1,0:T(8,128)(2,1)S(1)}, u32[]{:S(2)}, u32[]{:S(2)}) async-start(bf16[16,256,256]{2,1,0:T(8,128)(2,1)} %shard_map.124), calls=%async_computation.1 | async-start | bytes 4194304 | tf_op jit(solution)/shard_map/all_to_all | solution.py:591
  24.7 16.1 %copy-start.2 = (s32[256]{0:T(256)S(1)}, s32[256]{0:T(256)}, u32[]{:S(2)}) copy-start(s32[256]{0:T(256)} %user_of.1) | copy-start | bytes 3076
  24.7 16.1 %copy-start.3 = (s32[256]{0:T(256)S(1)}, s32[256]{0:T(256)}, u32[]{:S(2)}) copy-start(s32[256]{0:T(256)} %slot_of.1) | copy-start | bytes 3076
  63.4 7.5 %copy-start.6 = (bf16[512,256]{1,0:T(8,128)(2,1)S(1)}, bf16[512,256]{1,0:T(8,128)(2,1)}, u32[]{:S(2)}) copy-start(bf16[512,256]{1,0:T(8,128)(2,1)} %get-tuple-element.22) | copy-start | bytes 786436
  63.4 9.1 %copy-start.1 = (f32[512,256]{1,0:T(8,128)S(1)}, f32[512,256]{1,0:T(8,128)}, u32[]{:S(2)}) copy-start(f32[512,256]{1,0:T(8,128)} %get-tuple-element.21.kept_ref) | copy-start | bytes 1572868
  63.4 58.7 %all-to-all-start.2 = ((bf16[16,256,256]{2,1,0:T(8,128)(2,1)}), bf16[16,256,256]{2,1,0:T(8,128)(2,1)S(1)}, u32[]{:S(2)}, u32[]{:S(2)}) async-start(bf16[16,256,256]{2,1,0:T(8,128)(2,1)} %get-tuple-element.23), calls=%async_computation.2 | async-start | bytes 4194304 | tf_op jit(solution)/shard_map/all_to_all | solution.py:600
  70.8 21.2 %copy-start.5 = (f32[1,256]{1,0:T(1,128)S(1)}, f32[1,256]{1,0:T(1,128)}, u32[]{:S(2)}) copy-start(f32[1,256]{1,0:T(1,128)} %get-tuple-element.25) | copy-start | bytes 3076
  70.8 41.8 %copy-start.4 = (f32[1024,1]{1,0:T(8,128)S(1)}, f32[1024,1]{1,0:T(8,128)}, u32[]{:S(2)}) copy-start(f32[1024,1]{1,0:T(8,128)} %get-tuple-element.20.level_from) | copy-start | bytes 12292
  70.8 1.6 %collective-permute-start = (bf16[512,256]{1,0:T(8,128)(2,1)S(1)}, bf16[512,256]{1,0:T(8,128)(2,1)S(1)}, u32[]{:S(2)}, u32[]{:S(2)}) collective-permute-start(bf16[512,256]{1,0:T(8,128)(2,1)S(1)} %copy-done.6), channel_id=1, source_target_pairs={{0,1},{1,0},{2,3},{3,2},{4,5},{5,4},{6,7},{7,6},{8,9},{9,8},{10,11... | collective-permute-start | bytes 786440 | tf_op jit(solution)/shard_map/ppermute | solution.py:576
  73.2 10.1 %collective-permute-start.1 = (bf16[512,256]{1,0:T(8,128)(2,1)}, bf16[512,256]{1,0:T(8,128)(2,1)S(1)}, u32[]{:S(2)}, u32[]{:S(2)}) collective-permute-start(bf16[512,256]{1,0:T(8,128)(2,1)} %shard_map.126.rest_0_), channel_id=1, source_target_pairs={{0,2},{1,3},{2,4},{3,5},{4,6},{5,7},{6,0},{7,1},{8,10},{9,11},{10,... | collective-permute-start | bytes 786440 | tf_op jit(solution)/shard_map/ppermute | solution.py:572
  74.0 15.1 %collective-permute-start.2 = (bf16[512,256]{1,0:T(8,128)(2,1)}, bf16[512,256]{1,0:T(8,128)(2,1)S(1)}, u32[]{:S(2)}, u32[]{:S(2)}) collective-permute-start(bf16[512,256]{1,0:T(8,128)(2,1)} %shard_map.126.rest_0_), channel_id=1, source_target_pairs={{0,4},{1,5},{2,6},{3,7},{4,0},{5,1},{6,2},{7,3},{8,12},{9,13},{10,... | collective-permute-start | bytes 786440 | tf_op jit(solution)/shard_map/ppermute | solution.py:572
  76.9 12.3 %collective-permute-start.3 = (bf16[512,256]{1,0:T(8,128)(2,1)}, bf16[512,256]{1,0:T(8,128)(2,1)S(1)}, u32[]{:S(2)}, u32[]{:S(2)}) collective-permute-start(bf16[512,256]{1,0:T(8,128)(2,1)} %shard_map.126.rest_0_), channel_id=1, source_target_pairs={{0,6},{1,7},{2,0},{3,1},{4,2},{5,3},{6,4},{7,5},{8,14},{9,15},{10,... | collective-permute-start | bytes 786440 | tf_op jit(solution)/shard_map/ppermute | solution.py:572
  89.2 1.0 copy-start
  92.0 27.8 %collective-permute-start.4 = (f32[512,256]{1,0:T(8,128)}, f32[512,256]{1,0:T(8,128)S(1)}, u32[]{:S(2)}, u32[]{:S(2)}) collective-permute-start(f32[512,256]{1,0:T(8,128)} %shard_map.127), channel_id=1, source_target_pairs={{0,1},{1,0},{2,3},{3,2},{4,5},{5,4},{6,7},{7,6},{8,9},{9,8},{10,11... | collective-permute-start | bytes 1572872 | tf_op jit(solution)/shard_map/ppermute | solution.py:576
  102.4 3.6 %collective-permute-start.5 = (f32[1,256]{1,0:T(1,128)S(1)}, f32[1,256]{1,0:T(1,128)S(1)}, u32[]{:S(2)}, u32[]{:S(2)}) collective-permute-start(f32[1,256]{1,0:T(1,128)S(1)} %bitcast.11), channel_id=1, source_target_pairs={{0,8},{8,0},{16,24},{24,16},{32,40},{40,32},{48,56},{56,48},{64,72... | collective-permute-start | bytes 3080 | tf_op jit(solution)/shard_map/ppermute | solution.py:576
  106.1 5.1 %collective-permute-start.6 = (f32[1,256]{1,0:T(1,128)S(1)}, f32[1,256]{1,0:T(1,128)S(1)}, u32[]{:S(2)}, u32[]{:S(2)}) collective-permute-start(f32[1,256]{1,0:T(1,128)S(1)} %add.36), channel_id=1, source_target_pairs={{0,16},{8,24},{16,0},{24,8},{32,48},{40,56},{48,32},{56,40},{64,80... | collective-permute-start | bytes 3080 | tf_op jit(solution)/shard_map/ppermute | solution.py:576
  111.1 3.6 %collective-permute-start.7 = (f32[1,256]{1,0:T(1,128)S(1)}, f32[1,256]{1,0:T(1,128)S(1)}, u32[]{:S(2)}, u32[]{:S(2)}) collective-permute-start(f32[1,256]{1,0:T(1,128)S(1)} %add.37), channel_id=1, source_target_pairs={{0,32},{8,40},{16,48},{24,56},{32,0},{40,8},{48,16},{56,24},{64,96... | collective-permute-start | bytes 3080 | tf_op jit(solution)/shard_map/ppermute | solution.py:576
  114.7 5.1 %collective-permute-start.8 = (f32[1,256]{1,0:T(1,128)S(1)}, f32[1,256]{1,0:T(1,128)S(1)}, u32[]{:S(2)}, u32[]{:S(2)}) collective-permute-start(f32[1,256]{1,0:T(1,128)S(1)} %add.38), channel_id=1, source_target_pairs={{0,64},{8,72},{16,80},{24,88},{32,96},{40,104},{48,112},{56,120},{... | collective-permute-start | bytes 3080 | tf_op jit(solution)/shard_map/ppermute | solution.py:576

commit v7 on v6

--- a/solution.py
+++ b/solution.py
@@ -284,7 +284,7 @@
             pltpu.VMEM((slot_count, user_blocks, edge, edge), jnp.bfloat16),
             pltpu.VMEM((depth, group, edge, edge), jnp.int32),
             pltpu.SemaphoreType.DMA((depth,)),
-            pltpu.SemaphoreType.DMA((16,)),
+            pltpu.SemaphoreType.DMA((min(16, slot_count),)),
         ],
         out_shape=pltpu.HBM((slot_count, user_blocks, edge, edge), jnp.bfloat16),
         compiler_params=pltpu.CompilerParams(vmem_limit_bytes=VMEM_BYTES),
@@ -478,7 +478,7 @@
     )(kept, got)
 
 
-def slab_kernel(place_ref, gain_ref, *rest):
+def slab_kernel(place_ref, after_ref, gain_ref, *rest):
     sums_refs, shape_ref = rest[:-1], rest[-1]
     parts = [ref[...].astype(jnp.float32) for ref in sums_refs]
     while len(parts) > 1:
@@ -487,7 +487,7 @@
     shape_ref[...] = user_prior + gain_ref[...].astype(jnp.float32) * parts[0]
 
 
-def slab_shapes(place, sums, user_gain):
+def slab_shapes(place, sums, user_gain, after):
     rows, factors = sums[0].shape
     spec = pl.BlockSpec((rows // 2, factors), lambda r, place_ref: (r, 0))
     return pl.pallas_call(
@@ -495,7 +495,10 @@
         grid_spec=pltpu.PrefetchScalarGridSpec(
             num_scalar_prefetch=1,
             grid=(2,),
-            in_specs=[pl.BlockSpec((rows // 2, factors), lambda r, place_ref: (lax.rem(place_ref[0], 2) * 2 + r, 0))]
+            in_specs=[
+                IN_PLACE,
+                pl.BlockSpec((rows // 2, factors), lambda r, place_ref: (lax.rem(place_ref[0], 2) * 2 + r, 0)),
+            ]
             + [spec] * len(sums),
             out_specs=spec,
         ),
@@ -504,11 +507,11 @@
         cost_estimate=pl.CostEstimate(
             flops=len(sums) * rows * factors, bytes_accessed=2 * (len(sums) + 3) * rows * factors, transcendentals=0
         ),
-    )(place, in_hbm(user_gain), *sums)
+    )(place, after, in_hbm(user_gain), in_hbm(sums[0]), *sums[1:])
 
 
 def item_kernel(
-    per_owner, seat_ref, head_from, sums_ref, gain_from, level_from, total_ref, shape_out, elog_out,
+    per_owner, seat_ref, head_from, sums_ref, gain_from, level_from, near_ref, far_ref, shape_out, elog_out,
     table_ref, acc_ref, gain_ref, level_ref, shape_ref, elog_ref, arrived, sent,
 ):
     blocks, edge, _ = acc_ref.shape
@@ -528,12 +531,13 @@
             acc_ref[block] += sums_ref[sender, pl.ds(place * edge, edge), :].astype(jnp.float32)
     for copy in fetches[1:]:
         copy.wait()
+    user_total = near_ref[...] + far_ref[...]
     copies = []
     for block in range(blocks):
         rows = pl.ds(block * edge, edge)
         shape_new = item_prior + gain_ref[rows, :].astype(jnp.float32) * acc_ref[block]
         shape_ref[rows, :] = shape_new
-        elog_ref[rows, :] = digamma(shape_new) - jnp.log(level_ref[rows, :] + total_ref[...])
+        elog_ref[rows, :] = digamma(shape_new) - jnp.log(level_ref[rows, :] + user_total)
         copies.append(pltpu.make_async_copy(shape_ref.at[rows], shape_out.at[rows], sent.at[2 * block]))
         copies.append(pltpu.make_async_copy(elog_ref.at[rows], elog_out.at[rows], sent.at[2 * block + 1]))
         for copy in copies[-2:]:
@@ -542,11 +546,11 @@
         copy.wait()
 
 
-def item_update(seat, heads, sums, item_gain, item_level, user_total, edge, per_owner):
+def item_update(seat, heads, sums, item_gain, item_level, near, far, edge, per_owner):
     items, factors = item_gain.shape
     return pl.pallas_call(
         functools.partial(item_kernel, per_owner),
-        in_specs=[IN_SMEM, IN_PLACE, IN_VMEM, IN_PLACE, IN_PLACE, IN_VMEM],
+        in_specs=[IN_SMEM, IN_PLACE, IN_VMEM, IN_PLACE, IN_PLACE, IN_VMEM, IN_VMEM],
         out_specs=[IN_PLACE, IN_PLACE],
         scratch_shapes=[
             pltpu.SMEM((heads.shape[0], 1, LANES), jnp.float32),
@@ -564,7 +568,7 @@
             flops=40 * items * factors, bytes_accessed=2 * sums.size + 10 * items * factors,
             transcendentals=4 * items * factors,
         ),
-    )(seat, heads, sums, in_hbm(item_gain), in_hbm(item_level), user_total)
+    )(seat, heads, sums, in_hbm(item_gain), in_hbm(item_level), near, far)
 
 
 def ahead(array, axis, count):
@@ -599,12 +603,16 @@
     )
     item_sums = lax.all_to_all(item_sums, "user", 0, 0)
     user_total = jnp.sum(lax.all_gather(user_total, "item", axis=0, tiled=True), axis=0, keepdims=True)
-    bit = 1
-    while bit < owners:
+    bits = [1 << step for step in range(owners.bit_length() - 1)]
+    for bit in bits[:2]:
         user_total = user_total + across(user_total, "user", bit)
-        bit *= 2
     chip = chip_sums(kept, across(given, "item", 1))
-    own_shapes = slab_shapes(place, [chip] + [ahead(chip, "item", count) for count in range(2, columns, 2)], user_gain)
+    own_shapes = slab_shapes(
+        place, [chip] + [ahead(chip, "item", count) for count in range(2, columns, 2)], user_gain, user_total
+    )
+    for bit in bits[2:-1]:
+        user_total = user_total + across(user_total, "user", bit)
+    far_total = across(user_total, "user", bits[-1])
     other_shapes = across(own_shapes, "item", 1)
     user_shape_new = jnp.where(
         place[0] % 2 == 0,
@@ -613,7 +621,7 @@
     )
     user_rate_new = user_level + item_total
     item_shape_new, item_elog = item_update(
-        seat, heads, item_sums, item_gain, item_level, user_total, edge, per_owner
+        seat, heads, item_sums, item_gain, item_level, user_total, far_total, edge, per_owner
     )
     return (user_shape_new, user_rate_new, item_shape_new, item_elog)
 

time: 125 us -> 119 us (0.952)
  the two profiles are of different devices: /device:TPU:2 before, /device:TPU:1 now
where the time goes in v7:
time: 119 us; the launch traced here: 120 us
  Pallas kernels  35.3 us (30%)
  starting transfers between devices  33 us (28%)
  blocking collectives  29.5 us (25%)
  waiting for transfers between devices  17.2 us (14%)
  other arithmetic  3.7 us (3%)
  between operations  1.46 us (1%)
    all_gather x1, blocking collectives, shards(): lax.all_gather(user_total, 'item', axis=0, tiled=True)  16.5 us
    all_gather x1, blocking collectives, shards(): lax.all_gather(column_total, 'item', axis=0, tiled=True)  13 us
    pallas_call x1, Pallas kernels, sweep(): pl.pallas_call(functools.partial(sweep_kernel, user_prior / columns), in_...  12 us
    ppermute x6, waiting for transfers between devices, across(): lax.ppermute(array, axis, [(j, j ^ bit) for j in range(lax.axis_size(axis...  11.3 us
    all_to_all x1, starting transfers between devices, shards(): item_sums = lax.all_to_all(item_sums, 'user', 0, 0)  8.46 us
    all_to_all x1, starting transfers between devices, shards(): lax.all_to_all(head_of(touched, item_shape, item_rate), 'user', 0, 0)  8.44 us
    ppermute x6, starting transfers between devices, across(): lax.ppermute(array, axis, [(j, j ^ bit) for j in range(lax.axis_size(axis...  7.65 us
    pallas_call x1, Pallas kernels, dense_counts(): pl.pallas_call(dense_kernel, in_specs=[IN_SMEM, IN_SMEM, IN_SMEM, IN_PLAC...  6.88 us
  transfers between devices with their start and end apart: 12, of which 6 were waited for; matrix products, arithmetic and copies ran while one was open for 3% of the time, Pallas kernels for 14%

profile of v7, /device:TPU:1, one launch (start us, length us, event | category | flops | bytes accessed | tf_op | source)
XLA Modules:
  0.0 120.2 jit_solution(13165531603805076605)
XLA Ops:
  0.6 2.1 %shard_map.120 = f32[16,1,384]{2,1,0:T(1,128)} custom-call(s32[2,16]{1,0:T(2,128)} %bitcast.13, f32[512,256]{1,0:T(8,128)} %shape_ref.3, f32[512,256]{1,0:T(8,128)} %rate_ref.3), custom_call_target="tpu_custom_call" | custom-call | flops 524288 | bytes 1048576 | tf_op jit(solution)/shard_map/pallas_call | solution.py:87
  2.7 8.4 %all-to-all-start = ((f32[16,1,384]{2,1,0:T(1,128)}), f32[16,1,384]{2,1,0:T(1,128)S(1)}, u32[]{:S(2)}, u32[]{:S(2)}) async-start(f32[16,1,384]{2,1,0:T(1,128)} %shard_map.120), calls=%async_computation | async-start | bytes 49152 | tf_op jit(solution)/shard_map/all_to_all | solution.py:593
  11.2 2.4 %shard_map.123 = (bf16[512,256]{1,0:T(8,128)(2,1)}, f32[512,1]{1,0:T(8,128)}) custom-call(f32[512,256]{1,0:T(8,128)} %shape_ref.3, f32[512,256]{1,0:T(8,128)} %rate_ref.3), custom_call_target="tpu_custom_call" | custom-call | flops 5242880 | bytes 1310720 | tf_op jit(solution)/shard_map/pallas_call | solution.py:116
  13.6 4.0 %all-to-all-done.head_ref.head_from = f32[16,1,384]{2,1,0:T(1,128)S(1)} async-done(((f32[16,1,384]{2,1,0:T(1,128)}), f32[16,1,384]{2,1,0:T(1,128)S(1)}, u32[]{:S(2)}, u32[]{:S(2)}) %all-to-all-start) | async-done | bytes 24608 | tf_op jit(solution)/shard_map/all_to_all | solution.py:593
  17.6 2.4 %shard_map.124 = bf16[16,256,256]{2,1,0:T(8,128)(2,1)} custom-call(s32[1]{0:T(128)} %bitcast.4.seat_ref, f32[16,1,384]{2,1,0:T(1,128)S(1)} %all-to-all-done.head_ref.head_from, bf16[4,128,256]{2,1,0:T(8,128)(2,1)} %bitcast.10), custom_call_target="tpu_custom_call" | custom-call | bytes 2359296 | tf_op jit(solution)/shard_map/pallas_call | solution.py:202
  20.1 3.7 %all-to-all-start.1 = ((bf16[16,256,256]{2,1,0:T(8,128)(2,1)}), bf16[16,256,256]{2,1,0:T(8,128)(2,1)S(1)}, u32[]{:S(2)}, u32[]{:S(2)}) async-start(bf16[16,256,256]{2,1,0:T(8,128)(2,1)} %shard_map.124), calls=%async_computation.1 | async-start | bytes 4194304 | tf_op jit(solution)/shard_map/all_to_all | solution.py:595
  23.8 0.0 copy-start.1
  23.8 0.0 copy-start.2
  24.5 4.3 %shard_map.121 = (bf16[1024,256]{1,0:T(8,128)(2,1)}, f32[1024,1]{1,0:T(8,128)}, bf16[256,1024]{1,0:T(8,128)(2,1)}, f32[1,256]{1,0:T(1,128)}) custom-call(f32[1024,256]{1,0:T(8,128)} %shape_ref.2, f32[1024,256]{1,0:T(8,128)} %rate_ref.2, f32[16,1,384]{2,1,0:T(1,128)S(1)} %all-to-all-done.head_ref.head_from), custom_call_target="tpu_custom_call" | custom-call | flops 10485760 | bytes 3145728 | tf_op jit(solution)/shard_map/pallas_call | solution.py:148
  28.8 13.0 %all-gather = f32[8,1,256]{2,1,0:T(1,128)S(1)} all-gather(f32[1,1,256]{2,1,0:T(1,128)} %bitcast.15), channel_id=1, replica_groups=mesh['user'=16,'item'=8] {'item'}, dimensions={0}, use_global_device_ids=true | all-gather | bytes 9216 | tf_op jit(solution)/shard_map/all_gather | solution.py:597
  41.8 0.0 copy-done.1
  41.8 0.0 copy-done.2
  41.8 6.9 %shard_map.122.dense_from = bf16[32,8,128,128]{3,2,1,0:T(8,128)(2,1)} custom-call(s32[256]{0:T(256)S(1)} %copy-done.1, s32[256]{0:T(256)S(1)} %copy-done.2, s32[1]{0:T(128)S(6)} %copy.13.live_ref, s32[256,128,128]{2,1,0:T(8,128)} %counts_ref.1, f32[1,256]{1,0:T(1,128)S(1)} %bitcast.8), custom_call_target="tpu_custom_call" | custom-call | flops 4194304 | bytes 25165824 | tf_op jit(solution)/shard_map/pallas_call | solution.py:279
  48.7 1.9 %all-to-all-done.1.items_ref = bf16[16,256,256]{2,1,0:T(8,128)(2,1)S(1)} async-done(((bf16[16,256,256]{2,1,0:T(8,128)(2,1)}), bf16[16,256,256]{2,1,0:T(8,128)(2,1)S(1)}, u32[]{:S(2)}, u32[]{:S(2)}) %all-to-all-start.1) | async-done | bytes 2097184 | tf_op jit(solution)/shard_map/all_to_all | solution.py:595
  50.6 12.0 %shard_map.125 = (bf16[16,256,256]{2,1,0:T(8,128)(2,1)}, f32[512,256]{1,0:T(8,128)}, bf16[512,256]{1,0:T(8,128)(2,1)}, f32[1,256]{1,0:T(1,128)}) custom-call(s32[1]{0:T(128)} %bitcast.place_ref, bf16[32,8,128,128]{3,2,1,0:T(8,128)(2,1)} %shard_map.122.dense_from, bf16[16,256,256]{2,1,0:T(8,128)(2,1)S(1)} %all-to-all-done.1.items_ref, ...), custom_call_target="tpu_custom_call" | custom-call | flops 6442450944 | bytes 13631488 | tf_op jit(solution)/shard_map/pallas_call | solution.py:430
  62.6 0.0 copy-start.5
  62.6 0.0 copy-start
  62.6 0.0 copy-start.4
  62.7 8.5 %all-to-all-start.2 = ((bf16[16,256,256]{2,1,0:T(8,128)(2,1)}), bf16[16,256,256]{2,1,0:T(8,128)(2,1)S(1)}, u32[]{:S(2)}, u32[]{:S(2)}) async-start(bf16[16,256,256]{2,1,0:T(8,128)(2,1)} %get-tuple-element.24), calls=%async_computation.2 | async-start | bytes 4194304 | tf_op jit(solution)/shard_map/all_to_all | solution.py:604
  71.1 0.0 copy-start.3
  71.1 0.2 collective-permute-start.2
  71.3 1.5 %collective-permute-done.2.got_ref = bf16[512,256]{1,0:T(8,128)(2,1)S(1)} collective-permute-done((bf16[512,256]{1,0:T(8,128)(2,1)S(1)}, bf16[512,256]{1,0:T(8,128)(2,1)S(1)}, u32[]{:S(2)}, u32[]{:S(2)}) %collective-permute-start.2) | collective-permute-done | bytes 262176 | tf_op jit(solution)/shard_map/ppermute | solution.py:580
  72.8 0.0 copy-done
  72.8 0.7 shard_map.126.rest_0_
  73.5 1.0 collective-permute-start.3
  74.5 2.6 %collective-permute-start.4 = (bf16[512,256]{1,0:T(8,128)(2,1)}, bf16[512,256]{1,0:T(8,128)(2,1)S(1)}, u32[]{:S(2)}, u32[]{:S(2)}) collective-permute-start(bf16[512,256]{1,0:T(8,128)(2,1)} %shard_map.126.rest_0_), channel_id=1, source_target_pairs={{0,4},{1,5},{2,6},{3,7},{4,0},{5,1},{6,2},{7,3},{8,12},{9,13},{10,... | collective-permute-start | bytes 786440 | tf_op jit(solution)/shard_map/ppermute | solution.py:576
  77.1 1.1 collective-permute-start.5
  78.2 16.5 %all-gather.1 = f32[8,1,256]{2,1,0:T(1,128)S(1)} all-gather(f32[1,1,256]{2,1,0:T(1,128)S(1)} %bitcast.14), channel_id=1, replica_groups=mesh['user'=16,'item'=8] {'item'}, dimensions={0}, use_global_device_ids=true | all-gather | bytes 9216 | tf_op jit(solution)/shard_map/all_gather | solution.py:605
  94.8 1.4 %collective-permute-start = (f32[1,256]{1,0:T(1,128)S(1)}, f32[1,256]{1,0:T(1,128)S(1)}, u32[]{:S(2)}, u32[]{:S(2)}) collective-permute-start(f32[1,256]{1,0:T(1,128)S(1)} %bitcast.11), channel_id=1, source_target_pairs={{0,8},{8,0},{16,24},{24,16},{32,40},{40,32},{48,56},{56,48},{64,72... | collective-permute-start | bytes 3080 | tf_op jit(solution)/shard_map/ppermute | solution.py:580
  96.2 6.0 %collective-permute-done = f32[1,256]{1,0:T(1,128)S(1)} collective-permute-done((f32[1,256]{1,0:T(1,128)S(1)}, f32[1,256]{1,0:T(1,128)S(1)}, u32[]{:S(2)}, u32[]{:S(2)}) %collective-permute-start) | collective-permute-done | bytes 1056 | tf_op jit(solution)/shard_map/ppermute | solution.py:580
  102.2 1.3 %collective-permute-start.1 = (f32[1,256]{1,0:T(1,128)S(1)}, f32[1,256]{1,0:T(1,128)S(1)}, u32[]{:S(2)}, u32[]{:S(2)}) collective-permute-start(f32[1,256]{1,0:T(1,128)S(1)} %add.29), channel_id=1, source_target_pairs={{0,16},{8,24},{16,0},{24,8},{32,48},{40,56},{48,32},{56,40},{64,80... | collective-permute-start | bytes 3080 | tf_op jit(solution)/shard_map/ppermute | solution.py:580
  103.6 2.6 %collective-permute-done.1 = f32[1,256]{1,0:T(1,128)S(1)} collective-permute-done((f32[1,256]{1,0:T(1,128)S(1)}, f32[1,256]{1,0:T(1,128)S(1)}, u32[]{:S(2)}, u32[]{:S(2)}) %collective-permute-start.1) | collective-permute-done | bytes 1056 | tf_op jit(solution)/shard_map/ppermute | solution.py:580
  106.1 0.0 collective-permute-done.3.rest_1_
  106.2 0.0 collective-permute-done.4.rest_2_
  106.2 0.0 collective-permute-done.5.rest_3_
  106.2 1.9 %shard_map.127 = f32[512,256]{1,0:T(8,128)} custom-call(s32[1]{0:T(128)} %bitcast.place_ref, f32[1,256]{1,0:T(1,128)S(1)} %add.30.after_ref, bf16[1024,256]{1,0:T(8,128)(2,1)} %get-tuple-element.18.gain_from.gain_ref, bf16[512,256]{1,0:T(8,128)(2,1)} %shard_map.126.rest_0_, bf16[512,256]{1,0:T(8,128)(2,1)S(1)} %collective-permute-done.3.rest_1_, ...), custom_call_target="tpu_custom_call" | custom-call | flops 524288 | bytes 1835008 | tf_op jit(solution)/shard_map/pallas_call | solution.py:493
  108.1 2.2 %collective-permute-start.6 = (f32[512,256]{1,0:T(8,128)}, f32[512,256]{1,0:T(8,128)S(1)}, u32[]{:S(2)}, u32[]{:S(2)}) collective-permute-start(f32[512,256]{1,0:T(8,128)} %shard_map.127), channel_id=1, source_target_pairs={{0,1},{1,0},{2,3},{3,2},{4,5},{5,4},{6,7},{7,6},{8,9},{9,8},{10,11... | collective-permute-start | bytes 1572872 | tf_op jit(solution)/shard_map/ppermute | solution.py:580
  110.3 0.0 copy-done.3
  110.3 0.2 reduce.2
  110.5 0.1 collective-permute-start.7
  110.6 1.2 broadcast_add_fusion
  111.7 1.2 %collective-permute-done.7 = f32[1,256]{1,0:T(1,128)S(1)} collective-permute-done((f32[1,256]{1,0:T(1,128)S(1)}, f32[1,256]{1,0:T(1,128)S(1)}, u32[]{:S(2)}, u32[]{:S(2)}) %collective-permute-start.7) | collective-permute-done | bytes 1056 | tf_op jit(solution)/shard_map/ppermute | solution.py:580
  113.0 2.5 %collective-permute-start.8 = (f32[1,256]{1,0:T(1,128)S(1)}, f32[1,256]{1,0:T(1,128)S(1)}, u32[]{:S(2)}, u32[]{:S(2)}) collective-permute-start(f32[1,256]{1,0:T(1,128)S(1)} %add.35.near_ref), channel_id=1, source_target_pairs={{0,64},{8,72},{16,80},{24,88},{32,96},{40,104},{48,112},{56,120},{... | collective-permute-start | bytes 3080 | tf_op jit(solution)/shard_map/ppermute | solution.py:580
  115.4 0.0 collective-permute-done.6
  115.4 2.3 %maximum_select_fusion = f32[1024,256]{1,0:T(8,128)} fusion(f32[512,256]{1,0:T(8,128)S(1)} %collective-permute-done.6, f32[512,256]{1,0:T(8,128)} %shard_map.127, pred[]{:T(512)S(6)} %eq.5), kind=kLoop, calls=%fused_computation | loop fusion | flops 786432 | bytes 2097153 | tf_op jit(solution)/shard_map/jit(_where)/select_n | solution.py:617
  117.7 0.0 collective-permute-done.8.far_ref
  117.7 0.0 all-to-all-done.2.sums_ref
  117.7 2.5 %shard_map.128 = (f32[512,256]{1,0:T(8,128)}, f32[512,256]{1,0:T(8,128)}) custom-call(s32[1]{0:T(128)} %bitcast.4.seat_ref, f32[16,1,384]{2,1,0:T(1,128)S(1)} %all-to-all-done.head_ref.head_from, bf16[16,256,256]{2,1,0:T(8,128)(2,1)S(1)} %all-to-all-done.2.sums_ref, bf16[512,256]{1,0:T(8,128)(2,1)} %get-tuple-element.17.gain_from, ...), custom_call_target="tpu_custom_call" | custom-call | flops 5242880 | bytes 3407872 | tf_op jit(solution)/shard_map/pallas_call | solution.py:551
  (7 shorter events, 0.1 us)
Async XLA Ops:
  2.7 14.9 %all-to-all-start = ((f32[16,1,384]{2,1,0:T(1,128)}), f32[16,1,384]{2,1,0:T(1,128)S(1)}, u32[]{:S(2)}, u32[]{:S(2)}) async-start(f32[16,1,384]{2,1,0:T(1,128)} %shard_map.120), calls=%async_computation | async-start | bytes 49152 | tf_op jit(solution)/shard_map/all_to_all | solution.py:593
  20.1 30.5 %all-to-all-start.1 = ((bf16[16,256,256]{2,1,0:T(8,128)(2,1)}), bf16[16,256,256]{2,1,0:T(8,128)(2,1)S(1)}, u32[]{:S(2)}, u32[]{:S(2)}) async-start(bf16[16,256,256]{2,1,0:T(8,128)(2,1)} %shard_map.124), calls=%async_computation.1 | async-start | bytes 4194304 | tf_op jit(solution)/shard_map/all_to_all | solution.py:595
  23.8 18.0 %copy-start.1 = (s32[256]{0:T(256)S(1)}, s32[256]{0:T(256)}, u32[]{:S(2)}) copy-start(s32[256]{0:T(256)} %user_of.1) | copy-start | bytes 3076
  23.8 18.0 %copy-start.2 = (s32[256]{0:T(256)S(1)}, s32[256]{0:T(256)}, u32[]{:S(2)}) copy-start(s32[256]{0:T(256)} %slot_of.1) | copy-start | bytes 3076
  62.6 8.5 %copy-start.5 = (bf16[512,256]{1,0:T(8,128)(2,1)S(1)}, bf16[512,256]{1,0:T(8,128)(2,1)}, u32[]{:S(2)}) copy-start(bf16[512,256]{1,0:T(8,128)(2,1)} %get-tuple-element.23) | copy-start | bytes 786436
  62.6 10.1 %copy-start = (f32[512,256]{1,0:T(8,128)S(1)}, f32[512,256]{1,0:T(8,128)}, u32[]{:S(2)}) copy-start(f32[512,256]{1,0:T(8,128)} %get-tuple-element.22.kept_ref) | copy-start | bytes 1572868
  62.6 15.5 %copy-start.4 = (f32[1,256]{1,0:T(1,128)S(1)}, f32[1,256]{1,0:T(1,128)}, u32[]{:S(2)}) copy-start(f32[1,256]{1,0:T(1,128)} %get-tuple-element.21) | copy-start | bytes 3076
  62.7 55.0 %all-to-all-start.2 = ((bf16[16,256,256]{2,1,0:T(8,128)(2,1)}), bf16[16,256,256]{2,1,0:T(8,128)(2,1)S(1)}, u32[]{:S(2)}, u32[]{:S(2)}) async-start(bf16[16,256,256]{2,1,0:T(8,128)(2,1)} %get-tuple-element.24), calls=%async_computation.2 | async-start | bytes 4194304 | tf_op jit(solution)/shard_map/all_to_all | solution.py:604
  71.1 39.1 %copy-start.3 = (f32[1024,1]{1,0:T(8,128)S(1)}, f32[1024,1]{1,0:T(8,128)}, u32[]{:S(2)}) copy-start(f32[1024,1]{1,0:T(8,128)} %get-tuple-element.20.level_from) | copy-start | bytes 12292
  71.1 1.6 %collective-permute-start.2 = (bf16[512,256]{1,0:T(8,128)(2,1)S(1)}, bf16[512,256]{1,0:T(8,128)(2,1)S(1)}, u32[]{:S(2)}, u32[]{:S(2)}) collective-permute-start(bf16[512,256]{1,0:T(8,128)(2,1)S(1)} %copy-done.5), channel_id=1, source_target_pairs={{0,1},{1,0},{2,3},{3,2},{4,5},{5,4},{6,7},{7,6},{8,9},{9,8},{10,11... | collective-permute-start | bytes 786440 | tf_op jit(solution)/shard_map/ppermute | solution.py:580
  73.5 32.7 %collective-permute-start.3 = (bf16[512,256]{1,0:T(8,128)(2,1)}, bf16[512,256]{1,0:T(8,128)(2,1)S(1)}, u32[]{:S(2)}, u32[]{:S(2)}) collective-permute-start(bf16[512,256]{1,0:T(8,128)(2,1)} %shard_map.126.rest_0_), channel_id=1, source_target_pairs={{0,2},{1,3},{2,4},{3,5},{4,6},{5,7},{6,0},{7,1},{8,10},{9,11},{10,... | collective-permute-start | bytes 786440 | tf_op jit(solution)/shard_map/ppermute | solution.py:576
  74.5 31.7 %collective-permute-start.4 = (bf16[512,256]{1,0:T(8,128)(2,1)}, bf16[512,256]{1,0:T(8,128)(2,1)S(1)}, u32[]{:S(2)}, u32[]{:S(2)}) collective-permute-start(bf16[512,256]{1,0:T(8,128)(2,1)} %shard_map.126.rest_0_), channel_id=1, source_target_pairs={{0,4},{1,5},{2,6},{3,7},{4,0},{5,1},{6,2},{7,3},{8,12},{9,13},{10,... | collective-permute-start | bytes 786440 | tf_op jit(solution)/shard_map/ppermute | solution.py:576
  77.1 29.0 %collective-permute-start.5 = (bf16[512,256]{1,0:T(8,128)(2,1)}, bf16[512,256]{1,0:T(8,128)(2,1)S(1)}, u32[]{:S(2)}, u32[]{:S(2)}) collective-permute-start(bf16[512,256]{1,0:T(8,128)(2,1)} %shard_map.126.rest_0_), channel_id=1, source_target_pairs={{0,6},{1,7},{2,0},{3,1},{4,2},{5,3},{6,4},{7,5},{8,14},{9,15},{10,... | collective-permute-start | bytes 786440 | tf_op jit(solution)/shard_map/ppermute | solution.py:576
  94.8 7.5 %collective-permute-start = (f32[1,256]{1,0:T(1,128)S(1)}, f32[1,256]{1,0:T(1,128)S(1)}, u32[]{:S(2)}, u32[]{:S(2)}) collective-permute-start(f32[1,256]{1,0:T(1,128)S(1)} %bitcast.11), channel_id=1, source_target_pairs={{0,8},{8,0},{16,24},{24,16},{32,40},{40,32},{48,56},{56,48},{64,72... | collective-permute-start | bytes 3080 | tf_op jit(solution)/shard_map/ppermute | solution.py:580
  102.2 3.9 %collective-permute-start.1 = (f32[1,256]{1,0:T(1,128)S(1)}, f32[1,256]{1,0:T(1,128)S(1)}, u32[]{:S(2)}, u32[]{:S(2)}) collective-permute-start(f32[1,256]{1,0:T(1,128)S(1)} %add.29), channel_id=1, source_target_pairs={{0,16},{8,24},{16,0},{24,8},{32,48},{40,56},{48,32},{56,40},{64,80... | collective-permute-start | bytes 3080 | tf_op jit(solution)/shard_map/ppermute | solution.py:580
  108.1 7.4 %collective-permute-start.6 = (f32[512,256]{1,0:T(8,128)}, f32[512,256]{1,0:T(8,128)S(1)}, u32[]{:S(2)}, u32[]{:S(2)}) collective-permute-start(f32[512,256]{1,0:T(8,128)} %shard_map.127), channel_id=1, source_target_pairs={{0,1},{1,0},{2,3},{3,2},{4,5},{5,4},{6,7},{7,6},{8,9},{9,8},{10,11... | collective-permute-start | bytes 1572872 | tf_op jit(solution)/shard_map/ppermute | solution.py:580
  110.5 2.5 %collective-permute-start.7 = (f32[1,256]{1,0:T(1,128)S(1)}, f32[1,256]{1,0:T(1,128)S(1)}, u32[]{:S(2)}, u32[]{:S(2)}) collective-permute-start(f32[1,256]{1,0:T(1,128)S(1)} %add.30.after_ref), channel_id=1, source_target_pairs={{0,32},{8,40},{16,48},{24,56},{32,0},{40,8},{48,16},{56,24},{64,96... | collective-permute-start | bytes 3080 | tf_op jit(solution)/shard_map/ppermute | solution.py:580
  113.0 4.7 %collective-permute-start.8 = (f32[1,256]{1,0:T(1,128)S(1)}, f32[1,256]{1,0:T(1,128)S(1)}, u32[]{:S(2)}, u32[]{:S(2)}) collective-permute-start(f32[1,256]{1,0:T(1,128)S(1)} %add.35.near_ref), channel_id=1, source_target_pairs={{0,64},{8,72},{16,80},{24,88},{32,96},{40,104},{48,112},{56,120},{... | collective-permute-start | bytes 3080 | tf_op jit(solution)/shard_map/ppermute | solution.py:580
